TPU v7x, 32 devices: a whole 2x2x4 slice. The times are simulated.
32 devices in a mesh: dp: 16 (over z, x, core), seq: 2 (over y).
Axes of the slice: x: 2, y: 2, z: 4, core: 2. Of those that a mesh axis runs over, the one named last changes fastest.
Arguments:
- pixels_a: bfloat16 [16, 24, 24, 300], P('dp', 'seq'), may hold values from -6 to 6
- pixels_b: bfloat16 [64, 32, 32, 432], P('dp', 'seq'), may hold values from -6 to 6
- labels_a: int32 [16], P('dp'), may hold values from 0 to 999
- labels_b: int32 [64], P('dp'), may hold values from 0 to 999
- live_a: int32 [16], P('dp'), may hold values 0 or 1
- live_b: int32 [64], P('dp'), may hold values 0 or 1
- qkv_w: float32 [768, 2304], P(('dp', 'seq')), may hold values from -0.21875 to 0.21875
- out_w: float32 [768, 768], P(('dp', 'seq')), may hold values from -3 to 3
- mlp_w: float32 [2, 768, 3072], P(None, ('dp', 'seq')), may hold values from -0.21875 to 0.21875
- kern_w: float32 [3072, 768], P(('dp', 'seq')), may hold values from -0.5 to 0.5
- pos_w: float32 [49, 768], P(None, ('dp', 'seq')), may hold values from -3 to 3
- head_w: float32 [768, 1000], P(('dp', 'seq')), may hold values from -0.875 to 0.875
- gains: float32 [2, 768], P(None, ('dp', 'seq')), may hold values from 0.25 to 3.2
- qkv_m: float32 [768, 2304], P(('dp', 'seq')), may hold values from -4.7683716e-07 to 4.7683716e-07
- out_m: float32 [768, 768], P(('dp', 'seq')), may hold values from -1.4901161e-07 to 1.4901161e-07
- mlp_m: float32 [2, 768, 3072], P(None, ('dp', 'seq')), may hold values from -4.7683716e-07 to 4.7683716e-07
- kern_m: float32 [3072, 768], P(('dp', 'seq')), may hold values from -4.7683716e-07 to 4.7683716e-07
- pos_m: float32 [49, 768], P(None, ('dp', 'seq')), may hold values from -4.7683716e-07 to 4.7683716e-07
- head_m: float32 [768, 1000], P(('dp', 'seq')), may hold values from -4.7683716e-07 to 4.7683716e-07
- gains_m: float32 [2, 768], P(None, ('dp', 'seq')), may hold values from -2.3841858e-06 to 2.3841858e-06
- qkv_v: float32 [768, 2304], P(('dp', 'seq')), may hold values from 9.7614764e-17 to 3.9045905e-16
- out_v: float32 [768, 768], P(('dp', 'seq')), may hold values from 5.856886e-18 to 2.3427543e-17
- mlp_v: float32 [2, 768, 3072], P(None, ('dp', 'seq')), may hold values from 9.7614764e-17 to 3.9045905e-16
- kern_v: float32 [3072, 768], P(('dp', 'seq')), may hold values from 9.7614764e-17 to 3.9045905e-16
- pos_v: float32 [49, 768], P(None, ('dp', 'seq')), may hold values from 9.7614764e-17 to 3.9045905e-16
- head_v: float32 [768, 1000], P(('dp', 'seq')), may hold values from 9.7614764e-17 to 3.9045905e-16
- gains_v: float32 [2, 768], P(None, ('dp', 'seq')), may hold values from 2.440369e-15 to 9.761476e-15
Outputs:
- qkv_new: float32 [768, 2304], P(('dp', 'seq'))
- out_new: float32 [768, 768], P(('dp', 'seq'))
- mlp_new: float32 [2, 768, 3072], P(None, ('dp', 'seq'))
- kern_new: float32 [3072, 768], P(('dp', 'seq'))
- pos_new: float32 [49, 768], P(None, ('dp', 'seq'))
- head_new: float32 [768, 1000], P(('dp', 'seq'))
- gains_new: float32 [2, 768], P(None, ('dp', 'seq'))
- qkv_m_new: float32 [768, 2304], P(('dp', 'seq'))
- out_m_new: float32 [768, 768], P(('dp', 'seq'))
- mlp_m_new: float32 [2, 768, 3072], P(None, ('dp', 'seq'))
- kern_m_new: float32 [3072, 768], P(('dp', 'seq'))
- pos_m_new: float32 [49, 768], P(None, ('dp', 'seq'))
- head_m_new: float32 [768, 1000], P(('dp', 'seq'))
- gains_m_new: float32 [2, 768], P(None, ('dp', 'seq'))
- qkv_v_new: float32 [768, 2304], P(('dp', 'seq'))
- out_v_new: float32 [768, 768], P(('dp', 'seq'))
- mlp_v_new: float32 [2, 768, 3072], P(None, ('dp', 'seq'))
- kern_v_new: float32 [3072, 768], P(('dp', 'seq'))
- pos_v_new: float32 [49, 768], P(None, ('dp', 'seq'))
- head_v_new: float32 [768, 1000], P(('dp', 'seq'))
- gains_v_new: float32 [2, 768], P(None, ('dp', 'seq'))
- size_stats: float32 [2], replicated
- grad_norm: float32 [], replicated
All inputs are finite; a program needn't handle non-finite values. No bound on the sum of `live_a` or of `live_b` on one device may be relied on, other than what follows from the above.
Results may differ from a plain program's by a relative error of at most 0.019.
Values may be sent and summed in bfloat16 or wider, within the bound.
No kernel may reach another device: no remote copies, remote signals or barrier semaphores. Data moves between devices by JAX's collectives and lax.ppermute only.
A program may use at most 576 MiB of HBM per device.

v0:
```python
from functools import partial

import jax
import jax.numpy as jnp
from jax import lax
from jax.sharding import PartitionSpec as P

HEADS = 12
HEAD_DIM = 64
BASE = 32
PATCH_A = 10
PATCH_B = 12


HIGH = lax.Precision.HIGHEST
RATES = (0.012, 0.2, 0.012, 0.03, 0.15, 0.06, 0.25)
CLIP = 0.001
ROWS_DIM = (((0,), (0,)), ((), ()))
COLS_DIM = (((1,), (1,)), ((), ()))


def from_behind(value, axis, steps):
    count = lax.axis_size(axis)
    pairs = [(source, (source + steps) % count) for source in range(count)]
    return lax.ppermute(value, axis, pairs)


def interp_matrix(n_out, n_in):
    places = jnp.arange(n_out, dtype=jnp.float32) * ((n_in - 1) / (n_out - 1))
    return jnp.maximum(
        0.0, 1.0 - jnp.abs(places[:, None] - jnp.arange(n_in, dtype=jnp.float32)[None, :])
    )


def pinv_table(patch):
    basis = interp_matrix(patch, BASE)
    gram = jnp.dot(basis, basis.T, precision=HIGH)
    factor = jnp.linalg.cholesky(gram)
    return jax.scipy.linalg.cho_solve((factor, True), basis)


def layer_norm(values, gain):
    centred = values - jnp.mean(values, -1, keepdims=True)
    spread = jnp.mean(centred * centred, -1, keepdims=True)
    return centred * lax.rsqrt(spread + 1e-06) * gain


def kernel_resize(kernel, patch):
    table = pinv_table(patch)
    shaped = kernel.reshape(3, BASE, BASE, -1)
    return jnp.einsum("ia,jb,cabd->cijd", table, table, shaped, precision=HIGH).reshape(
        3 * patch * patch, -1
    )


def grid_resize(position, row_table, grid):
    table = interp_matrix(grid, 7)
    return jnp.einsum(
        "ia,jb,abd->ijd", row_table, table, position.reshape(7, 7, -1), precision=HIGH
    )


def adamw(weight, first, second, grad, rate):
    first = 0.9 * first + 0.1 * grad
    second = 0.999 * second + 0.001 * grad * grad
    step_dir = first / (1.0 - 0.9**3) / (jnp.sqrt(second / (1.0 - 0.999**3)) + 1e-08)
    return (weight - rate * (step_dir + 0.1 * weight), first, second)


def attend(query, keys, values):
    scores = jnp.einsum(
        "ithe,ishe->ihts", query, keys, preferred_element_type=jnp.float32
    ) * HEAD_DIM ** (-0.5)
    norm_log = jax.nn.logsumexp(scores, -1, keepdims=True)
    probs = jnp.exp(scores - norm_log).astype(jnp.bfloat16)
    return (
        jnp.einsum("ihts,ishe->ithe", probs, values, preferred_element_type=jnp.float32),
        norm_log,
    )


def attend_back(query, keys, values, norm_log, d_out):
    scale = HEAD_DIM ** (-0.5)
    scores = jnp.einsum("ithe,ishe->ihts", query, keys, preferred_element_type=jnp.float32) * scale
    probs = jnp.exp(scores - norm_log)
    d_probs = jnp.einsum("ithe,ishe->ihts", d_out, values, preferred_element_type=jnp.float32)
    d_scores = (probs * (d_probs - jnp.sum(probs * d_probs, -1, keepdims=True))).astype(
        jnp.bfloat16
    )
    d_query = (
        jnp.einsum("ihts,ishe->ithe", d_scores, keys, preferred_element_type=jnp.float32) * scale
    )
    d_keys = (
        jnp.einsum("ihts,ithe->ishe", d_scores, query, preferred_element_type=jnp.float32) * scale
    )
    d_values = jnp.einsum(
        "ihts,ithe->ishe", probs.astype(jnp.bfloat16), d_out, preferred_element_type=jnp.float32
    )
    return (d_query, d_keys, d_values)


def grid_shape(size_sets, index):
    pixels = size_sets[index][0]
    return (pixels.shape[1], pixels.shape[2], -1)


def on_device(
    pixels_a,
    pixels_b,
    labels_a,
    labels_b,
    live_a,
    live_b,
    qkv_w,
    out_w,
    mlp_w,
    kern_w,
    pos_w,
    head_w,
    gains,
    qkv_m,
    out_m,
    mlp_m,
    kern_m,
    pos_m,
    head_m,
    gains_m,
    qkv_v,
    out_v,
    mlp_v,
    kern_v,
    pos_v,
    head_v,
    gains_v,
):
    masters = (qkv_w, out_w, mlp_w, kern_w, pos_w, head_w, gains)
    firsts = (qkv_m, out_m, mlp_m, kern_m, pos_m, head_m, gains_m)
    seconds = (qkv_v, out_v, mlp_v, kern_v, pos_v, head_v, gains_v)
    bf16 = jnp.bfloat16
    w_qkv, w_out, w_mlp, w_kern, w_pos, w_head, w_gain = (
        lax.all_gather(qkv_w.astype(bf16), ("dp", "seq"), axis=0, tiled=True),
        lax.all_gather(out_w.astype(bf16), ("dp", "seq"), axis=0, tiled=True),
        lax.all_gather(mlp_w.astype(bf16), ("dp", "seq"), axis=1, tiled=True),
        lax.all_gather(kern_w.astype(bf16), ("dp", "seq"), axis=0, tiled=True),
        lax.all_gather(pos_w.astype(bf16), ("dp", "seq"), axis=1, tiled=True),
        lax.all_gather(head_w.astype(bf16), ("dp", "seq"), axis=0, tiled=True),
        lax.all_gather(gains.astype(bf16), ("dp", "seq"), axis=1, tiled=True),
    )
    seq_count = lax.axis_size("seq")
    seq_place = lax.axis_index("seq")
    gain_full = w_gain.astype(jnp.float32)
    kern_full = w_kern.astype(jnp.float32)
    pos_full = w_pos.astype(jnp.float32)
    size_sets = ((pixels_a, labels_a, live_a, PATCH_A), (pixels_b, labels_b, live_b, PATCH_B))
    embeds, flats, kern_backs, pos_backs, layouts = ([], [], [], [], [])
    start = 0
    for pixels, labels, live, patch in size_sets:
        images, rows, grid, depth = pixels.shape
        flat = pixels.reshape(images * rows * grid, depth)
        resized, kern_back = jax.vjp(partial(kernel_resize, patch=patch), kern_full)
        row_table = lax.dynamic_slice_in_dim(interp_matrix(grid, 7), seq_place * rows, rows, 0)
        place, pos_back = jax.vjp(partial(grid_resize, row_table=row_table, grid=grid), pos_full)
        embed = jnp.dot(flat, resized.astype(bf16), preferred_element_type=jnp.float32)
        embed = embed.reshape(images, rows * grid, -1) + place.reshape(1, rows * grid, -1)
        embeds.append(embed.reshape(images * rows * grid, -1))
        flats.append(flat)
        kern_backs.append(kern_back)
        pos_backs.append(pos_back)
        layouts.append((start, start + images * rows * grid, images, rows * grid, grid * grid))
        start = start + images * rows * grid
    x0 = jnp.concatenate(embeds, 0)
    h1_full, norm1_back = jax.vjp(layer_norm, x0, gain_full[0])
    h1 = h1_full.astype(bf16)
    qkv = jnp.dot(h1, w_qkv, preferred_element_type=jnp.float32).astype(bf16)
    width = qkv.shape[1] // 3
    local_kv = qkv[:, width:]
    blocks = [local_kv]
    moving = local_kv
    for turn in range(1, seq_count):
        moving = from_behind(moving, "seq", 1)
        blocks.append(moving)
    all_kv = jnp.stack(blocks, 0)
    mixed_parts, saved = ([], [])
    for first_row, last_row, images, length, whole in layouts:
        query = qkv[first_row:last_row, :width].reshape(images, length, HEADS, HEAD_DIM)
        remote = all_kv[:, first_row:last_row].reshape(
            seq_count, images, length, 2, HEADS, HEAD_DIM
        )
        remote = remote.transpose(1, 0, 2, 3, 4, 5).reshape(
            images, seq_count * length, 2, HEADS, HEAD_DIM
        )
        keys, values = (remote[:, :, 0], remote[:, :, 1])
        attended, norm_log = attend(query, keys, values)
        mixed_parts.append(attended.reshape(last_row - first_row, width))
        saved.append((query, keys, values, norm_log))
    mixed = jnp.concatenate(mixed_parts, 0).astype(bf16)
    x1 = x0 + jnp.dot(mixed, w_out, preferred_element_type=jnp.float32)
    h2_full, norm2_back = jax.vjp(layer_norm, x1, gain_full[1])
    h2 = h2_full.astype(bf16)
    inner = jnp.dot(h2, w_mlp[0], preferred_element_type=jnp.float32)
    act_full, gelu_back = jax.vjp(partial(jax.nn.gelu, approximate=False), inner)
    act = act_full.astype(bf16)
    x2 = x1 + lax.dot_general(act, w_mlp[1], COLS_DIM, preferred_element_type=jnp.float32)
    sum_a = x2[layouts[0][0] : layouts[0][1]].reshape(layouts[0][2], layouts[0][3], -1).sum(1)
    sum_b = x2[layouts[1][0] : layouts[1][1]].reshape(layouts[1][2], layouts[1][3], -1).sum(1)
    pooled_sums = lax.psum((sum_a, sum_b), "seq")
    stats, head_parts = ([], [])
    for index in range(2):
        labels, live = (size_sets[index][1], size_sets[index][2])
        pooled_low = (pooled_sums[index] / float(layouts[index][4])).astype(bf16)
        logits = jnp.dot(pooled_low, w_head, preferred_element_type=jnp.float32)
        norm_log = jax.nn.logsumexp(logits, -1)
        hot = (labels[:, None] == jnp.arange(logits.shape[1], dtype=jnp.int32)[None, :]).astype(
            jnp.float32
        )
        true_logit = jnp.sum(hot * logits, -1)
        alive = live.astype(jnp.float32)
        stats.append(jnp.stack([jnp.sum(alive * (norm_log - true_logit)), jnp.sum(alive)]))
        head_parts.append((pooled_low, jnp.exp(logits - norm_log[:, None]) - hot, alive))
    stats_a, stats_b = lax.psum((stats[0], stats[1]), "dp")
    total = jnp.maximum(stats_a[1] + stats_b[1], 1.0)
    grad_head = jnp.zeros(w_head.shape, jnp.float32)
    d_x2_parts = []
    for index in range(2):
        pooled_low, soft_minus, alive = head_parts[index]
        d_logits = (soft_minus * alive[:, None] / total).astype(bf16)
        grad_head = grad_head + lax.dot_general(
            pooled_low, d_logits, ROWS_DIM, preferred_element_type=jnp.float32
        )
        d_pooled = lax.dot_general(d_logits, w_head, COLS_DIM, preferred_element_type=jnp.float32)
        images, length, whole = (layouts[index][2], layouts[index][3], layouts[index][4])
        spread = jnp.broadcast_to(
            (d_pooled / float(whole))[:, None, :], (images, length, d_pooled.shape[1])
        )
        d_x2_parts.append(spread.reshape(images * length, -1))
    d_x2 = jnp.concatenate(d_x2_parts, 0)
    d_mix = d_x2.astype(bf16)
    grad_down = lax.dot_general(d_mix, act, ROWS_DIM, preferred_element_type=jnp.float32)
    d_act = jnp.dot(d_mix, w_mlp[1], preferred_element_type=jnp.float32)
    d_inner = gelu_back(d_act)[0].astype(bf16)
    grad_up = lax.dot_general(h2, d_inner, ROWS_DIM, preferred_element_type=jnp.float32)
    d_h2 = lax.dot_general(d_inner, w_mlp[0], COLS_DIM, preferred_element_type=jnp.float32)
    d_x1_norm, grad_gain2 = norm2_back(d_h2)
    d_x1 = d_x2 + d_x1_norm
    d_attn = d_x1.astype(bf16)
    grad_out = lax.dot_general(mixed, d_attn, ROWS_DIM, preferred_element_type=jnp.float32)
    d_mixed = lax.dot_general(d_attn, w_out, COLS_DIM, preferred_element_type=jnp.float32).astype(
        bf16
    )
    d_query_parts, d_kv_parts = ([], [])
    for index in range(2):
        first_row, last_row, images, length, whole = layouts[index]
        query, keys, values, norm_log = saved[index]
        d_out = d_mixed[first_row:last_row].reshape(images, length, HEADS, HEAD_DIM)
        d_query, d_keys, d_values = attend_back(query, keys, values, norm_log, d_out)
        d_query_parts.append(d_query.reshape(last_row - first_row, width))
        paired = jnp.stack([d_keys, d_values], 2).reshape(images, seq_count, length, 2 * width)
        d_kv_parts.append(
            paired.transpose(1, 0, 2, 3).reshape(seq_count, last_row - first_row, 2 * width)
        )
    d_all = jnp.concatenate(d_kv_parts, 1)
    mine_kv = d_all[1 % seq_count]
    for turn in range(1, seq_count):
        mine_kv = (
            from_behind(mine_kv.astype(jnp.bfloat16), "seq", 1).astype(mine_kv.dtype)
            + d_all[(turn + 1) % seq_count]
        )
    d_qkv = jnp.concatenate([jnp.concatenate(d_query_parts, 0), mine_kv], 1).astype(bf16)
    grad_qkv = lax.dot_general(h1, d_qkv, ROWS_DIM, preferred_element_type=jnp.float32)
    d_h1 = lax.dot_general(d_qkv, w_qkv, COLS_DIM, preferred_element_type=jnp.float32)
    d_x0_norm, grad_gain1 = norm1_back(d_h1)
    d_x0 = d_x1 + d_x0_norm
    grad_kern = jnp.zeros(kern_full.shape, jnp.float32)
    grad_pos = jnp.zeros(pos_full.shape, jnp.float32)
    for index in range(2):
        first_row, last_row, images, length, whole = layouts[index]
        d_rows = d_x0[first_row:last_row]
        d_kernel = lax.dot_general(
            flats[index], d_rows.astype(bf16), ROWS_DIM, preferred_element_type=jnp.float32
        )
        grad_kern = grad_kern + kern_backs[index](d_kernel)[0]
        d_place = d_rows.reshape(images, length, -1).sum(0)
        grad_pos = grad_pos + pos_backs[index](d_place.reshape(grid_shape(size_sets, index)))[0]
    grad_mlp = jnp.stack([grad_up, grad_down], 0)
    grad_gain = jnp.stack([grad_gain1, grad_gain2], 0)
    grad_head = grad_head / float(seq_count)
    owned = (
        lax.psum_scatter(grad_qkv, ("dp", "seq"), scatter_dimension=0, tiled=True),
        lax.psum_scatter(grad_out, ("dp", "seq"), scatter_dimension=0, tiled=True),
        lax.psum_scatter(grad_mlp, ("dp", "seq"), scatter_dimension=1, tiled=True),
        lax.psum_scatter(grad_kern, ("dp", "seq"), scatter_dimension=0, tiled=True),
        lax.psum_scatter(grad_pos, ("dp", "seq"), scatter_dimension=1, tiled=True),
        lax.psum_scatter(grad_head, ("dp", "seq"), scatter_dimension=0, tiled=True),
        lax.psum_scatter(grad_gain, ("dp", "seq"), scatter_dimension=1, tiled=True),
    )
    square_sum = sum((jnp.sum(piece * piece) for piece in owned))
    grad_norm = jnp.sqrt(lax.psum(square_sum, ("dp", "seq")))
    factor = jnp.minimum(1.0, CLIP / (grad_norm + 1e-06))
    done = [adamw(masters[i], firsts[i], seconds[i], owned[i] * factor, RATES[i]) for i in range(7)]
    size_stats = jnp.stack(
        [stats_a[0] / jnp.maximum(stats_a[1], 1.0), stats_b[0] / jnp.maximum(stats_b[1], 1.0)]
    )
    return (
        done[0][0],
        done[1][0],
        done[2][0],
        done[3][0],
        done[4][0],
        done[5][0],
        done[6][0],
        done[0][1],
        done[1][1],
        done[2][1],
        done[3][1],
        done[4][1],
        done[5][1],
        done[6][1],
        done[0][2],
        done[1][2],
        done[2][2],
        done[3][2],
        done[4][2],
        done[5][2],
        done[6][2],
        size_stats,
        grad_norm,
    )


def solution(mesh):
    placed = (
        P("dp", "seq", None, None),
        P("dp", "seq", None, None),
        P("dp"),
        P("dp"),
        P("dp"),
        P("dp"),
        P(("dp", "seq"), None),
        P(("dp", "seq"), None),
        P(None, ("dp", "seq"), None),
        P(("dp", "seq"), None),
        P(None, ("dp", "seq")),
        P(("dp", "seq"), None),
        P(None, ("dp", "seq")),
        P(("dp", "seq"), None),
        P(("dp", "seq"), None),
        P(None, ("dp", "seq"), None),
        P(("dp", "seq"), None),
        P(None, ("dp", "seq")),
        P(("dp", "seq"), None),
        P(None, ("dp", "seq")),
        P(("dp", "seq"), None),
        P(("dp", "seq"), None),
        P(None, ("dp", "seq"), None),
        P(("dp", "seq"), None),
        P(None, ("dp", "seq")),
        P(("dp", "seq"), None),
        P(None, ("dp", "seq")),
    )
    return jax.shard_map(
        on_device,
        mesh=mesh,
        in_specs=placed,
        out_specs=(
            P(("dp", "seq"), None),
            P(("dp", "seq"), None),
            P(None, ("dp", "seq"), None),
            P(("dp", "seq"), None),
            P(None, ("dp", "seq")),
            P(("dp", "seq"), None),
            P(None, ("dp", "seq")),
            P(("dp", "seq"), None),
            P(("dp", "seq"), None),
            P(None, ("dp", "seq"), None),
            P(("dp", "seq"), None),
            P(None, ("dp", "seq")),
            P(("dp", "seq"), None),
            P(None, ("dp", "seq")),
            P(("dp", "seq"), None),
            P(("dp", "seq"), None),
            P(None, ("dp", "seq"), None),
            P(("dp", "seq"), None),
            P(None, ("dp", "seq")),
            P(("dp", "seq"), None),
            P(None, ("dp", "seq")),
            P(),
            P(),
        ),
        check_vma=False,
    )
```

profile of v0, /device:TPU:1, one launch (start us, length us, event | category | flops | bytes accessed | tf_op | source)
XLA Modules:
  0.0 2179.6 jit_solution(5935262864826059509)
XLA Ops:
  22.7 66.1 %all-gather = bf16[32,24,2]{1,2,0:T(2,128)(2,1)S(1)} all-gather(bf16[1,24,2]{1,2,0:T(2,128)(2,1)S(1)} %convert_bitcast_fusion.1), channel_id=1, replica_groups=mesh['dp'=16,'seq'=2] {'dp','seq'}, dimensions={0}, use_global_device_ids=true | all-gather | bytes 3168 | tf_op jit(solution)/shard_map/all_gather | solution.py:147
  89.0 65.0 %all_gather.22 = bf16[49,768]{0,1:T(8,128)(2,1)S(1)} all-gather(bf16[49,24]{0,1:T(8,128)(2,1)S(1)} %convert_element_type.129), channel_id=1, replica_groups=mesh['dp'=16,'seq'=2] {'dp','seq'}, dimensions={1}, use_global_device_ids=true | all-gather | bytes 77616 | tf_op jit(solution)/shard_map/all_gather | solution.py:145
  211.4 19.3 convolution_convert_fusion
  230.8 9.3 slice_bitcast_fusion.22
  259.4 153.9 %collective-permute-done = bf16[2336,1536]{1,0:T(8,128)(2,1)} collective-permute-done((bf16[2336,1536]{1,0:T(8,128)(2,1)}, bf16[2336,1536]{1,0:T(8,128)(2,1)}, u32[]{:S(2)}, u32[]{:S(2)}) %collective-permute-start) | collective-permute-done | bytes 7176224 | tf_op jit(solution)/shard_map/ppermute | solution.py:25
  416.1 10.3 pad_maximum_fusion.3
  426.5 15.7 copy.243
  442.2 21.1 reshape.439
  463.3 23.8 %copy.244 = bf16[4,2,512,2,12,64]{2,1,5,4,0,3:T(2,128)(2,1)} copy(bf16[4,2,512,2,12,64]{2,0,5,4,3,1:T(4,128)(2,1)} %bitcast.324) | data formatting | bytes 25165824 | tf_op jit(solution)/shard_map/transpose | solution.py:189
  487.1 20.8 reshape.440
  530.0 38.0 %multiply_reduce_fusion.1 = (f32[4,12,512]{2,1,0:T(8,128)S(1)}, f32[4,12,512,1024]{3,2,1,0:T(8,128)}) fusion(bf16[4,1024,2,12,64]{1,4,3,0,2:T(8,128)(2,1)} %reshape.440, bf16[4,512,12,64]{1,0,3,2:T(4,128)(2,1)} %reshape.441), kind=kOutput, calls=%fused_computation.4 | convolution fusion | flops 3271532544 | bytes 110198784 | tf_op jit(solution)/shard_map/ithe,ishe->ihts/dot_general | solution.py:71
  568.1 31.4 %exponential_reduce_fusion = f32[4,12,512]{2,1,0:T(8,128)S(1)} fusion(f32[4,12,512,1024]{3,2,1,0:T(8,128)} %get-tuple-element.145, f32[4,12,512]{2,1,0:T(8,128)S(1)} %is-finite_select_fusion), kind=kLoop, calls=%fused_computation.3 | loop fusion | flops 75472896 | bytes 100859904 | tf_op jit(solution)/shard_map/reduce_sum | solution.py:74
  600.2 36.5 %convert_bitcast_fusion = bf16[4,512,12,64]{1,3,2,0:T(8,128)(2,1)} fusion(f32[4,12,512,1024]{3,2,1,0:T(8,128)} %get-tuple-element.145, f32[4,12,512]{2,1,0:T(8,128)S(1)} %log_add_fusion, bf16[4,1024,2,12,64]{1,4,3,0,2:T(8,128)(2,1)} %reshape.440), kind=kOutput, calls=%fused_computation.98 | convolution fusion | flops 3298295808 | bytes 110198784 | tf_op jit(solution)/shard_map/ihts,ishe->ithe/dot_general | solution.py:77
  643.9 8.2 fusion.212
  658.0 79.6 %multiply_convert_fusion.1 = (bf16[2336,3072]{1,0:T(8,128)(2,1)}, f32[2336,3072]{1,0:T(8,128)}, f32[2336,3072]{1,0:T(8,128)}) fusion(bf16[2,768,3072]{2,1,0:T(8,128)(2,1)} %all-gather.13.cloned.1.call-done, bf16[2336,768]{0,1:T(8,128)(2,1)} %multiply_convert_fusion.10.clone.5), kind=kOutput, calls=%fused_computation.11 | convolution fusion | flops 11489083392 | bytes 80216064 | tf_op jit(solution)/shard_map/dot_general | solution.py:200
  737.6 19.2 convolution_add_fusion
  765.5 8.4 reshape.444
  792.9 36.3 %all-reduce.2 = (f32[2]{0:T(128)S(1)}, f32[2]{0:T(128)S(1)}) all-reduce(f32[2]{0:T(128)S(1)} %pad_maximum_fusion.16, f32[2]{0:T(128)S(1)} %pad_maximum_fusion.17), channel_id=1, replica_groups=mesh['dp'=16,'seq'=2] {'dp'}, use_global_device_ids=true, to_apply=%region_17.18 | all-reduce | flops 4 | bytes 32 | tf_op jit(solution)/shard_map/psum | solution.py:220
  842.9 34.8 %add_convert_fusion = bf16[2336,3072]{1,0:T(8,128)(2,1)} fusion(f32[2336,3072]{1,0:T(8,128)} %get-tuple-element.137, f32[2336,3072]{1,0:T(8,128)} %get-tuple-element.150, bf16[2,768,3072]{2,1,0:T(8,128)(2,1)} %all-gather.13.cloned.1.call-done, f32[2048,768]{0,1:T(8,128)} %bitcast.320, f32[288,768]{0,1:T(8,128)S(1)} %reshape.445), kind=kOutput, calls=%fused_computation.10 | convolution fusion | flops 11130273792 | bytes 83656704 | tf_op jit(solution)/shard_map/dot_general | solution.py:239
  877.7 22.0 %multiply_reduce_fusion.4 = (f32[768]{0:T(1024)}, f32[2336]{0:T(1024)S(1)}, f32[2336,768]{0,1:T(8,128)}) fusion(f32[2336,768]{0,1:T(8,128)} %copy-done.3, f32[2336]{0:T(1024)S(1)} %copy-done.56, f32[2336]{0:T(1024)S(1)} %copy-done.45, f32[768]{0:T(1024)S(1)} %copy-done.67, bf16[2336,3072]{1,0:T(8,128)(2,1)} %add_convert_fusion, ...), kind=kOutput, calls=%fused_computation.47 | convolution fusion | flops 11035186176 | bytes 33752448 | tf_op jit(solution)/shard_map/dot_general | solution.py:242
  939.6 38.9 %fusion.28 = f32[4,1024,1,12,64]{1,4,3,0,2:T(8,128)} fusion(f32[4,12,512,1024]{3,2,1,0:T(8,128)} %get-tuple-element.145, f32[4,12,512]{2,1,0:T(8,128)S(1)} %copy-done.20, bf16[4,512,12,64]{1,0,3,2:T(4,128)(2,1)} %reshape.449), kind=kOutput, calls=%fused_computation.82 | convolution fusion | flops 3296722944 | bytes 116490240 | tf_op jit(solution)/shard_map/ihts,ithe->ishe/dot_general | solution.py:96
  978.4 69.4 %multiply_reduce_fusion = (f32[4,12,512]{2,1,0:T(8,128)S(1)}, f32[4,12,512,1024]{3,2,1,0:T(8,128)}) fusion(f32[4,12,512,1024]{3,2,1,0:T(8,128)} %get-tuple-element.145, f32[4,12,512]{2,1,0:T(8,128)S(1)} %copy-done.20, bf16[4,1024,2,12,64]{1,4,3,0,2:T(8,128)(2,1)} %reshape.440, bf16[4,512,12,64]{1,0,3,2:T(4,128)(2,1)} %reshape.449), kind=kOutput, calls=%fused_computation.1 | convolution fusion | flops 3321864192 | bytes 210960384 | tf_op jit(solution)/shard_map/ithe,ishe->ihts/dot_general | solution.py:86
  1067.5 7.8 copy.261
  1075.3 78.1 %multiply_convert_fusion = bf16[4,12,512,1024]{3,2,1,0:T(8,128)(2,1)} fusion(f32[4,12,512,1024]{3,2,1,0:T(8,128)} %get-tuple-element.155, f32[4,12,512,1024]{3,2,1,0:T(8,128)} %get-tuple-element.145, f32[4,12,512]{2,1,0:T(8,128)S(1)} %get-tuple-element.154, f32[4,12,512]{2,1,0:T(8,128)S(1)} %copy-done.20), kind=kLoop, calls=%fused_computation | loop fusion | flops 125829120 | bytes 251854848 | tf_op jit(solution)/shard_map/convert_element_type | solution.py:87
  1153.4 23.3 %multiply_bitcast_fusion = f32[4,1024,1,12,64]{1,4,3,0,2:T(8,128)} fusion(bf16[4,12,512,1024]{3,2,1,0:T(8,128)(2,1)} %multiply_convert_fusion, bf16[4,512,12,64]{1,0,3,2:T(4,128)(2,1)} %reshape.441), kind=kOutput, calls=%fused_computation.35 | convolution fusion | flops 3224371200 | bytes 66060288 | tf_op jit(solution)/shard_map/ihts,ithe->ishe/dot_general | solution.py:94
  1176.7 9.4 pad_maximum_fusion
  1186.1 8.7 copy.259
  1194.8 32.3 %reshape.451 = f32[4,2,512,1536]{2,1,3,0:T(2,128)} reshape(f32[4,1024,2,12,64]{1,4,3,2,0:T(8,128)} %copy.259) | data formatting | bytes 50331648 | tf_op jit(solution)/shard_map/reshape | solution.py:257
  1227.1 36.9 %copy.260 = f32[2,4,512,1536]{3,2,1,0:T(8,128)} copy(f32[2,4,512,1536]{2,0,3,1:T(2,128)} %bitcast.319) | data formatting | bytes 50331648 | tf_op jit(solution)/shard_map/transpose | solution.py:259
  1264.0 9.2 fusion.16
  1278.8 24.8 %fusion.41 = bf16[4,512,12,64]{1,3,2,0:T(8,128)(2,1)} fusion(bf16[4,12,512,1024]{3,2,1,0:T(8,128)(2,1)} %multiply_convert_fusion, bf16[4,1024,2,12,64]{1,4,3,0,2:T(8,128)(2,1)} %reshape.440), kind=kOutput, calls=%fused_computation.94 | convolution fusion | flops 3224371200 | bytes 59768832 | tf_op jit(solution)/shard_map/ihts,ishe->ithe/dot_general | solution.py:91
  1323.0 112.8 %collective-permute-done.1 = bf16[2336,1536]{1,0:T(8,128)(2,1)} collective-permute-done((bf16[2336,1536]{1,0:T(8,128)(2,1)}, bf16[2336,1536]{1,0:T(8,128)(2,1)}, u32[]{:S(2)}, u32[]{:S(2)}) %collective-permute-start.1) | collective-permute-done | bytes 7176224 | tf_op jit(solution)/shard_map/ppermute | solution.py:25
  1435.8 11.4 fusion.11
  1447.2 16.6 multiply_reduce_fusion.6
  1469.7 11.6 add_add_fusion.2
  1490.0 8.6 reshape.456
  1498.6 7.7 reduce_sum.336
  1515.1 18.8 fusion.18
  1552.1 10.8 fusion.24
  1563.0 10.8 add_bitcast_fusion
  1573.7 9.2 copy.266
  1584.2 17.1 convolution_bitcast_fusion
  1601.3 17.5 convolution_bitcast_fusion.1
  1632.2 37.2 %all-reduce.1 = f32[2,768]{1,0:T(2,128)S(1)} all-reduce(f32[2,768]{1,0:T(2,128)S(1)} %pad_maximum_fusion.15), channel_id=8, replica_groups=mesh['dp'=16,'seq'=2] {'dp','seq'}, use_global_device_ids=true, to_apply=%region_47.48.clone | all-reduce | flops 1536 | bytes 12288
  1671.6 89.3 %reduce-scatter.8.cloned.1.call-done = f32[24,2304]{1,0:T(8,128)} async-done(((f32[768,2304]{1,0:T(8,128)}), f32[24,2304]{1,0:T(8,128)}) %reduce-scatter.8.cloned.1.call-update) | async-done | bytes 221200 | tf_op jit(solution)/shard_map/reduce_scatter | solution.py:288
  1763.7 137.4 %reduce-scatter.14.cloned.1.call-done = f32[96,768]{1,0:T(8,128)} async-done(((f32[3072,768]{1,0:T(8,128)}), f32[96,768]{1,0:T(8,128)}) %reduce-scatter.14.cloned.1.call-update) | async-done | bytes 294928 | tf_op jit(solution)/shard_map/reduce_scatter | solution.py:291
  1902.8 210.8 %reduce-scatter.12.cloned.1.call-done = f32[2,24,3072]{2,1,0:T(8,128)} async-done(((f32[2,768,3072]{2,1,0:T(8,128)}), f32[2,24,3072]{2,1,0:T(8,128)}) %reduce-scatter.12.cloned.1.call-update) | async-done | bytes 589840 | tf_op jit(solution)/shard_map/reduce_scatter | solution.py:290
  2118.7 39.6 %psum.39 = f32[]{:T(128)} all-reduce(f32[]{:T(128)S(6)} %add.318), channel_id=1, replica_groups=mesh['dp'=16,'seq'=2] {'dp','seq'}, use_global_device_ids=true, to_apply=%region_49.50 | all-reduce | flops 1 | bytes 8 | tf_op jit(solution)/shard_map/psum | solution.py:297
  (393 shorter events, 323.9 us)
Async XLA Ops:
  7.2 194.3 %copy-start = (bf16[4,16,32,432]{3,2,1,0:T(8,128)(2,1)S(1)}, bf16[4,16,32,432]{3,2,1,0:T(8,128)(2,1)}, u32[]{:S(2)}) copy-start(bf16[4,16,32,432]{3,2,1,0:T(8,128)(2,1)} %param.28) | copy-start | bytes 5308420
  7.2 165.3 %all-gather.7.cloned.1.call-start = ((), (), s32[]{:S(2)}) async-start(), calls=%async_computation.5 | async-start | bytes 4866048 | tf_op jit(solution)/shard_map/all_gather | solution.py:144
  9.1 202.3 %all-gather.9.cloned.1.call-start = ((), (), s32[]{:S(2)}) async-start(), calls=%async_computation.6 | async-start | bytes 3649536 | tf_op jit(solution)/shard_map/all_gather | solution.py:141
  10.7 633.1 %all-gather.11.cloned.1.call-start = ((), (), s32[]{:S(2)}) async-start(), calls=%async_computation.7 | async-start | bytes 1216512 | tf_op jit(solution)/shard_map/all_gather | solution.py:142
  12.3 645.7 %all-gather.13.cloned.1.call-start = ((), (), s32[]{:S(2)}) async-start(), calls=%async_computation.8 | async-start | bytes 9732096 | tf_op jit(solution)/shard_map/all_gather | solution.py:143
  14.2 769.0 %all-gather.15.cloned.1.call-start = ((), (), s32[]{:S(2)}) async-start(), calls=%async_computation.9 | async-start | bytes 1622016 | tf_op jit(solution)/shard_map/all_gather | solution.py:146
  169.5 22.6 %copy-start.40 = (f32[10,32,1,1]{1,0,3,2:T(8,128)}, f32[10,32,1,1]{1,0,3,2:T(8,128)S(1)}, u32[]{:S(2)}) copy-start(f32[10,32,1,1]{1,0,3,2:T(8,128)S(1)} %convolution_bitcast_fusion.10) | copy-start | bytes 3844
  170.5 40.9 %copy-start.69 = (f32[768]{0:T(1024)}, f32[768]{0:T(1024)S(1)}, u32[]{:S(2)}) copy-start(f32[768]{0:T(1024)S(1)} %get-tuple-element.99) | copy-start | bytes 9220
  208.7 22.1 %copy-start.42 = (f32[2336]{0:T(1024)}, f32[2336]{0:T(1024)S(1)}, u32[]{:S(2)}) copy-start(f32[2336]{0:T(1024)S(1)} %broadcast_multiply_fusion.1) | copy-start | bytes 28036
  211.4 19.4 copy-start.47
  240.0 173.3 %collective-permute-start = (bf16[2336,1536]{1,0:T(8,128)(2,1)}, bf16[2336,1536]{1,0:T(8,128)(2,1)}, u32[]{:S(2)}, u32[]{:S(2)}) collective-permute-start(bf16[2336,1536]{1,0:T(8,128)(2,1)} %get-tuple-element.139), channel_id=1, source_target_pairs={{0,1},{1,0},{2,3},{3,2},{4,5},{5,4},{6,7},{7,6},{8,9},{9,8},{10,11... | collective-permute-start | bytes 21528584 | tf_op jit(solution)/shard_map/ppermute | solution.py:25
  241.8 1387.4 %reduce-scatter.10.cloned.1.call-start = ((), (), s32[]{:S(2)}) async-start(), calls=%async_computation.11 | async-start | bytes 2433024 | tf_op jit(solution)/shard_map/reduce_scatter | solution.py:289
  248.2 272.1 %copy-start.21 = (bf16[288,768]{0,1:T(8,128)(2,1)}, bf16[288,768]{0,1:T(8,128)(2,1)S(1)}, u32[]{:S(2)}) copy-start(bf16[288,768]{0,1:T(8,128)(2,1)S(1)} %copy.242) | copy-start | bytes 1327108
  658.0 79.6 %copy-start.4 = (f32[2336,768]{0,1:T(8,128)S(1)}, f32[2336,768]{0,1:T(8,128)}, u32[]{:S(2)}) copy-start(f32[2336,768]{0,1:T(8,128)} %copy-done.3) | copy-start | bytes 21528580
  783.1 50.5 %copy-start.59 = (f32[4,768]{1,0:T(4,128)}, f32[4,768]{1,0:T(4,128)S(1)}, u32[]{:S(2)}) copy-start(f32[4,768]{1,0:T(4,128)S(1)} %get-tuple-element.106) | copy-start | bytes 36868
  790.7 43.0 %copy-start.36 = (f32[4,1000]{1,0:T(4,128)}, f32[4,1000]{1,0:T(4,128)S(1)}, u32[]{:S(2)}) copy-start(f32[4,1000]{1,0:T(4,128)S(1)} %get-tuple-element.152) | copy-start | bytes 48004
  791.6 51.1 %copy-start.83 = (f32[4]{0:T(128)}, f32[4]{0:T(128)S(1)}, u32[]{:S(2)}) copy-start(f32[4]{0:T(128)S(1)} %get-tuple-element.135) | copy-start | bytes 52
  792.9 40.8 %copy-start.86 = (f32[4]{0:T(128)}, f32[4]{0:T(128)S(1)}, u32[]{:S(2)}) copy-start(f32[4]{0:T(128)S(1)} %convert_element_type.148) | copy-start | bytes 52
  842.8 63.4 %copy-start.15 = (f32[288,768]{0,1:T(8,128)}, f32[288,768]{0,1:T(8,128)S(1)}, u32[]{:S(2)}) copy-start(f32[288,768]{0,1:T(8,128)S(1)} %reshape.445) | copy-start | bytes 2654212
  842.9 34.8 %copy-start.45 = (f32[2336]{0:T(1024)S(1)}, f32[2336]{0:T(1024)}, u32[]{:S(2)}) copy-start(f32[2336]{0:T(1024)} %copy-done.44) | copy-start | bytes 28036
  842.9 34.8 %copy-start.56 = (f32[2336]{0:T(1024)S(1)}, f32[2336]{0:T(1024)}, u32[]{:S(2)}) copy-start(f32[2336]{0:T(1024)} %copy-done.55) | copy-start | bytes 28036
  842.9 34.8 %copy-start.67 = (f32[768]{0:T(1024)S(1)}, f32[768]{0:T(1024)}, u32[]{:S(2)}) copy-start(f32[768]{0:T(1024)} %get-tuple-element.98) | copy-start | bytes 9220
  877.7 22.0 %copy-start.54 = (f32[2336]{0:T(1024)S(1)}, f32[2336]{0:T(1024)}, u32[]{:S(2)}) copy-start(f32[2336]{0:T(1024)} %copy-done.53) | copy-start | bytes 28036
  1273.2 162.6 %collective-permute-start.1 = (bf16[2336,1536]{1,0:T(8,128)(2,1)}, bf16[2336,1536]{1,0:T(8,128)(2,1)}, u32[]{:S(2)}, u32[]{:S(2)}) collective-permute-start(bf16[2336,1536]{1,0:T(8,128)(2,1)} %fusion.16), channel_id=1, source_target_pairs={{0,1},{1,0},{2,3},{3,2},{4,5},{5,4},{6,7},{7,6},{8,9},{9,8},{10,11... | collective-permute-start | bytes 21528584 | tf_op jit(solution)/shard_map/ppermute | solution.py:25
  1278.7 24.8 %copy-start.75 = (f32[1,768]{1,0:T(1,128)S(1)}, f32[1,768]{1,0:T(1,128)}, u32[]{:S(2)}) copy-start(f32[1,768]{1,0:T(1,128)} %copy-done.74) | copy-start | bytes 9220
  1278.7 351.9 %reduce-scatter.16.cloned.1.call-start = ((), (), s32[]{:S(2)}) async-start(), calls=%async_computation.14 | async-start | bytes 3244032 | tf_op jit(solution)/shard_map/reduce_scatter | solution.py:293
  1322.9 124.3 %copy-start.10 = (f32[288,768]{0,1:T(8,128)S(1)}, f32[288,768]{0,1:T(8,128)}, u32[]{:S(2)}) copy-start(f32[288,768]{0,1:T(8,128)} %copy-done.8) | copy-start | bytes 2654212
  1322.9 124.3 %copy-start.43 = (f32[2336]{0:T(1024)S(1)}, f32[2336]{0:T(1024)}, u32[]{:S(2)}) copy-start(f32[2336]{0:T(1024)} %copy-done.42) | copy-start | bytes 28036
  1322.9 124.3 %copy-start.70 = (f32[768]{0:T(1024)S(1)}, f32[768]{0:T(1024)}, u32[]{:S(2)}) copy-start(f32[768]{0:T(1024)} %copy-done.69) | copy-start | bytes 9220
  1322.9 347.1 %all-reduce.6.cloned.1.call-start = ((), (), s32[]{:S(2)}) async-start(), calls=%async_computation.15 | async-start | bytes 344064
  1435.8 28.1 %slice-start = ((s8[6291456]{0:T(1024)(128)(4,1)}), s8[4194304]{0:T(1024)(128)(4,1)S(1)}, s32[]{:S(2)}) async-start(s8[6291456]{0:T(1024)(128)(4,1)} %bitcast.317), calls=%async_computation.16 | async-start | bytes 8388608
  1515.0 19.2 copy-start.28
  1515.0 245.8 %reduce-scatter.8.cloned.1.call-start = ((), (), s32[]{:S(2)}) async-start(), calls=%async_computation.10 | async-start | bytes 7299072 | tf_op jit(solution)/shard_map/reduce_scatter | solution.py:288
  1533.9 367.2 %reduce-scatter.14.cloned.1.call-start = ((), (), s32[]{:S(2)}) async-start(), calls=%async_computation.13 | async-start | bytes 9732096 | tf_op jit(solution)/shard_map/reduce_scatter | solution.py:291
  1582.9 18.3 copy-start.46
  1582.9 18.3 copy-start.57
  1582.9 18.3 copy-start.68
  1583.0 530.6 %reduce-scatter.12.cloned.1.call-start = ((), (), s32[]{:S(2)}) async-start(), calls=%async_computation.12 | async-start | bytes 19464192 | tf_op jit(solution)/shard_map/reduce_scatter | solution.py:290
  1625.7 534.8 %copy-start.61 = (f32[49,24]{0,1:T(8,128)S(1)}, f32[49,24]{0,1:T(8,128)}, u32[]{:S(2)}) copy-start(f32[49,24]{0,1:T(8,128)} %param.37) | copy-start | bytes 14116
  1625.7 534.8 %copy-start.72 = (f32[49,24]{0,1:T(8,128)S(1)}, f32[49,24]{0,1:T(8,128)}, u32[]{:S(2)}) copy-start(f32[49,24]{0,1:T(8,128)} %param.44) | copy-start | bytes 14116
  1625.7 534.8 %copy-start.73 = (f32[49,24]{0,1:T(8,128)S(1)}, f32[49,24]{0,1:T(8,128)}, u32[]{:S(2)}) copy-start(f32[49,24]{0,1:T(8,128)} %param.51) | copy-start | bytes 14116
  1625.7 535.4 %copy-start.35 = (f32[24,768]{1,0:T(8,128)S(1)}, f32[24,768]{1,0:T(8,128)}, u32[]{:S(2)}) copy-start(f32[24,768]{1,0:T(8,128)} %param.34) | copy-start | bytes 221188
  1625.7 537.1 %copy-start.34 = (f32[24,1000]{1,0:T(8,128)S(1)}, f32[24,1000]{1,0:T(8,128)}, u32[]{:S(2)}) copy-start(f32[24,1000]{1,0:T(8,128)} %param.38) | copy-start | bytes 288004
  1625.7 537.1 %copy-start.58 = (f32[24,1000]{1,0:T(8,128)S(1)}, f32[24,1000]{1,0:T(8,128)}, u32[]{:S(2)}) copy-start(f32[24,1000]{1,0:T(8,128)} %param.45) | copy-start | bytes 288004
  1625.7 538.8 %copy-start.29 = (f32[24,2304]{1,0:T(8,128)S(1)}, f32[24,2304]{1,0:T(8,128)}, u32[]{:S(2)}) copy-start(f32[24,2304]{1,0:T(8,128)} %param.33) | copy-start | bytes 663556
  1625.7 540.8 %copy-start.27 = (f32[96,768]{1,0:T(8,128)S(1)}, f32[96,768]{1,0:T(8,128)}, u32[]{:S(2)}) copy-start(f32[96,768]{1,0:T(8,128)} %param.36) | copy-start | bytes 884740
  1625.8 543.0 %copy-start.26 = (f32[2,24,3072]{2,1,0:T(8,128)S(1)}, f32[2,24,3072]{2,1,0:T(8,128)}, u32[]{:S(2)}) copy-start(f32[2,24,3072]{2,1,0:T(8,128)} %param.35) | copy-start | bytes 1769476
  1669.4 449.3 %copy-start.76 = (f32[2,768]{1,0:T(2,128)}, f32[2,768]{1,0:T(2,128)S(1)}, u32[]{:S(2)}) copy-start(f32[2,768]{1,0:T(2,128)S(1)} %all-reduce.1) | copy-start | bytes 18436
  (60 other events, 446.4 us)
Sparse Core Ops, SparseCore 0:
  11.5 66.1 all-gather.6
  81.3 59.3 all-gather.8
  144.2 52.8 all-gather.10
  200.4 99.1 all-gather.12
  302.9 55.6 all-gather.14
  1278.9 100.5 reduce-scatter.9
  1385.8 100.3 reduce-scatter.15
  1515.1 120.0 all-reduce.5
  1641.8 118.9 reduce-scatter.7
  1766.6 134.4 reduce-scatter.13
  1908.7 204.8 reduce-scatter.11
where the time goes:
time: 2190 us; the launch traced here: 2180 us
  waiting for transfers between devices  704 us (32%)
  matrix products  600 us (27%)
  local copies, waits for them, and re-layouts  329 us (15%)
  other arithmetic  264 us (12%)
  blocking collectives  250 us (11%)
  between operations  29.9 us (1%)
    ppermute x2, waiting for transfers between devices, from_behind(): return lax.ppermute(value, axis, pairs)  267 us
    reduce_scatter x1, waiting for transfers between devices, on_device(): lax.psum_scatter(grad_mlp, ('dp', 'seq'), scatter_dimension=1, tiled=True)  211 us
    reduce_scatter x1, waiting for transfers between devices, on_device(): lax.psum_scatter(grad_kern, ('dp', 'seq'), scatter_dimension=0, tiled=True)  137 us
    reduce_scatter x1, waiting for transfers between devices, on_device(): lax.psum_scatter(grad_qkv, ('dp', 'seq'), scatter_dimension=0, tiled=True)  89.3 us
    convert_element_type x2, other arithmetic, attend_back(): (probs * (d_probs - jnp.sum(probs * d_probs, -1, keepdims=True))).astype(...  85.2 us
    dot_general x1, matrix products, on_device(): inner = jnp.dot(h2, w_mlp[0], preferred_element_type=jnp.float32)  79.6 us
    dot_general x2, matrix products, attend_back(): jnp.einsum('ithe,ishe->ihts', d_out, values, preferred_element_type=jnp.f...  76.5 us
    all_gather x1, blocking collectives, on_device(): lax.all_gather(gains.astype(bf16), ('dp', 'seq'), axis=1, tiled=True)  66.1 us
  transfers between devices with their start and end apart: 13, of which 5 were waited for; matrix products, arithmetic and copies ran while one was open for 33% of the time, Pallas kernels for 0%

commit v1 on v0

--- a/solution.py
+++ b/solution.py
@@ -2,7 +2,11 @@
 
 import jax
 import jax.numpy as jnp
+import ml_dtypes
+import numpy as np
 from jax import lax
+from jax.experimental import pallas as pl
+from jax.experimental.pallas import tpu as pltpu
 from jax.sharding import PartitionSpec as P
 
 HEADS = 12
@@ -102,6 +106,930 @@
 def grid_shape(size_sets, index):
     pixels = size_sets[index][0]
     return (pixels.shape[1], pixels.shape[2], -1)
+
+
+AXES = ("dp", "seq")
+NT = (((1,), (1,)), ((), ()))
+NN = (((1,), (0,)), ((), ()))
+BF = jnp.bfloat16
+F32 = jnp.float32
+VMEM_BYTES = 58 << 20
+
+
+class Places:
+    def __init__(self):
+        dp, seq = lax.axis_size("dp"), lax.axis_size("seq")
+        self.count = dp * seq
+        deep = 4 if dp % 8 == 0 else 1
+        self.z = (dp // deep * seq, deep)
+        self.x = (2 * seq, dp // deep // 2)
+        self.core = (seq, 2)
+        self.y = (1, seq)
+        self.flat = lax.axis_index("dp") * seq + lax.axis_index("seq")
+
+    def digit(self, digit):
+        return (self.flat // digit[0]) % digit[1]
+
+    def send(self, value, digit, steps):
+        stride, radix = digit
+        pairs = []
+        for source in range(self.count):
+            place = (source // stride) % radix
+            pairs.append((source, source + ((place + steps) % radix - place) * stride))
+        return lax.ppermute(value, AXES, pairs)
+
+    def gather(self, value, order):
+        held = value[None]
+        shifts = [{}]
+        for turn, digit in enumerate(order):
+            parts = [held] + [self.send(held, digit, step) for step in range(1, digit[1])]
+            shifts = [{**shift, digit: step} for step in range(digit[1]) for shift in shifts]
+            if turn < len(order) - 1:
+                held = jnp.concatenate(parts, 0)
+        owner = jnp.zeros((self.count,), jnp.int32)
+        for digit in order:
+            steps = np.array([shift[digit] for shift in shifts], np.int32)
+            owner = owner + ((self.digit(digit) - steps) % digit[1]) * digit[0]
+        return parts, owner
+
+    def scatter_sum(self, value, order):
+        rows = value.shape[0] // self.count
+        kept = [self.z, self.x, self.core, self.y]
+        held = value.reshape([digit[1] for digit in kept] + [rows, value.shape[1]])
+        for digit in order:
+            axis = kept.index(digit)
+            place, radix = self.digit(digit), digit[1]
+            total = lax.dynamic_index_in_dim(held, place, axis, False).astype(F32)
+            for step in range(1, radix):
+                away = lax.dynamic_index_in_dim(held, (place + step) % radix, axis, False)
+                total = total + self.send(away.astype(BF), digit, step).astype(F32)
+            held = total
+            kept.pop(axis)
+        return held
+
+    def sum_all(self, value, digits):
+        for digit in digits:
+            stride, radix = digit
+            parts = [value] + [self.send(value, digit, step) for step in range(1, radix)]
+            if radix == 2:
+                value = parts[0] + parts[1]
+            elif radix == 4:
+                value = (parts[0] + parts[2]) + (parts[1] + parts[3])
+            else:
+                order = (self.digit(digit) - jnp.arange(radix)) % radix
+                value = jnp.sum(jnp.take(jnp.stack(parts), order, 0), 0)
+        return value
+
+
+def placed_kernel(owner_ref, *refs, cuts):
+    out_ref, sems = refs[-2], refs[-1]
+    copies = []
+    at = 0
+    for half, (first, width, pieces) in enumerate(cuts):
+        block = 0
+        for _ in range(pieces):
+            piece = refs[at]
+            at += 1
+            for index in range(piece.shape[0]):
+                copies.append(
+                    pltpu.make_async_copy(
+                        piece.at[index],
+                        out_ref.at[owner_ref[half, block], :, pl.ds(first, width)],
+                        sems.at[half, block],
+                    )
+                )
+                block += 1
+    for copy in copies:
+        copy.start()
+    for copy in copies:
+        copy.wait()
+
+
+def place_blocks(halves):
+    cuts, arrays, owners, first = [], [], [], 0
+    for pieces, owner in halves:
+        cuts.append((first, pieces[0].shape[2], len(pieces)))
+        first += pieces[0].shape[2]
+        arrays += pieces
+        owners.append(owner)
+    count, rows = owners[0].shape[0], arrays[0].shape[1]
+    size = count * rows * first * 2
+    out = pl.pallas_call(
+        partial(placed_kernel, cuts=tuple(cuts)),
+        out_shape=jax.ShapeDtypeStruct((count, rows, first), BF),
+        in_specs=[pl.BlockSpec(memory_space=pltpu.SMEM)]
+        + [pl.BlockSpec(memory_space=pl.ANY)] * len(arrays),
+        out_specs=pl.BlockSpec(memory_space=pltpu.VMEM),
+        scratch_shapes=[pltpu.SemaphoreType.DMA((len(cuts), count))],
+        compiler_params=pltpu.CompilerParams(vmem_limit_bytes=VMEM_BYTES),
+        cost_estimate=pl.CostEstimate(flops=0, bytes_accessed=2 * size, transcendentals=0),
+        name="place_blocks",
+    )(jnp.stack(owners), *arrays)
+    return out.reshape(count * rows, first)
+
+
+def interp_table(n_out, n_in):
+    places = np.arange(n_out) * ((n_in - 1) / (n_out - 1))
+    return np.maximum(0.0, 1.0 - np.abs(places[:, None] - np.arange(n_in)[None, :]))
+
+
+def resize_table(patch):
+    basis = interp_table(patch, BASE)
+    table = np.linalg.solve(basis @ basis.T, basis)
+    return np.kron(table, table).astype(np.float32)
+
+
+def place_table(grid):
+    table = interp_table(grid, 7)
+    full = np.kron(table, table).astype(np.float32)
+    high = full.astype(ml_dtypes.bfloat16)
+    low = (full - high.astype(np.float32)).astype(ml_dtypes.bfloat16)
+    return np.concatenate([high, low], 1)
+
+
+def dot(left, right, dims):
+    return lax.dot_general(left, right, dims, preferred_element_type=F32)
+
+
+def estimate(flops, nbytes):
+    return pl.CostEstimate(flops=int(flops), bytes_accessed=int(nbytes), transcendentals=0)
+
+
+def normed(values):
+    centred = values - jnp.mean(values, -1, keepdims=True)
+    scale = lax.rsqrt(jnp.mean(centred * centred, -1, keepdims=True) + 1e-06)
+    return centred * scale, scale
+
+
+def norm_back(d_out, gain, hat, scale):
+    d_hat = d_out * gain
+    return scale * (
+        d_hat
+        - jnp.mean(d_hat, -1, keepdims=True)
+        - hat * jnp.mean(d_hat * hat, -1, keepdims=True)
+    )
+
+
+def embed_kernel(flat_ref, weight_ref, gain_ref, qkvw_ref, x0_ref, qkv_ref):
+    x0 = dot(flat_ref[...], weight_ref[...], NN)
+    x0_ref[...] = x0
+    h1 = (normed(x0)[0] * gain_ref[...]).astype(BF)
+    width = 768
+    for first in range(0, qkvw_ref.shape[1], width):
+        cols = slice(first, first + width)
+        qkv_ref[:, cols] = dot(h1, qkvw_ref[:, cols], NN).astype(BF)
+
+
+def embed(flat, weight, gain, w_qkv, block):
+    rows, depth = flat.shape
+    width, out = w_qkv.shape
+    return pl.pallas_call(
+        embed_kernel,
+        out_shape=(
+            jax.ShapeDtypeStruct((rows, width), F32),
+            jax.ShapeDtypeStruct((rows, out), BF),
+        ),
+        grid=(rows // block,),
+        in_specs=[
+            pl.BlockSpec((block, depth), lambda i: (i, 0)),
+            pl.BlockSpec((depth, width), lambda i: (0, 0)),
+            pl.BlockSpec((1, width), lambda i: (0, 0)),
+            pl.BlockSpec((width, out), lambda i: (0, 0)),
+        ],
+        out_specs=[
+            pl.BlockSpec((block, width), lambda i: (i, 0)),
+            pl.BlockSpec((block, out), lambda i: (i, 0)),
+        ],
+        compiler_params=pltpu.CompilerParams(vmem_limit_bytes=VMEM_BYTES),
+        cost_estimate=estimate(2 * rows * width * (depth + out), rows * (width + out) * 4),
+        name="embed",
+    )(flat, weight, gain, w_qkv)
+
+
+def head_split(first, values):
+    zero = jnp.zeros((), values.dtype)
+    return jnp.where(first, values, zero), jnp.where(first, zero, values)
+
+
+def attend_kernel(q_ref, k_ref, v_ref, out_ref, log_ref):
+    lane = lax.broadcasted_iota(jnp.int32, (1, 128), 1)
+    first = lane < HEAD_DIM
+    one = jnp.ones((), BF)
+    values = v_ref[...]
+    keys = head_split(first, k_ref[...])
+    sided = (jnp.where(first, values, one).T, jnp.where(first, one, values).T)
+    query = q_ref[...] * jnp.asarray(HEAD_DIM**-0.5, BF)
+    outs = []
+    for head in range(2):
+        scores = dot(keys[head], query, NT)
+        top = jnp.max(scores, 0, keepdims=True)
+        probs = jnp.exp(scores - top).astype(BF)
+        mixed = dot(sided[head], probs, NN)
+        at = HEAD_DIM * (1 - head)
+        total = mixed[at : at + 1]
+        own = HEAD_DIM * head
+        outs.append(mixed[own : own + HEAD_DIM] / total)
+        log_ref[0, 0, head : head + 1, :] = top + jnp.log(total)
+    out_ref[...] = jnp.concatenate(outs, 0).T.astype(BF)
+
+
+def attend_pairs(query, keys, values, cols, images, n_query, n_key):
+    pairs = HEADS // 2
+    width = HEADS * HEAD_DIM
+    return pl.pallas_call(
+        attend_kernel,
+        out_shape=(
+            jax.ShapeDtypeStruct((images * n_query, width), BF),
+            jax.ShapeDtypeStruct((images, pairs, 2, n_query), F32),
+        ),
+        grid=(images, pairs),
+        in_specs=[
+            pl.BlockSpec((n_query, 128), lambda i, h: (i, h + cols[0])),
+            pl.BlockSpec((n_key, 128), lambda i, h: (i, h + cols[1])),
+            pl.BlockSpec((n_key, 128), lambda i, h: (i, h + cols[2])),
+        ],
+        out_specs=[
+            pl.BlockSpec((n_query, 128), lambda i, h: (i, h)),
+            pl.BlockSpec((1, 1, 2, n_query), lambda i, h: (i, h, 0, 0)),
+        ],
+        compiler_params=pltpu.CompilerParams(vmem_limit_bytes=VMEM_BYTES),
+        cost_estimate=estimate(
+            images * HEADS * n_query * n_key * 1600, images * (n_query + n_key) * width * 4
+        ),
+        name="attend",
+    )(query, keys, values)
+
+
+def attend_back_kernel(q_ref, k_ref, v_ref, do_ref, o_ref, log_ref, dq_ref, dk_ref, dv_ref):
+    lane = lax.broadcasted_iota(jnp.int32, (1, 128), 1)
+    first = lane < HEAD_DIM
+    scale = jnp.asarray(HEAD_DIM**-0.5, BF)
+    keys_all = k_ref[...]
+    keys = head_split(first, keys_all)
+    values = head_split(first, v_ref[...])
+    query = q_ref[...] * scale
+    d_out = do_ref[...]
+    queries = head_split(first, query)
+    d_outs = head_split(first, d_out)
+    keys_t = tuple(part.T for part in head_split(first, keys_all * scale))
+    both = (d_out.astype(F32) * o_ref[...].astype(F32)).T
+    d_query, d_keys, d_values = 0.0, 0.0, 0.0
+    for head in range(2):
+        row = jnp.sum(both[HEAD_DIM * head : HEAD_DIM * (head + 1)], 0, keepdims=True)
+        scores = dot(keys[head], query, NT)
+        probs = jnp.exp(scores - log_ref[0, 0, head : head + 1, :])
+        d_probs = dot(values[head], d_out, NT)
+        d_scores = (probs * (d_probs - row)).astype(BF)
+        d_keys = d_keys + dot(d_scores, queries[head], NN)
+        d_values = d_values + dot(probs.astype(BF), d_outs[head], NN)
+        d_query = d_query + dot(keys_t[head], d_scores, NN)
+    dq_ref[...] = d_query.T.astype(BF)
+    dk_ref[...] = d_keys.astype(dk_ref.dtype)
+    dv_ref[...] = d_values.astype(dv_ref.dtype)
+
+
+def attend_back_pairs(query, keys, values, cols, d_out, out, log, images, n_query, n_key, pair_set):
+    begin, end = pair_set
+    width = (end - begin) * 128
+    rows = pl.BlockSpec((n_query, 128), lambda i, h: (i, h + begin))
+    over_q = pl.BlockSpec((n_query, 128), lambda i, h: (i, h))
+    over_k = pl.BlockSpec((n_key, 128), lambda i, h: (i, h))
+    return pl.pallas_call(
+        attend_back_kernel,
+        out_shape=(
+            jax.ShapeDtypeStruct((images * n_query, width), BF),
+            jax.ShapeDtypeStruct((images * n_key, width), BF),
+            jax.ShapeDtypeStruct((images * n_key, width), BF),
+        ),
+        grid=(images, end - begin),
+        in_specs=[
+            pl.BlockSpec((n_query, 128), lambda i, h: (i, h + cols[0] + begin)),
+            pl.BlockSpec((n_key, 128), lambda i, h: (i, h + cols[1] + begin)),
+            pl.BlockSpec((n_key, 128), lambda i, h: (i, h + cols[2] + begin)),
+            rows,
+            rows,
+            pl.BlockSpec((1, 1, 2, n_query), lambda i, h: (i, h + begin, 0, 0)),
+        ],
+        out_specs=[over_q, over_k, over_k],
+        compiler_params=pltpu.CompilerParams(vmem_limit_bytes=VMEM_BYTES),
+        cost_estimate=estimate(
+            images * 2 * (end - begin) * n_query * n_key * 2900,
+            images * (n_query + n_key) * width * 8,
+        ),
+        name="attend_back",
+    )(query, keys, values, d_out, out, log)
+
+
+def gelu_parts(inner):
+    bell = jnp.exp(-0.5 * inner * inner)
+    base = 1.0 + (0.3275911 * 0.7071067811865476) * jnp.abs(inner)
+    turn = pl.reciprocal(base, approx=True)
+    turn = turn * (2.0 - base * turn)
+    poly = 0.5 * 1.061405429
+    for term in (-1.453152027, 1.421413741, -0.284496736, 0.254829592):
+        poly = poly * turn + 0.5 * term
+    tail = poly * turn * bell
+    upper = jnp.where(inner < 0.0, tail, 1.0 - tail)
+    return upper, inner * bell * 0.3989422804014327
+
+
+def mlp_kernel(x0_ref, mixed_ref, wout_ref, gain_ref, wup_ref, x1_ref, slope_ref, xsum_ref, asum_ref, *, per):
+    x1 = x0_ref[...] + dot(mixed_ref[...], wout_ref[...], NN)
+    x1_ref[...] = x1
+    h2 = (normed(x1)[0] * gain_ref[...]).astype(BF)
+
+    @pl.when(pl.program_id(0) % per == 0)
+    def _():
+        xsum_ref[...] = jnp.zeros_like(xsum_ref)
+        asum_ref[...] = jnp.zeros_like(asum_ref)
+
+    xsum_ref[0] += jnp.sum(x1, 0, keepdims=True)
+    width = 512
+    for first in range(0, wup_ref.shape[1], width):
+        cols = slice(first, first + width)
+        inner = dot(h2, wup_ref[:, cols], NN)
+        upper, slope = gelu_parts(inner)
+        slope_ref[:, cols] = (upper + slope).astype(BF)
+        act = (inner * upper).astype(BF).astype(F32)
+        asum_ref[0, :, cols] += jnp.sum(act, 0, keepdims=True)
+
+
+def mlp(x0, mixed, w_up_out, gain, images, block):
+    rows, width = x0.shape
+    hidden = w_up_out.shape[1] - width
+    per = rows // images // block
+    return pl.pallas_call(
+        partial(mlp_kernel, per=per),
+        out_shape=(
+            jax.ShapeDtypeStruct((rows, width), F32),
+            jax.ShapeDtypeStruct((rows, hidden), BF),
+            jax.ShapeDtypeStruct((images, 1, width), F32),
+            jax.ShapeDtypeStruct((images, 1, hidden), F32),
+        ),
+        grid=(rows // block,),
+        in_specs=[
+            pl.BlockSpec((block, width), lambda i: (i, 0)),
+            pl.BlockSpec((block, width), lambda i: (i, 0)),
+            pl.BlockSpec((width, width), lambda i: (0, hidden // width)),
+            pl.BlockSpec((1, width), lambda i: (0, 0)),
+            pl.BlockSpec((width, hidden), lambda i: (0, 0)),
+        ],
+        out_specs=[
+            pl.BlockSpec((block, width), lambda i: (i, 0)),
+            pl.BlockSpec((block, hidden), lambda i: (i, 0)),
+            pl.BlockSpec((1, 1, width), lambda i: (i // per, 0, 0)),
+            pl.BlockSpec((1, 1, hidden), lambda i: (i // per, 0, 0)),
+        ],
+        compiler_params=pltpu.CompilerParams(vmem_limit_bytes=VMEM_BYTES),
+        cost_estimate=estimate(4 * rows * width * (hidden + width), rows * hidden * 4),
+        name="mlp",
+    )(x0, mixed, w_up_out, gain, w_up_out)
+
+
+def head_kernel(
+    xsum_ref, asum_ref, down_ref, head_ref, label_ref, alive_ref, whole_ref, total_ref,
+    loss_ref, dlogit_ref, pooled_ref, dx2_ref, dact_ref, *, classes
+):
+    asum = asum_ref[...]
+    high = asum.astype(BF)
+    low = (asum - high.astype(F32)).astype(BF)
+    whole = whole_ref[...]
+    down = down_ref[...]
+    pooled = (xsum_ref[...] + (dot(high, down, NT) + dot(low, down, NT))) / whole
+    pooled_low = pooled.astype(BF)
+    pooled_ref[...] = pooled_low
+    head = head_ref[...]
+    place = lax.broadcasted_iota(jnp.int32, (1, head.shape[1]), 1)
+    logits = jnp.where(place < classes, dot(pooled_low, head, NN), -1e30)
+    top = jnp.max(logits, -1, keepdims=True)
+    norm_log = top + jnp.log(jnp.sum(jnp.exp(logits - top), -1, keepdims=True))
+    hot = place == label_ref[...]
+    true_logit = jnp.sum(jnp.where(hot, logits, 0.0), -1, keepdims=True)
+    loss_ref[...] = jnp.broadcast_to(norm_log - true_logit, loss_ref.shape)
+    soft = jnp.exp(logits - norm_log) - hot.astype(F32)
+    d_logits = (soft * alive_ref[...] / total_ref[...]).astype(BF)
+    dlogit_ref[...] = d_logits
+    d_x2 = dot(d_logits, head, NT) / whole
+    dx2_ref[...] = d_x2
+    dact_ref[...] = dot(d_x2.astype(BF), down, NN)
+
+
+def head_step(xsum, asum, w_down_head, labels, alive, whole, total, classes):
+    rows, width = xsum.shape
+    hidden = asum.shape[1]
+    padded = w_down_head.shape[1] - hidden
+    full = pl.BlockSpec(memory_space=pltpu.VMEM)
+    spec = lambda shape, place: pl.BlockSpec(shape, lambda i: place)
+    return pl.pallas_call(
+        partial(head_kernel, classes=classes),
+        out_shape=(
+            jax.ShapeDtypeStruct((rows, 128), F32),
+            jax.ShapeDtypeStruct((rows, padded), BF),
+            jax.ShapeDtypeStruct((rows, width), BF),
+            jax.ShapeDtypeStruct((rows, width), F32),
+            jax.ShapeDtypeStruct((rows, hidden), F32),
+        ),
+        grid=(1,),
+        in_specs=[
+            spec((rows, width), (0, 0)),
+            spec((rows, hidden), (0, 0)),
+            spec((width, hidden), (0, 0)),
+            spec((width, padded), (0, hidden // padded)),
+            spec((rows, 1), (0, 0)),
+            spec((rows, 1), (0, 0)),
+            spec((rows, 1), (0, 0)),
+            spec((1, 1), (0, 0)),
+        ],
+        out_specs=[
+            spec((rows, 128), (0, 0)),
+            spec((rows, padded), (0, 0)),
+            spec((rows, width), (0, 0)),
+            spec((rows, width), (0, 0)),
+            spec((rows, hidden), (0, 0)),
+        ],
+        compiler_params=pltpu.CompilerParams(vmem_limit_bytes=VMEM_BYTES),
+        cost_estimate=estimate(1 << 32, 8 << 20),
+        name="head",
+    )(xsum, asum, w_down_head, w_down_head, labels, alive, whole, total)
+
+
+def mlp_back_kernel(*refs, steps):
+    parts = (refs[0:5], refs[5:10])
+    wout_ref, gain_ref, wup_ref = refs[10:13]
+    outs = (refs[13:15], refs[15:17])
+    gup_ref, gout_ref, ggain_ref = refs[17:20]
+    up_acc, out_acc = refs[20:22]
+    step = pl.program_id(0)
+
+    def body(inputs, outputs, begin):
+        slope_ref, dact_ref, x1_ref, dx2_ref, mixed_ref = inputs
+        dx1_ref, dmixed_ref = outputs
+        gain = gain_ref[...]
+        hat, scale = normed(x1_ref[...])
+        h2_t = (hat * gain).astype(BF).T
+        d_h2 = 0.0
+        width = 768
+        for first in range(0, slope_ref.shape[1], width):
+            cols = slice(first, first + width)
+            d_inner = (slope_ref[:, cols].astype(F32) * dact_ref[0, :, cols]).astype(BF)
+            d_h2 = d_h2 + dot(d_inner, wup_ref[:, cols], NT)
+            grad = dot(h2_t, d_inner, NN)
+            up_acc[:, cols] = grad if begin else up_acc[:, cols] + grad
+        gain_grad = jnp.sum(d_h2 * hat, 0, keepdims=True)
+        ggain_ref[...] = gain_grad if begin else ggain_ref[...] + gain_grad
+        d_x1 = dx2_ref[0] + norm_back(d_h2, gain, hat, scale)
+        dx1_ref[...] = d_x1
+        d_attn = d_x1.astype(BF)
+        grad = dot(mixed_ref[...].T, d_attn, NN)
+        out_acc[...] = grad if begin else out_acc[...] + grad
+        dmixed_ref[...] = dot(d_attn, wout_ref[...], NT).astype(BF)
+
+    @pl.when(step == 0)
+    def _():
+        body(parts[1], outs[1], True)
+
+    @pl.when(step > 0)
+    def _():
+        body(parts[0], outs[0], False)
+
+    @pl.when(step == steps)
+    def _():
+        gup_ref[...] = up_acc[...].astype(BF)
+        gout_ref[...] = out_acc[...].astype(BF)
+
+
+def mlp_back(part_b, part_a, w_up_out, gain, images, block):
+    slope_b, dact_b, x1_b, dx2_b, mixed_b = part_b
+    slope_a, dact_a, x1_a, dx2_a, mixed_a = part_a
+    rows, width = x1_b.shape
+    rows_a = x1_a.shape[0]
+    hidden = slope_b.shape[1]
+    steps = rows // block
+    per = steps // images
+    at = lambda i: jnp.maximum(i - 1, 0)
+    moving = lambda cols: pl.BlockSpec((block, cols), lambda i: (at(i), 0))
+    still = lambda shape: pl.BlockSpec(shape, lambda i: (0,) * len(shape))
+    image = lambda cols: pl.BlockSpec((1, 1, cols), lambda i: (at(i) // per, 0, 0))
+    return pl.pallas_call(
+        partial(mlp_back_kernel, steps=steps),
+        out_shape=(
+            jax.ShapeDtypeStruct((rows, width), F32),
+            jax.ShapeDtypeStruct((rows, width), BF),
+            jax.ShapeDtypeStruct((rows_a, width), F32),
+            jax.ShapeDtypeStruct((rows_a, width), BF),
+            jax.ShapeDtypeStruct((width, hidden), BF),
+            jax.ShapeDtypeStruct((width, width), BF),
+            jax.ShapeDtypeStruct((1, width), F32),
+        ),
+        grid=(steps + 1,),
+        in_specs=[
+            moving(hidden), image(hidden), moving(width), image(width), moving(width),
+            still((rows_a, hidden)), still((1, 1, hidden)), still((rows_a, width)),
+            still((1, 1, width)), still((rows_a, width)),
+            pl.BlockSpec((width, width), lambda i: (0, hidden // width)),
+            still((1, width)),
+            still((width, hidden)),
+        ],
+        out_specs=[
+            moving(width), moving(width), still((rows_a, width)), still((rows_a, width)),
+            still((width, hidden)), still((width, width)), still((1, width)),
+        ],
+        scratch_shapes=[pltpu.VMEM((width, hidden), F32), pltpu.VMEM((width, width), F32)],
+        compiler_params=pltpu.CompilerParams(vmem_limit_bytes=VMEM_BYTES),
+        cost_estimate=estimate(
+            4 * (rows + rows_a) * width * (hidden + width), (rows + rows_a) * hidden * 4
+        ),
+        name="mlp_back",
+    )(slope_b, dact_b, x1_b, dx2_b, mixed_b, slope_a, dact_a, x1_a, dx2_a, mixed_a,
+      w_up_out, gain, w_up_out)
+
+
+def qkv_grad_kernel(*refs, steps, groups):
+    n_in = 1 + groups
+    parts = (refs[0:n_in], refs[n_in : 2 * n_in])
+    gain_ref = refs[2 * n_in]
+    out_ref, acc = refs[2 * n_in + 1], refs[2 * n_in + 2]
+    step = pl.program_id(0)
+
+    def body(inputs, begin):
+        h1_t = (normed(inputs[0][...])[0] * gain_ref[...]).astype(BF).T
+        first = 0
+        for ref in inputs[1:]:
+            cols = slice(first, first + ref.shape[1])
+            first += ref.shape[1]
+            grad = dot(h1_t, ref[...], NN)
+            acc[:, cols] = grad if begin else acc[:, cols] + grad
+
+    @pl.when(step == 0)
+    def _():
+        body(parts[1], True)
+
+    @pl.when(step > 0)
+    def _():
+        body(parts[0], False)
+
+    @pl.when(step == steps)
+    def _():
+        out_ref[...] = acc[...].astype(BF)
+
+
+def qkv_grad(x0_b, d_b, x0_a, d_a, gain, block):
+    rows, width = x0_b.shape
+    rows_a = x0_a.shape[0]
+    steps = rows // block
+    at = lambda i: jnp.maximum(i - 1, 0)
+    moving = lambda cols: pl.BlockSpec((block, cols), lambda i: (at(i), 0))
+    still = lambda shape: pl.BlockSpec(shape, lambda i: (0,) * len(shape))
+    total = sum(piece.shape[1] for piece in d_b)
+    return pl.pallas_call(
+        partial(qkv_grad_kernel, steps=steps, groups=len(d_b)),
+        out_shape=jax.ShapeDtypeStruct((width, total), BF),
+        grid=(steps + 1,),
+        in_specs=[moving(width)]
+        + [moving(piece.shape[1]) for piece in d_b]
+        + [still((rows_a, width))]
+        + [still((rows_a, piece.shape[1])) for piece in d_a]
+        + [still((1, width))],
+        out_specs=still((width, total)),
+        scratch_shapes=[pltpu.VMEM((width, total), F32)],
+        compiler_params=pltpu.CompilerParams(vmem_limit_bytes=VMEM_BYTES),
+        cost_estimate=estimate(2 * (rows + rows_a) * width * total, (rows + rows_a) * total * 4),
+        name="qkv_grad",
+    )(x0_b, *d_b, x0_a, *d_a, gain)
+
+
+def embed_back_kernel(*refs, steps, groups, places):
+    n_in = 3 + groups
+    parts = (refs[0:n_in], refs[n_in : 2 * n_in])
+    gain_ref, qkvw_ref = refs[2 * n_in : 2 * n_in + 2]
+    outs = refs[2 * n_in + 2 : 2 * n_in + 4]
+    ggain_ref = refs[2 * n_in + 4]
+    step = pl.program_id(0)
+
+    def body(inputs, out_ref, begin, first_of_sum):
+        x0_ref, dx1_ref, flat_ref = inputs[:3]
+        gain = gain_ref[...]
+        hat, scale = normed(x0_ref[...])
+        d_h1 = 0.0
+        for ref, (first, width) in zip(inputs[3:], places):
+            d_h1 = d_h1 + dot(ref[...], qkvw_ref[:, first : first + width], NT)
+        gain_grad = jnp.sum(d_h1 * hat, 0, keepdims=True)
+        ggain_ref[...] = gain_grad if first_of_sum else ggain_ref[...] + gain_grad
+        d_x0 = (dx1_ref[...] + norm_back(d_h1, gain, hat, scale)).astype(BF)
+        grad = dot(d_x0.T, flat_ref[...], NN)
+        if begin is None:
+            out_ref[...] = grad
+        else:
+            out_ref[...] = jnp.where(begin, 0.0, out_ref[...]) + grad
+
+    @pl.when(step == 0)
+    def _():
+        outs[0][...] = jnp.zeros_like(outs[0])
+        body(parts[1], outs[1], None, True)
+
+    @pl.when(step > 0)
+    def _():
+        body(parts[0], outs[0], False, False)
+
+
+def embed_back(x0_b, dx1_b, flat_b, d_b, x0_a, dx1_a, flat_a, d_a, gain, w_qkv, places, block):
+    rows, width = x0_b.shape
+    rows_a = x0_a.shape[0]
+    steps = rows // block
+    at = lambda i: jnp.maximum(i - 1, 0)
+    moving = lambda array: pl.BlockSpec((block, array.shape[1]), lambda i: (at(i), 0))
+    still = lambda shape: pl.BlockSpec(shape, lambda i: (0,) * len(shape))
+    inputs_b = (x0_b, dx1_b, flat_b, *d_b)
+    inputs_a = (x0_a, dx1_a, flat_a, *d_a)
+    return pl.pallas_call(
+        partial(embed_back_kernel, steps=steps, groups=len(d_b), places=tuple(places)),
+        out_shape=(
+            jax.ShapeDtypeStruct((width, flat_b.shape[1]), F32),
+            jax.ShapeDtypeStruct((width, flat_a.shape[1]), F32),
+            jax.ShapeDtypeStruct((1, width), F32),
+        ),
+        grid=(steps + 1,),
+        in_specs=[moving(array) for array in inputs_b]
+        + [still(array.shape) for array in inputs_a]
+        + [still((1, width)), still(w_qkv.shape)],
+        out_specs=[
+            still((width, flat_b.shape[1])),
+            still((width, flat_a.shape[1])),
+            still((1, width)),
+        ],
+        compiler_params=pltpu.CompilerParams(vmem_limit_bytes=VMEM_BYTES),
+        cost_estimate=estimate(
+            2 * (rows + rows_a) * width * (w_qkv.shape[1] + 640), (rows + rows_a) * 10000
+        ),
+        name="embed_back",
+    )(*inputs_b, *inputs_a, gain, w_qkv)
+
+
+def after(value, *others):
+    return lax.optimization_barrier((value, *others))[0]
+
+
+def padded_cols(array, width):
+    return jnp.pad(array, ((0, 0), (0, width - array.shape[1])))
+
+
+def round_up(count, unit):
+    return -(-count // unit) * unit
+
+
+def fast_step(
+    pixels_a, pixels_b, labels_a, labels_b, live_a, live_b, masters, firsts, seconds
+):
+    qkv_w, out_w, mlp_w, kern_w, pos_w, head_w, gains = masters
+    places = Places()
+    z, x, core, y = places.z, places.x, places.core, places.y
+    seq = lax.axis_size("seq")
+    row = lax.axis_index("seq")
+    lead = (row == 0).astype(F32)
+    width = HEADS * HEAD_DIM
+    hidden = mlp_w.shape[2]
+    classes = head_w.shape[1]
+    classes_up = round_up(classes, 1024)
+    rows_own = qkv_w.shape[0]
+
+    images_a, rows_a, grid_a, depth_a = pixels_a.shape
+    images_b, rows_b, grid_b, depth_b = pixels_b.shape
+    own_b = images_b // seq
+    parts_b, tabs_b = [], []
+    table_b = jnp.asarray(place_table(grid_b))
+    table_a = jnp.asarray(place_table(grid_a))
+    span_b, span_a = rows_b * grid_b, rows_a * grid_a
+    for step in range(seq):
+        part = lax.dynamic_slice_in_dim(pixels_b, ((row + step) % seq) * own_b, own_b, 0)
+        parts_b.append(places.send(part, y, step) if step else part)
+        tabs_b.append(lax.dynamic_slice_in_dim(table_b, ((row - step) % seq) * span_b, span_b, 0))
+    tab_a = lax.dynamic_slice_in_dim(table_a, row * span_a, span_a, 0)
+    whole_a, whole_b = grid_a * grid_a, grid_b * grid_b
+
+    tables = [resize_table(PATCH_B), resize_table(PATCH_A)]
+    sizes = [3 * table.shape[0] for table in tables]
+    kern_cols = lax.all_to_all(
+        kern_w.astype(BF).T, AXES, split_axis=0, concat_axis=1, tiled=True
+    )
+    kern_cols = kern_cols.astype(F32).reshape(rows_own, 3, BASE * BASE)
+    resized = [
+        jnp.einsum("dck,pk->dcp", kern_cols, jnp.asarray(table), precision=HIGH).reshape(
+            rows_own, -1
+        )
+        for table in tables
+    ]
+    small = jnp.concatenate(
+        [piece.astype(BF) for piece in resized] + [pos_w.astype(BF).T, gains.astype(BF).T], 1
+    )
+    small_width = small.shape[1]
+    small = padded_cols(small, round_up(small_width, 128))
+
+    def gather_halves(value):
+        cut = value.shape[1] // 2
+        return [
+            places.gather(value[:, :cut], (z, x, y, core)),
+            places.gather(value[:, cut:], (z, y, x, core)),
+        ]
+
+    qkv_halves = gather_halves(qkv_w.astype(BF))
+    w_small = place_blocks([places.gather(small, (z, x, y, core))])
+    w_qkv = place_blocks(qkv_halves)
+    up_out = jnp.concatenate([mlp_w[0].astype(BF), out_w.astype(BF)], 1)
+    up_out = after(up_out, qkv_halves[0][0][0], qkv_halves[1][0][0])
+    up_halves = gather_halves(up_out)
+    down_head = jnp.concatenate(
+        [mlp_w[1].astype(BF), padded_cols(head_w.astype(BF), classes_up)], 1
+    )
+    down_head = after(down_head, up_halves[0][0][0], up_halves[1][0][0])
+    down_halves = gather_halves(down_head)
+
+    count = jnp.stack([jnp.sum(live_a), jnp.sum(live_b)]).astype(F32).reshape(1, 2)
+    count = places.sum_all(count, (z, x, core))
+    total = jnp.maximum(jnp.sum(count), 1.0)
+
+    small_t = w_small.T
+    pos_rows = small_t[sum(sizes) : sum(sizes) + 49]
+    gain_rows = small_t[sum(sizes) + 49 : sum(sizes) + 51].astype(F32)
+    gain1, gain2 = gain_rows[0:1], gain_rows[1:2]
+
+    def embedding(rows, tab, kernel):
+        depth = round_up(rows.shape[1] + 98, 128)
+        flat = padded_cols(jnp.concatenate([rows, tab], 1), depth)
+        weight = jnp.concatenate([kernel, pos_rows, pos_rows], 0)
+        return flat, jnp.pad(weight, ((0, depth - weight.shape[0]), (0, 0)))
+
+    pix_b = jnp.concatenate(parts_b, 1).reshape(own_b * whole_b, depth_b)
+    tab_b = jnp.broadcast_to(
+        jnp.concatenate(tabs_b, 0)[None], (own_b, whole_b, 98)
+    ).reshape(-1, 98)
+    flat_b, weight_b = embedding(pix_b, tab_b, small_t[: sizes[0]])
+    flat_a, weight_a = embedding(
+        pixels_a.reshape(span_a, depth_a), tab_a, small_t[sizes[0] : sizes[0] + sizes[1]]
+    )
+    block = 256
+    x0_a, qkv_a = embed(flat_a, weight_a, gain1, w_qkv, span_a)
+    kv_a = [qkv_a[:, width:]]
+    kv_a += [places.send(kv_a[0], y, step) for step in range(1, seq)]
+    x0_b, qkv_b = embed(flat_b, weight_b, gain1, w_qkv, block)
+    pairs = HEADS // 2
+    cols_b = (0, pairs, 2 * pairs)
+    cols_a = (0, 0, pairs)
+    mixed_b, log_b = attend_pairs(qkv_b, qkv_b, qkv_b, cols_b, own_b, whole_b, whole_b)
+    kv_a = jnp.concatenate(kv_a, 0)
+    mixed_a, log_a = attend_pairs(qkv_a, kv_a, kv_a, cols_a, 1, span_a, seq * span_a)
+
+    w_up_out = place_blocks(up_halves)
+    x1_a, slope_a, xsum_a, asum_a = mlp(x0_a, mixed_a, w_up_out, gain2, 1, span_a)
+    sums_a = places.sum_all(jnp.concatenate([xsum_a[0], asum_a[0]], 1), (y,))
+    x1_b, slope_b, xsum_b, asum_b = mlp(x0_b, mixed_b, w_up_out, gain2, own_b, block)
+    w_down_head = place_blocks(down_halves)
+
+    rows_up = round_up(own_b + 1, 8)
+    fill = rows_up - own_b - 1
+    stack = lambda first, last: jnp.pad(
+        jnp.concatenate([first, last], 0), ((0, fill), (0, 0))
+    )
+    xsum = stack(xsum_b[:, 0], sums_a[:, :width])
+    asum = stack(asum_b[:, 0], sums_a[:, width:])
+    mine = lambda array: lax.dynamic_slice_in_dim(array, row * own_b, own_b, 0)[:, None]
+    labels = stack(mine(labels_b), labels_a[:, None])
+    alive_b = mine(live_b).astype(F32)
+    alive_a = live_a.astype(F32)[:, None]
+    alive = stack(alive_b, alive_a)
+    whole = np.ones((rows_up, 1), np.float32)
+    whole[:own_b], whole[own_b] = whole_b, whole_a
+    losses, d_logits, pooled, d_x2, d_act = head_step(
+        xsum, asum, w_down_head, labels, alive, jnp.asarray(whole), total.reshape(1, 1), classes
+    )
+    loss_sums = jnp.stack(
+        [lead * jnp.sum(alive_a * losses[own_b : own_b + 1, :1]),
+         jnp.sum(alive_b * losses[:own_b, :1])]
+    ).reshape(1, 2)
+    loss_sums = places.sum_all(loss_sums, (z, x, core, y))
+
+    once = jnp.concatenate(
+        [jnp.ones((own_b, 1), F32), lead.reshape(1, 1), jnp.zeros((fill, 1), F32)], 0
+    ).astype(BF)
+    rows_out = jnp.concatenate(
+        [asum.astype(BF), pooled, d_x2.astype(BF) * once, d_logits * once], 1
+    )
+    image_rows, _ = places.gather(rows_out, (z, x, y, core))
+    image_rows = jnp.concatenate(image_rows, 0).reshape(places.count * rows_up, -1)
+
+    part = lambda array, lo, hi: array[lo:hi][:, None]
+    d_x1_b, d_mixed_b, d_x1_a, d_mixed_a, grad_up, grad_out, grad_gain2 = mlp_back(
+        (slope_b, part(d_act, 0, own_b), x1_b, part(d_x2, 0, own_b), mixed_b),
+        (slope_a, part(d_act, own_b, own_b + 1), x1_a, part(d_x2, own_b, own_b + 1), mixed_a),
+        w_up_out, gain2, own_b, block,
+    )
+    cut = hidden // 2
+    own_up = [
+        places.scatter_sum(grad_up[:, :cut], (core, x, y, z)),
+        places.scatter_sum(grad_up[:, cut:], (core, y, x, z)),
+    ]
+    own_out = places.scatter_sum(grad_out, (core, x, y, z))
+
+    dq_a, dk_a, dv_a = attend_back_pairs(
+        qkv_a, kv_a, kv_a, cols_a, d_mixed_a, mixed_a, log_a, 1, span_a, seq * span_a, (0, pairs)
+    )
+    dkv_a = jnp.concatenate([dk_a, dv_a], 1)
+    dkv_own = dkv_a[:span_a].astype(F32)
+    for step in range(1, seq):
+        dkv_own = dkv_own + places.send(
+            dkv_a[step * span_a : (step + 1) * span_a], y, seq - step
+        ).astype(F32)
+    dkv_own = dkv_own.astype(BF)
+
+    group_sets = ((0, pairs // 2), (pairs // 2, pairs))
+    d_parts_b, d_parts_a, spots, own_groups = [], [], [], []
+    for begin, end in group_sets:
+        got = attend_back_pairs(
+            qkv_b, qkv_b, qkv_b, cols_b, d_mixed_b, mixed_b, log_b, own_b, whole_b, whole_b,
+            (begin, end),
+        )
+        lo, hi = begin * 128, end * 128
+        from_a = (dq_a[:, lo:hi], dkv_own[:, lo:hi], dkv_own[:, width + lo : width + hi])
+        grad = qkv_grad(x0_b, got, x0_a, from_a, gain1, block)
+        order = (core, x, y, z) if begin else (core, y, x, z)
+        own_groups.append(places.scatter_sum(grad, order))
+        d_parts_b += got
+        d_parts_a += from_a
+        spots += [(lo, hi - lo), (width + lo, hi - lo), (2 * width + lo, hi - lo)]
+    grad_b, grad_a, grad_gain1 = embed_back(
+        x0_b, d_x1_b, flat_b, d_parts_b, x0_a, d_x1_a, flat_a, d_parts_a, gain1, w_qkv, spots, block
+    )
+    span = hi - lo
+    own_qkv = jnp.concatenate(
+        [group[:, k * span : (k + 1) * span] for k in range(3) for group in own_groups], 1
+    )
+    twice = lambda array, at: array[:, at : at + 49] + array[:, at + 49 : at + 98]
+    grad_small = jnp.concatenate(
+        [
+            grad_b[:, : sizes[0]],
+            grad_a[:, : sizes[1]],
+            twice(grad_b, sizes[0]) + twice(grad_a, sizes[1]),
+            grad_gain1.T,
+            grad_gain2.T,
+        ],
+        1,
+    )
+    grad_small = padded_cols(grad_small, round_up(small_width, 128)).astype(BF)
+    own_small = places.scatter_sum(grad_small, (core, x, y, z))
+    kern_t = jnp.zeros((rows_own, 3, BASE * BASE), F32)
+    first = 0
+    for table, size in zip(tables, sizes):
+        piece = own_small[:, first : first + size].reshape(rows_own, 3, -1)
+        kern_t = kern_t + jnp.einsum("dcp,pk->dck", piece, jnp.asarray(table), precision=HIGH)
+        first += size
+    kern_t = kern_t.reshape(rows_own, -1)
+    own_pos = own_small[:, first : first + 49].T
+    own_gain = own_small[:, first + 49 : first + 51].T
+    own_kern = lax.all_to_all(kern_t, AXES, split_axis=1, concat_axis=0, tiled=True).T
+
+    mine_at = places.flat * rows_own
+    columns = lambda lo: lax.dynamic_slice_in_dim(
+        image_rows[:, lo : lo + width], mine_at, rows_own, 1
+    )
+    own_down = lax.dot_general(
+        columns(hidden + width), image_rows[:, :hidden], ROWS_DIM, preferred_element_type=F32
+    )
+    own_head = lax.dot_general(
+        columns(hidden),
+        image_rows[:, hidden + 2 * width : hidden + 2 * width + classes],
+        ROWS_DIM,
+        preferred_element_type=F32,
+    )
+    own_up = jnp.concatenate(own_up, 1)
+    own_mlp = jnp.stack([own_up, own_down], 0)
+    owned = (own_qkv, own_out, own_mlp, own_kern, own_pos, own_head, own_gain)
+    square_sum = sum(
+        jnp.sum(piece * piece)
+        for piece in (own_qkv, own_out, own_up, own_down, kern_t, own_pos, own_head, own_gain)
+    )
+    grad_norm = jnp.sqrt(places.sum_all(square_sum.reshape(1, 1), (z, x, core, y)))[0, 0]
+    factor = jnp.minimum(1.0, CLIP / (grad_norm + 1e-06))
+    done = [adamw(masters[i], firsts[i], seconds[i], owned[i] * factor, RATES[i]) for i in range(7)]
+    size_stats = (loss_sums / jnp.maximum(count, 1.0))[0]
+    return (
+        *(item[0] for item in done),
+        *(item[1] for item in done),
+        *(item[2] for item in done),
+        size_stats,
+        grad_norm,
+    )
+
+
+def fits_fast(pixels_a, pixels_b, qkv_w):
+    dp, seq = lax.axis_size("dp"), lax.axis_size("seq")
+    images_b, rows_b, grid_b, _ = pixels_b.shape
+    span_a = pixels_a.shape[1] * pixels_a.shape[2]
+    return (
+        dp % 8 == 0
+        and images_b % seq == 0
+        and pixels_a.shape[0] == 1
+        and grid_b * grid_b % 256 == 0
+        and span_a % 32 == 0
+    )
 
 
 def on_device(
@@ -136,6 +1064,10 @@
     masters = (qkv_w, out_w, mlp_w, kern_w, pos_w, head_w, gains)
     firsts = (qkv_m, out_m, mlp_m, kern_m, pos_m, head_m, gains_m)
     seconds = (qkv_v, out_v, mlp_v, kern_v, pos_v, head_v, gains_v)
+    if fits_fast(pixels_a, pixels_b, qkv_w):
+        return fast_step(
+            pixels_a, pixels_b, labels_a, labels_b, live_a, live_b, masters, firsts, seconds
+        )
     bf16 = jnp.bfloat16
     w_qkv, w_out, w_mlp, w_kern, w_pos, w_head, w_gain = (
         lax.all_gather(qkv_w.astype(bf16), ("dp", "seq"), axis=0, tiled=True),

time: 2190 us -> 826 us (0.38)
  matrix products: 600 us -> 5.81 us
  waiting for transfers between devices: 704 us -> 145 us
  Pallas kernels: 0 us -> 343 us
  blocking collectives: 250 us -> 0 us
  local copies, waits for them, and re-layouts: 329 us -> 101 us
  other arithmetic: 264 us -> 55 us
  starting transfers between devices: 2.41 us -> 151 us
    dot_general x51 -> x6, matrix products: 600 us -> 5.81 us  [the longest x1 1.74 us: fast_step(): lax.dot_general(columns(hidden + width), image_rows[:, :hidden], ROWS_DIM...]
    reduce_scatter x5 -> x0, waiting for transfers between devices: 437 us -> none  [the longest x1 211 us: on_device(): lax.psum_scatter(grad_mlp, ('dp', 'seq'), scatter_dimension=1, tiled=True)]
    pallas_call x0 -> x18, Pallas kernels: none -> 343 us  [the longest x3 77.5 us: attend_back_pairs(): pl.pallas_call(attend_back_kernel, out_shape=(jax.ShapeDtypeStruct((image...]
    ppermute x2 -> x105, starting transfers between devices: 1.53 us -> 140 us  [send(): return lax.ppermute(value, AXES, pairs)]
    all_gather x2 -> x0, blocking collectives: 131 us -> none  [the longest x1 66.1 us: on_device(): lax.all_gather(gains.astype(bf16), ('dp', 'seq'), axis=1, tiled=True)]
    ppermute x2 -> x105, waiting for transfers between devices: 267 us -> 145 us  [send(): return lax.ppermute(value, AXES, pairs)]
    convert_element_type x13 -> x9, other arithmetic: 108 us -> 2.6 us  [the longest x1 1.23 us: fast_step(): jnp.stack([jnp.sum(live_a), jnp.sum(live_b)]).astype(F32).reshape(1, 2)]
    reshape x13 -> x3, local copies, waits for them, and re-layouts: 106 us -> 2.24 us  [the longest x1 1.83 us: place_blocks(): return out.reshape(count * rows, first)]
  transfers between devices with their start and end apart: 13 -> 107, of which waited for: 5 -> 36; matrix products, arithmetic and copies ran while one was open for 33% -> 17% of each run, Pallas kernels for 0% -> 26%
where the time goes in v1:
time: 826 us; the launch traced here: 816 us
  Pallas kernels  343 us (42%)
  starting transfers between devices  151 us (18%)
  waiting for transfers between devices  145 us (18%)
  local copies, waits for them, and re-layouts  101 us (12%)
  other arithmetic  55 us (7%)
  between operations  15.9 us (2%)
    ppermute x105, waiting for transfers between devices, send(): return lax.ppermute(value, AXES, pairs)  145 us
    ppermute x105, starting transfers between devices, send(): return lax.ppermute(value, AXES, pairs)  140 us
    pallas_call x3, Pallas kernels, attend_back_pairs(): pl.pallas_call(attend_back_kernel, out_shape=(jax.ShapeDtypeStruct((image...  77.5 us
    pallas_call x2, Pallas kernels, mlp(): pl.pallas_call(partial(mlp_kernel, per=per), out_shape=(jax.ShapeDtypeStr...  54.8 us
    pallas_call x2, Pallas kernels, attend_pairs(): pl.pallas_call(attend_kernel, out_shape=(jax.ShapeDtypeStruct((images * n...  51.1 us
    pallas_call x1, Pallas kernels, mlp_back(): pl.pallas_call(partial(mlp_back_kernel, steps=steps), out_shape=(jax.Shap...  45.1 us
    unnamed x205, local copies, waits for them, and re-layouts  37.2 us
    pallas_call x1, Pallas kernels, embed_back(): pl.pallas_call(partial(embed_back_kernel, steps=steps, groups=len(d_b), p...  31.2 us
  transfers between devices with their start and end apart: 107, of which 36 were waited for; matrix products, arithmetic and copies ran while one was open for 17% of the time, Pallas kernels for 26%

profile of v1, /device:TPU:1, one launch (start us, length us, event | category | flops | bytes accessed | tf_op | source)
XLA Modules:
  0.0 816.5 jit_solution(16058364527416432929)
XLA Ops:
  16.1 5.0 all-to-all-start
  59.8 15.8 %collective-permute-done.16 = bf16[4,24,1152]{2,1,0:T(8,128)(2,1)S(1)} collective-permute-done((bf16[4,24,1152]{2,1,0:T(8,128)(2,1)S(1)}, bf16[4,24,1152]{2,1,0:T(8,128)(2,1)S(1)}, u32[]{:S(2)}, u32[]{:S(2)}) %collective-permute-start.16) | collective-permute-done | bytes 221216 | tf_op jit(solution)/shard_map/ppermute | solution.py:139
  85.9 9.0 %collective-permute-done.4 = bf16[4,24,896]{2,1,0:T(8,128)(2,1)S(1)} collective-permute-done((bf16[4,24,896]{2,1,0:T(8,128)(2,1)S(1)}, bf16[4,24,896]{2,1,0:T(8,128)(2,1)S(1)}, u32[]{:S(2)}, u32[]{:S(2)}) %collective-permute-start.4) | collective-permute-done | bytes 172064 | tf_op jit(solution)/shard_map/ppermute | solution.py:139
  98.0 5.6 collective-permute-start.12
  105.5 5.3 collective-permute-done.19
  118.4 3.3 collective-permute-done.25
  122.4 4.6 collective-permute-done.26
  132.9 4.4 collective-permute-start.6
  145.0 3.3 place_blocks.4
  152.9 5.0 place_blocks.5
  157.9 19.0 %embed.2 = (f32[2048,768]{1,0:T(8,128)}, bf16[2048,2304]{1,0:T(8,128)(2,1)}) custom-call(bf16[2048,640]{1,0:T(8,128)(2,1)} %fusion.2.flat_ref.refs_2_, bf16[640,768]{1,0:T(8,128)(2,1)} %fusion.13.weight_ref, f32[1,768]{1,0:T(1,128)} %get-tuple-element.388.gain_ref.refs_8_.refs_18_, bf16[768,2304]{1,0:T(8,128)(2,1)} %bitcast.330), custom_call_target="tpu_custom_call" | custom-call | flops 9261023232 | bytes 25165824 | tf_op jit(solution)/shard_map/embed/pallas_call | solution.py:286
  177.0 41.7 %attend.2 = (bf16[2048,768]{1,0:T(8,128)(2,1)}, f32[2,6,2,1024]{3,2,1,0:T(2,128)}) custom-call(bf16[2048,2304]{1,0:T(8,128)(2,1)} %get-tuple-element.66.q_ref.k_ref.v_ref, bf16[2048,2304]{1,0:T(8,128)(2,1)} %get-tuple-element.66.q_ref.k_ref.v_ref, bf16[2048,2304]{1,0:T(8,128)(2,1)} %get-tuple-element.66.q_ref.k_ref.v_ref), custom_call_target="tpu_custom_call" | custom-call | flops 40265318400 | bytes 12582912 | tf_op jit(solution)/shard_map/attend/pallas_call | solution.py:339
  218.7 5.4 embed.3
  238.0 3.3 collective-permute-done.34
  241.4 3.3 collective-permute-start.41
  245.7 4.1 collective-permute-done.40
  255.1 4.1 collective-permute-done.36
  263.6 9.4 %attend.3 = (bf16[288,768]{1,0:T(8,128)(2,1)}, f32[1,6,2,288]{3,2,1,0:T(2,128)}) custom-call(bf16[288,2304]{1,0:T(8,128)(2,1)} %get-tuple-element.72.q_ref, bf16[576,1536]{1,0:T(8,128)(2,1)} %pad_maximum_fusion.1.k_ref.v_ref, bf16[576,1536]{1,0:T(8,128)(2,1)} %pad_maximum_fusion.1.k_ref.v_ref), custom_call_target="tpu_custom_call" | custom-call | flops 3185049600 | bytes 2654208 | tf_op jit(solution)/shard_map/attend/pallas_call | solution.py:339
  273.0 4.4 collective-permute-done.37
  283.4 6.5 place_blocks.6
  289.9 9.8 %mlp.3 = (f32[288,768]{1,0:T(8,128)}, bf16[288,3072]{1,0:T(8,128)(2,1)}, f32[1,1,768]{2,1,0:T(1,128)}, f32[1,1,3072]{2,1,0:T(1,128)}) custom-call(f32[288,768]{1,0:T(8,128)} %get-tuple-element.71.x0_ref.refs_4_.refs_9_, bf16[288,768]{1,0:T(8,128)(2,1)} %get-tuple-element.73.mixed_ref.refs_9_.o_ref, bf16[768,3840]{1,0:T(8,128)(2,1)} %bitcast.324, ...), custom_call_target="tpu_custom_call" | custom-call | flops 3397386240 | bytes 3538944 | tf_op jit(solution)/shard_map/mlp/pallas_call | solution.py:461
  301.0 45.1 %mlp.2 = (f32[2048,768]{1,0:T(8,128)}, bf16[2048,3072]{1,0:T(8,128)(2,1)}, f32[2,1,768]{2,1,0:T(1,128)}, f32[2,1,3072]{2,1,0:T(1,128)}) custom-call(f32[2048,768]{1,0:T(8,128)} %get-tuple-element.65.x0_ref.refs_0_, bf16[2048,768]{1,0:T(8,128)(2,1)} %get-tuple-element.67.mixed_ref.refs_4_.o_ref, bf16[768,3840]{1,0:T(8,128)(2,1)} %bitcast.326, ...), custom_call_target="tpu_custom_call" | custom-call | flops 24159191040 | bytes 25165824 | tf_op jit(solution)/shard_map/mlp/pallas_call | solution.py:461
  349.0 6.9 place_blocks.7
  355.8 7.9 head.1
  369.4 45.1 %mlp_back.1 = (f32[2048,768]{1,0:T(8,128)}, bf16[2048,768]{1,0:T(8,128)(2,1)}, f32[288,768]{1,0:T(8,128)}, bf16[288,768]{1,0:T(8,128)(2,1)}, bf16[768,3072]{1,0:...) custom-call(bf16[2048,3072]{1,0:T(8,128)(2,1)} %get-tuple-element.69.refs_0_, ...), custom_call_target="tpu_custom_call" | custom-call | flops 27556577280 | bytes 28704768 | tf_op jit(solution)/shard_map/mlp_back/pallas_call | solution.py:613
  414.5 33.4 %attend_back.5 = (bf16[2048,384]{1,0:T(8,128)(2,1)}, bf16[2048,384]{1,0:T(8,128)(2,1)}, bf16[2048,384]{1,0:T(8,128)(2,1)}) custom-call(bf16[2048,2304]{1,0:T(8,128)(2,1)} %get-tuple-element.66.q_ref.k_ref.v_ref, bf16[2048,2304]{1,0:T(8,128)(2,1)} %get-tuple-element.66.q_ref.k_ref.v_ref, bf16[2048,2304]{1,0:T(8,128)(2,1)} %get-tuple-element.66.q_ref.k_ref.v_ref, ...), custom_call_target="tpu_custom_call" | custom-call | flops 36490444800 | bytes 12582912 | tf_op jit(solution)/shard_map/attend_back/pallas_call | solution.py:397
  448.0 33.3 %attend_back.3 = (bf16[2048,384]{1,0:T(8,128)(2,1)}, bf16[2048,384]{1,0:T(8,128)(2,1)}, bf16[2048,384]{1,0:T(8,128)(2,1)}) custom-call(bf16[2048,2304]{1,0:T(8,128)(2,1)} %get-tuple-element.66.q_ref.k_ref.v_ref, bf16[2048,2304]{1,0:T(8,128)(2,1)} %get-tuple-element.66.q_ref.k_ref.v_ref, bf16[2048,2304]{1,0:T(8,128)(2,1)} %get-tuple-element.66.q_ref.k_ref.v_ref, ...), custom_call_target="tpu_custom_call" | custom-call | flops 36490444800 | bytes 12582912 | tf_op jit(solution)/shard_map/attend_back/pallas_call | solution.py:397
  493.7 10.8 %attend_back.4 = (bf16[288,768]{1,0:T(8,128)(2,1)}, bf16[576,768]{1,0:T(8,128)(2,1)}, bf16[576,768]{1,0:T(8,128)(2,1)}) custom-call(bf16[288,2304]{1,0:T(8,128)(2,1)} %get-tuple-element.72.q_ref, bf16[576,1536]{1,0:T(8,128)(2,1)} %pad_maximum_fusion.1.k_ref.v_ref, bf16[576,1536]{1,0:T(8,128)(2,1)} %pad_maximum_fusion.1.k_ref.v_ref, ...), custom_call_target="tpu_custom_call" | custom-call | flops 5772902400 | bytes 5308416 | tf_op jit(solution)/shard_map/attend_back/pallas_call | solution.py:397
  522.5 3.7 collective-permute-start.103
  528.0 7.3 collective-permute-done.104
  543.5 5.6 collective-permute-done.84
  552.9 5.5 collective-permute-done.64
  560.5 14.4 %qkv_grad.3 = bf16[768,1152]{1,0:T(8,128)(2,1)} custom-call(f32[2048,768]{1,0:T(8,128)} %get-tuple-element.65.x0_ref.refs_0_, bf16[2048,384]{1,0:T(8,128)(2,1)} %get-tuple-element.93.refs_1_.refs_6_, bf16[2048,384]{1,0:T(8,128)(2,1)} %get-tuple-element.94.refs_2_.refs_7_, bf16[2048,384]{1,0:T(8,128)(2,1)} %get-tuple-element.95.refs_3_.refs_8_, ...), custom_call_target="tpu_custom_call" | custom-call | flops 4133486592 | bytes 10764288 | tf_op jit(solution)/shard_map/qkv_grad/pallas_call | solution.py:684
  574.9 14.6 %qkv_grad.2 = bf16[768,1152]{1,0:T(8,128)(2,1)} custom-call(f32[2048,768]{1,0:T(8,128)} %get-tuple-element.65.x0_ref.refs_0_, bf16[2048,384]{1,0:T(8,128)(2,1)} %get-tuple-element.85.refs_1_.refs_3_, bf16[2048,384]{1,0:T(8,128)(2,1)} %get-tuple-element.86.refs_2_.refs_4_, bf16[2048,384]{1,0:T(8,128)(2,1)} %get-tuple-element.87.refs_3_.refs_5_, ...), custom_call_target="tpu_custom_call" | custom-call | flops 4133486592 | bytes 10764288 | tf_op jit(solution)/shard_map/qkv_grad/pallas_call | solution.py:684
  592.5 31.2 %embed_back.1 = (f32[768,640]{1,0:T(8,128)}, f32[768,512]{1,0:T(8,128)}, f32[1,768]{1,0:T(1,128)}) custom-call(f32[2048,768]{1,0:T(8,128)} %get-tuple-element.65.x0_ref.refs_0_, f32[2048,768]{1,0:T(8,128)} %get-tuple-element.100.refs_1_, bf16[2048,640]{1,0:T(8,128)(2,1)} %fusion.2.flat_ref.refs_2_, bf16[2048,384]{1,0:T(8,128)(2,1)} %get-tuple-element.85.refs_1_.refs_3_, ...), custom_call_target="tpu_custom_call" | custom-call | flops 10563354624 | bytes 23360000 | tf_op jit(solution)/shard_map/embed_back/pallas_call | solution.py:744
  642.2 3.6 collective-permute-start.69
  658.2 10.6 %collective-permute-done.76 = bf16[4,2,24,1536]{3,2,0,1:T(8,128)(2,1)S(1)} collective-permute-done((bf16[4,2,24,1536]{3,2,0,1:T(8,128)(2,1)S(1)}, bf16[4,2,24,1536]{3,2,0,1:T(8,128)(2,1)S(1)}, u32[]{:S(2)}, u32[]{:S(2)}) %collective-permute-start.76) | collective-permute-done | bytes 589856 | tf_op jit(solution)/shard_map/ppermute | solution.py:139
  674.1 3.3 collective-permute-done.88
  697.6 12.7 %collective-permute-done.91 = bf16[24,896]{0,1:T(8,128)(2,1)S(1)} collective-permute-done((bf16[24,896]{0,1:T(8,128)(2,1)S(1)}, bf16[24,896]{0,1:T(8,128)(2,1)S(1)}, u32[]{:S(2)}, u32[]{:S(2)}) %collective-permute-start.91) | collective-permute-done | bytes 43040 | tf_op jit(solution)/shard_map/ppermute | solution.py:139
  710.3 4.2 collective-permute-start.78
  718.6 5.6 all-to-all-start.1
  733.7 8.4 %collective-permute-done.73 = bf16[24,1536]{1,0:T(8,128)(2,1)S(1)} collective-permute-done((bf16[24,1536]{1,0:T(8,128)(2,1)}, bf16[24,1536]{1,0:T(8,128)(2,1)S(1)}, u32[]{:S(2)}, u32[]{:S(2)}) %collective-permute-start.73) | collective-permute-done | bytes 73760 | tf_op jit(solution)/shard_map/ppermute | solution.py:139
  748.2 3.5 collective-permute-done.53
  753.0 4.1 collective-permute-start.55
  757.2 3.3 collective-permute-start.62
  762.3 3.7 collective-permute-done.61
  779.7 4.0 collective-permute-start.95
  788.8 8.6 %collective-permute-start.97 = (f32[1,1]{1,0:T(1,128)}, f32[1,1]{1,0:T(1,128)}, u32[]{:S(2)}, u32[]{:S(2)}) collective-permute-start(f32[1,1]{1,0:T(1,128)} %add.948), channel_id=1, source_target_pairs={{0,2},{1,3},{2,0},{3,1},{4,6},{5,7},{6,4},{7,5},{8,10},{9,11},{10,... | collective-permute-start | bytes 20 | tf_op jit(solution)/shard_map/ppermute | solution.py:139
  (592 shorter events, 288.1 us)
Async XLA Ops:
  2.4 43.3 %collective-permute-start.7 = (bf16[1,24,1152]{2,1,0:T(8,128)(2,1)}, bf16[1,24,1152]{2,1,0:T(8,128)(2,1)}, u32[]{:S(2)}, u32[]{:S(2)}) collective-permute-start(bf16[1,24,1152]{2,1,0:T(8,128)(2,1)} %get-tuple-element.332), channel_id=1, source_target_pairs={{0,8},{1,9},{2,10},{3,11},{4,12},{5,13},{6,14},{7,15},{8,16},{9,17... | collective-permute-start | bytes 165896 | tf_op jit(solution)/shard_map/ppermute | solution.py:139
  4.5 42.4 %collective-permute-start.8 = (bf16[1,24,1152]{2,1,0:T(8,128)(2,1)}, bf16[1,24,1152]{2,1,0:T(8,128)(2,1)}, u32[]{:S(2)}, u32[]{:S(2)}) collective-permute-start(bf16[1,24,1152]{2,1,0:T(8,128)(2,1)} %get-tuple-element.332), channel_id=1, source_target_pairs={{0,16},{1,17},{2,18},{3,19},{4,20},{5,21},{6,22},{7,23},{8,24},{9,... | collective-permute-start | bytes 165896 | tf_op jit(solution)/shard_map/ppermute | solution.py:139
  6.8 41.3 %collective-permute-start.9 = (bf16[1,24,1152]{2,1,0:T(8,128)(2,1)}, bf16[1,24,1152]{2,1,0:T(8,128)(2,1)}, u32[]{:S(2)}, u32[]{:S(2)}) collective-permute-start(bf16[1,24,1152]{2,1,0:T(8,128)(2,1)} %get-tuple-element.332), channel_id=1, source_target_pairs={{0,24},{1,25},{2,26},{3,27},{4,28},{5,29},{6,30},{7,31},{8,0},{9,1... | collective-permute-start | bytes 165896 | tf_op jit(solution)/shard_map/ppermute | solution.py:139
  11.1 20.9 %collective-permute-start.46 = (f32[1,2]{1,0:T(1,128)}, f32[1,2]{1,0:T(1,128)S(1)}, u32[]{:S(2)}, u32[]{:S(2)}) collective-permute-start(f32[1,2]{1,0:T(1,128)} %add_convert_fusion.2), channel_id=1, source_target_pairs={{0,8},{1,9},{2,10},{3,11},{4,12},{5,13},{6,14},{7,15},{8,16},{9,17... | collective-permute-start | bytes 32 | tf_op jit(solution)/shard_map/ppermute | solution.py:139
  11.5 23.0 %collective-permute-start.47 = (f32[1,2]{1,0:T(1,128)}, f32[1,2]{1,0:T(1,128)S(1)}, u32[]{:S(2)}, u32[]{:S(2)}) collective-permute-start(f32[1,2]{1,0:T(1,128)} %add_convert_fusion.2), channel_id=1, source_target_pairs={{0,24},{1,25},{2,26},{3,27},{4,28},{5,29},{6,30},{7,31},{8,0},{9,1... | collective-permute-start | bytes 32 | tf_op jit(solution)/shard_map/ppermute | solution.py:139
  16.1 60.3 %all-to-all-start = ((bf16[32,24,96]{2,1,0:T(8,128)(2,1)}), bf16[32,24,96]{2,1,0:T(8,128)(2,1)}, u32[]{:S(2)}, u32[]{:S(2)}) async-start(bf16[32,24,96]{2,1,0:T(8,128)(2,1)} %bitcast.5), calls=%async_computation | async-start | bytes 393216 | tf_op jit(solution)/shard_map/all_to_all | solution.py:811
  34.4 15.9 %collective-permute-start.13 = (bf16[1,24,1152]{2,1,0:T(8,128)(2,1)}, bf16[1,24,1152]{2,1,0:T(8,128)(2,1)S(1)}, u32[]{:S(2)}, u32[]{:S(2)}) collective-permute-start(bf16[1,24,1152]{2,1,0:T(8,128)(2,1)} %get-tuple-element.331), channel_id=1, source_target_pairs={{0,8},{1,9},{2,10},{3,11},{4,12},{5,13},{6,14},{7,15},{8,16},{9,17... | collective-permute-start | bytes 165896 | tf_op jit(solution)/shard_map/ppermute | solution.py:139
  46.9 86.0 %collective-permute-start = (bf16[2,16,32,432]{3,2,1,0:T(8,128)(2,1)}, bf16[2,16,32,432]{3,2,1,0:T(8,128)(2,1)}, u32[]{:S(2)}, u32[]{:S(2)}) collective-permute-start(bf16[2,16,32,432]{3,2,1,0:T(8,128)(2,1)} %get-tuple-element.259), channel_id=1, source_target_pairs={{0,1},{1,0},{2,3},{3,2},{4,5},{5,4},{6,7},{7,6},{8,9},{9,8},{10,11... | collective-permute-start | bytes 2654216 | tf_op jit(solution)/shard_map/ppermute | solution.py:139
  51.2 24.5 %collective-permute-start.16 = (bf16[4,24,1152]{2,1,0:T(8,128)(2,1)S(1)}, bf16[4,24,1152]{2,1,0:T(8,128)(2,1)S(1)}, u32[]{:S(2)}, u32[]{:S(2)}) collective-permute-start(bf16[4,24,1152]{2,1,0:T(8,128)(2,1)S(1)} %pad_maximum_fusion.10), channel_id=1, source_target_pairs={{0,1},{1,0},{2,3},{3,2},{4,5},{5,4},{6,7},{7,6},{8,9},{9,8},{10,11... | collective-permute-start | bytes 663560 | tf_op jit(solution)/shard_map/ppermute | solution.py:139
  58.6 37.6 %collective-permute-start.11 = (bf16[8,24,1152]{2,1,0:T(8,128)(2,1)}, bf16[8,24,1152]{2,1,0:T(8,128)(2,1)}, u32[]{:S(2)}, u32[]{:S(2)}) collective-permute-start(bf16[8,24,1152]{2,1,0:T(8,128)(2,1)} %get-tuple-element.311), channel_id=1, source_target_pairs={{0,1},{1,0},{2,3},{3,2},{4,5},{5,4},{6,7},{7,6},{8,9},{9,8},{10,11... | collective-permute-start | bytes 1327112 | tf_op jit(solution)/shard_map/ppermute | solution.py:139
  83.7 19.9 %collective-permute-start.17 = (bf16[8,24,1152]{2,1,0:T(8,128)(2,1)}, bf16[8,24,1152]{2,1,0:T(8,128)(2,1)S(1)}, u32[]{:S(2)}, u32[]{:S(2)}) collective-permute-start(bf16[8,24,1152]{2,1,0:T(8,128)(2,1)} %get-tuple-element.309), channel_id=1, source_target_pairs={{0,4},{1,5},{2,6},{3,7},{4,0},{5,1},{6,2},{7,3},{8,12},{9,13},{10,... | collective-permute-start | bytes 1327112 | tf_op jit(solution)/shard_map/ppermute | solution.py:139
  94.9 37.6 %collective-permute-start.5 = (bf16[8,24,896]{2,1,0:T(8,128)(2,1)S(1)}, bf16[8,24,896]{2,1,0:T(8,128)(2,1)S(1)}, u32[]{:S(2)}, u32[]{:S(2)}) collective-permute-start(bf16[8,24,896]{2,1,0:T(8,128)(2,1)S(1)} %get-tuple-element.325), channel_id=1, source_target_pairs={{0,1},{1,0},{2,3},{3,2},{4,5},{5,4},{6,7},{7,6},{8,9},{9,8},{10,11... | collective-permute-start | bytes 1032200 | tf_op jit(solution)/shard_map/ppermute | solution.py:139
  98.0 54.9 %collective-permute-start.12 = (bf16[16,24,1152]{2,1,0:T(8,128)(2,1)}, bf16[16,24,1152]{2,1,0:T(8,128)(2,1)}, u32[]{:S(2)}, u32[]{:S(2)}) collective-permute-start(bf16[16,24,1152]{2,1,0:T(8,128)(2,1)} %constant_dynamic-update-slice_fusion.16.refs_0_), channel_id=1, source_target_pairs={{0,2},{1,3},{2,0},{3,1},{4,6},{5,7},{6,4},{7,5},{8,10},{9,11},{10,... | collective-permute-start | bytes 2654216 | tf_op jit(solution)/shard_map/ppermute | solution.py:139
  114.7 38.2 %collective-permute-start.18 = (bf16[16,24,1152]{2,1,0:T(8,128)(2,1)}, bf16[16,24,1152]{2,1,0:T(8,128)(2,1)}, u32[]{:S(2)}, u32[]{:S(2)}) collective-permute-start(bf16[16,24,1152]{2,1,0:T(8,128)(2,1)} %copy-done.40), channel_id=1, source_target_pairs={{0,2},{1,3},{2,0},{3,1},{4,6},{5,7},{6,4},{7,5},{8,10},{9,11},{10,... | collective-permute-start | bytes 2654216 | tf_op jit(solution)/shard_map/ppermute | solution.py:139
  141.8 83.8 %collective-permute-start.23 = (bf16[8,24,1920]{2,1,0:T(8,128)(2,1)}, bf16[8,24,1920]{2,1,0:T(8,128)(2,1)}, u32[]{:S(2)}, u32[]{:S(2)}) collective-permute-start(bf16[8,24,1920]{2,1,0:T(8,128)(2,1)} %get-tuple-element.295), channel_id=1, source_target_pairs={{0,1},{1,0},{2,3},{3,2},{4,5},{5,4},{6,7},{7,6},{8,9},{9,8},{10,11... | collective-permute-start | bytes 2211848 | tf_op jit(solution)/shard_map/ppermute | solution.py:139
  143.8 86.6 %collective-permute-start.29 = (bf16[8,24,1920]{2,1,0:T(8,128)(2,1)}, bf16[8,24,1920]{2,1,0:T(8,128)(2,1)}, u32[]{:S(2)}, u32[]{:S(2)}) collective-permute-start(bf16[8,24,1920]{2,1,0:T(8,128)(2,1)} %get-tuple-element.293), channel_id=1, source_target_pairs={{0,4},{1,5},{2,6},{3,7},{4,0},{5,1},{6,2},{7,3},{8,12},{9,13},{10,... | collective-permute-start | bytes 2211848 | tf_op jit(solution)/shard_map/ppermute | solution.py:139
  225.3 36.9 %collective-permute-start.31 = (bf16[288,1536]{1,0:T(8,128)(2,1)S(1)}, bf16[288,1536]{1,0:T(8,128)(2,1)S(1)}, u32[]{:S(2)}, u32[]{:S(2)}) collective-permute-start(bf16[288,1536]{1,0:T(8,128)(2,1)S(1)} %slice.175), channel_id=1, source_target_pairs={{0,1},{1,0},{2,3},{3,2},{4,5},{5,4},{6,7},{7,6},{8,9},{9,8},{10,11... | collective-permute-start | bytes 2654216 | tf_op jit(solution)/shard_map/ppermute | solution.py:139
  227.7 55.7 %collective-permute-start.24 = (bf16[16,24,1920]{2,1,0:T(8,128)(2,1)}, bf16[16,24,1920]{2,1,0:T(8,128)(2,1)}, u32[]{:S(2)}, u32[]{:S(2)}) collective-permute-start(bf16[16,24,1920]{2,1,0:T(8,128)(2,1)} %constant_dynamic-update-slice_fusion.38.refs_0_), channel_id=1, source_target_pairs={{0,2},{1,3},{2,0},{3,1},{4,6},{5,7},{6,4},{7,5},{8,10},{9,11},{10,... | collective-permute-start | bytes 4423688 | tf_op jit(solution)/shard_map/ppermute | solution.py:139
  244.7 38.7 %collective-permute-start.30 = (bf16[16,24,1920]{2,1,0:T(8,128)(2,1)S(1)}, bf16[16,24,1920]{2,1,0:T(8,128)(2,1)}, u32[]{:S(2)}, u32[]{:S(2)}) collective-permute-start(bf16[16,24,1920]{2,1,0:T(8,128)(2,1)S(1)} %constant_dynamic-update-slice_fusion.49.refs_2_), channel_id=1, source_target_pairs={{0,2},{1,3},{2,0},{3,1},{4,6},{5,7},{6,4},{7,5},{8,10},{9,11},{10,... | collective-permute-start | bytes 4423688 | tf_op jit(solution)/shard_map/ppermute | solution.py:139
  260.1 17.3 %collective-permute-start.37 = (bf16[8,24,2048]{2,1,0:T(8,128)(2,1)}, bf16[8,24,2048]{2,1,0:T(8,128)(2,1)}, u32[]{:S(2)}, u32[]{:S(2)}) collective-permute-start(bf16[8,24,2048]{2,1,0:T(8,128)(2,1)} %get-tuple-element.291), channel_id=1, source_target_pairs={{0,1},{1,0},{2,3},{3,2},{4,5},{5,4},{6,7},{7,6},{8,9},{9,8},{10,11... | collective-permute-start | bytes 2359304 | tf_op jit(solution)/shard_map/ppermute | solution.py:139
  261.2 20.5 %collective-permute-start.43 = (bf16[8,24,2048]{2,1,0:T(8,128)(2,1)}, bf16[8,24,2048]{2,1,0:T(8,128)(2,1)}, u32[]{:S(2)}, u32[]{:S(2)}) collective-permute-start(bf16[8,24,2048]{2,1,0:T(8,128)(2,1)} %get-tuple-element.289), channel_id=1, source_target_pairs={{0,4},{1,5},{2,6},{3,7},{4,0},{5,1},{6,2},{7,3},{8,12},{9,13},{10,... | collective-permute-start | bytes 2359304 | tf_op jit(solution)/shard_map/ppermute | solution.py:139
  278.5 70.4 %collective-permute-start.38 = (bf16[16,24,2048]{2,1,0:T(8,128)(2,1)S(1)}, bf16[16,24,2048]{2,1,0:T(8,128)(2,1)}, u32[]{:S(2)}, u32[]{:S(2)}) collective-permute-start(bf16[16,24,2048]{2,1,0:T(8,128)(2,1)S(1)} %constant_dynamic-update-slice_fusion.60.refs_0_), channel_id=1, source_target_pairs={{0,2},{1,3},{2,0},{3,1},{4,6},{5,7},{6,4},{7,5},{8,10},{9,11},{10,... | collective-permute-start | bytes 4718600 | tf_op jit(solution)/shard_map/ppermute | solution.py:139
  282.8 66.1 %collective-permute-start.44 = (bf16[16,24,2048]{2,1,0:T(8,128)(2,1)S(1)}, bf16[16,24,2048]{2,1,0:T(8,128)(2,1)}, u32[]{:S(2)}, u32[]{:S(2)}) collective-permute-start(bf16[16,24,2048]{2,1,0:T(8,128)(2,1)S(1)} %constant_dynamic-update-slice_fusion.71.refs_2_), channel_id=1, source_target_pairs={{0,2},{1,3},{2,0},{3,1},{4,6},{5,7},{6,4},{7,5},{8,10},{9,11},{10,... | collective-permute-start | bytes 4718600 | tf_op jit(solution)/shard_map/ppermute | solution.py:139
  300.4 47.1 %collective-permute-start.32 = (f32[1,3840]{1,0:T(1,128)S(1)}, f32[1,3840]{1,0:T(1,128)S(1)}, u32[]{:S(2)}, u32[]{:S(2)}) collective-permute-start(f32[1,3840]{1,0:T(1,128)S(1)} %pad_maximum_fusion.13), channel_id=1, source_target_pairs={{0,1},{1,0},{2,3},{3,2},{4,5},{5,4},{6,7},{7,6},{8,9},{9,8},{10,11... | collective-permute-start | bytes 46088 | tf_op jit(solution)/shard_map/ppermute | solution.py:139
  482.2 56.3 %collective-permute-start.81 = (bf16[1,8,5632]{2,1,0:T(8,128)(2,1)S(1)}, bf16[1,8,5632]{2,1,0:T(8,128)(2,1)}, u32[]{:S(2)}, u32[]{:S(2)}) collective-permute-start(bf16[1,8,5632]{2,1,0:T(8,128)(2,1)S(1)} %maximum_bitcast_fusion), channel_id=1, source_target_pairs={{0,8},{1,9},{2,10},{3,11},{4,12},{5,13},{6,14},{7,15},{8,16},{9,17... | collective-permute-start | bytes 270344 | tf_op jit(solution)/shard_map/ppermute | solution.py:139
  482.9 55.7 %collective-permute-start.82 = (bf16[1,8,5632]{2,1,0:T(8,128)(2,1)S(1)}, bf16[1,8,5632]{2,1,0:T(8,128)(2,1)S(1)}, u32[]{:S(2)}, u32[]{:S(2)}) collective-permute-start(bf16[1,8,5632]{2,1,0:T(8,128)(2,1)S(1)} %maximum_bitcast_fusion), channel_id=1, source_target_pairs={{0,16},{1,17},{2,18},{3,19},{4,20},{5,21},{6,22},{7,23},{8,24},{9,... | collective-permute-start | bytes 270344 | tf_op jit(solution)/shard_map/ppermute | solution.py:139
  486.0 52.6 %collective-permute-start.83 = (bf16[1,8,5632]{2,1,0:T(8,128)(2,1)S(1)}, bf16[1,8,5632]{2,1,0:T(8,128)(2,1)S(1)}, u32[]{:S(2)}, u32[]{:S(2)}) collective-permute-start(bf16[1,8,5632]{2,1,0:T(8,128)(2,1)S(1)} %maximum_bitcast_fusion), channel_id=1, source_target_pairs={{0,24},{1,25},{2,26},{3,27},{4,28},{5,29},{6,30},{7,31},{8,0},{9,1... | collective-permute-start | bytes 270344 | tf_op jit(solution)/shard_map/ppermute | solution.py:139
  490.4 25.4 %collective-permute-start.100 = (f32[1,2]{1,0:T(1,128)S(1)}, f32[1,2]{1,0:T(1,128)S(1)}, u32[]{:S(2)}, u32[]{:S(2)}) collective-permute-start(f32[1,2]{1,0:T(1,128)S(1)} %maximum_bitcast_fusion.1), channel_id=1, source_target_pairs={{0,8},{1,9},{2,10},{3,11},{4,12},{5,13},{6,14},{7,15},{8,16},{9,17... | collective-permute-start | bytes 32 | tf_op jit(solution)/shard_map/ppermute | solution.py:139
  491.3 24.5 %collective-permute-start.101 = (f32[1,2]{1,0:T(1,128)S(1)}, f32[1,2]{1,0:T(1,128)S(1)}, u32[]{:S(2)}, u32[]{:S(2)}) collective-permute-start(f32[1,2]{1,0:T(1,128)S(1)} %maximum_bitcast_fusion.1), channel_id=1, source_target_pairs={{0,24},{1,25},{2,26},{3,27},{4,28},{5,29},{6,30},{7,31},{8,0},{9,1... | collective-permute-start | bytes 32 | tf_op jit(solution)/shard_map/ppermute | solution.py:139
  515.8 35.9 %collective-permute-start.50 = (bf16[288,1536]{1,0:T(8,128)(2,1)S(1)}, bf16[288,1536]{1,0:T(8,128)(2,1)S(1)}, u32[]{:S(2)}, u32[]{:S(2)}) collective-permute-start(bf16[288,1536]{1,0:T(8,128)(2,1)S(1)} %slice.230), channel_id=1, source_target_pairs={{0,1},{1,0},{2,3},{3,2},{4,5},{5,4},{6,7},{7,6},{8,9},{9,8},{10,11... | collective-permute-start | bytes 2654216 | tf_op jit(solution)/shard_map/ppermute | solution.py:139
  535.3 15.8 %collective-permute-start.63 = (bf16[4,2,2,24,768]{4,3,0,2,1:T(8,128)(2,1)S(1)}, bf16[4,2,2,24,768]{4,3,0,2,1:T(8,128)(2,1)S(1)}, u32[]{:S(2)}, u32[]{:S(2)}) collective-permute-start(bf16[4,2,2,24,768]{4,3,0,2,1:T(8,128)(2,1)S(1)} %bitcast.358), channel_id=1, source_target_pairs={{0,2},{1,3},{2,0},{3,1},{4,6},{5,7},{6,4},{7,5},{8,10},{9,11},{10,... | collective-permute-start | bytes 1769480 | tf_op jit(solution)/shard_map/ppermute | solution.py:139
  538.6 113.0 %collective-permute-start.75 = (bf16[4,2,2,24,1536]{4,3,0,1,2:T(8,128)(2,1)}, bf16[4,2,2,24,1536]{4,3,0,1,2:T(8,128)(2,1)}, u32[]{:S(2)}, u32[]{:S(2)}) collective-permute-start(bf16[4,2,2,24,1536]{4,3,0,1,2:T(8,128)(2,1)} %bitcast.314), channel_id=1, source_target_pairs={{0,2},{1,3},{2,0},{3,1},{4,6},{5,7},{6,4},{7,5},{8,10},{9,11},{10,... | collective-permute-start | bytes 3538952 | tf_op jit(solution)/shard_map/ppermute | solution.py:139
  550.2 99.0 %collective-permute-start.85 = (bf16[8,8,5632]{2,1,0:T(8,128)(2,1)}, bf16[8,8,5632]{2,1,0:T(8,128)(2,1)}, u32[]{:S(2)}, u32[]{:S(2)}) collective-permute-start(bf16[8,8,5632]{2,1,0:T(8,128)(2,1)} %get-tuple-element.299), channel_id=1, source_target_pairs={{0,1},{1,0},{2,3},{3,2},{4,5},{5,4},{6,7},{7,6},{8,9},{9,8},{10,11... | collective-permute-start | bytes 2162696 | tf_op jit(solution)/shard_map/ppermute | solution.py:139
  559.9 75.0 %collective-permute-start.65 = (bf16[4,24,768]{2,1,0:T(8,128)(2,1)}, bf16[4,24,768]{2,1,0:T(8,128)(2,1)}, u32[]{:S(2)}, u32[]{:S(2)}) collective-permute-start(bf16[4,24,768]{2,1,0:T(8,128)(2,1)} %fusion.43), channel_id=1, source_target_pairs={{0,1},{1,0},{2,3},{3,2},{4,5},{5,4},{6,7},{7,6},{8,9},{9,8},{10,11... | collective-permute-start | bytes 442376 | tf_op jit(solution)/shard_map/ppermute | solution.py:139
  646.2 25.8 %collective-permute-start.57 = (bf16[4,2,2,24,1152]{4,3,0,2,1:T(8,128)(2,1)S(1)}, bf16[4,2,2,24,1152]{4,3,0,2,1:T(8,128)(2,1)S(1)}, u32[]{:S(2)}, u32[]{:S(2)}) collective-permute-start(bf16[4,2,2,24,1152]{4,3,0,2,1:T(8,128)(2,1)S(1)} %bitcast.355), channel_id=1, source_target_pairs={{0,2},{1,3},{2,0},{3,1},{4,6},{5,7},{6,4},{7,5},{8,10},{9,11},{10,... | collective-permute-start | bytes 2654216 | tf_op jit(solution)/shard_map/ppermute | solution.py:139
  651.6 117.9 %collective-permute-start.86 = (bf16[16,8,5632]{2,1,0:T(8,128)(2,1)}, bf16[16,8,5632]{2,1,0:T(8,128)(2,1)}, u32[]{:S(2)}, u32[]{:S(2)}) collective-permute-start(bf16[16,8,5632]{2,1,0:T(8,128)(2,1)} %get-tuple-element.273), channel_id=1, source_target_pairs={{0,2},{1,3},{2,0},{3,1},{4,6},{5,7},{6,4},{7,5},{8,10},{9,11},{10,... | collective-permute-start | bytes 4325384 | tf_op jit(solution)/shard_map/ppermute | solution.py:139
  653.8 15.0 %collective-permute-start.76 = (bf16[4,2,24,1536]{3,2,0,1:T(8,128)(2,1)S(1)}, bf16[4,2,24,1536]{3,2,0,1:T(8,128)(2,1)S(1)}, u32[]{:S(2)}, u32[]{:S(2)}) collective-permute-start(bf16[4,2,24,1536]{3,2,0,1:T(8,128)(2,1)S(1)} %fusion.17), channel_id=1, source_target_pairs={{0,1},{1,0},{2,3},{3,2},{4,5},{5,4},{6,7},{7,6},{8,9},{9,8},{10,11... | collective-permute-start | bytes 1769480 | tf_op jit(solution)/shard_map/ppermute | solution.py:139
  655.2 15.4 %collective-permute-start.70 = (bf16[4,2,24,1536]{3,2,0,1:T(8,128)(2,1)S(1)}, bf16[4,2,24,1536]{3,2,0,1:T(8,128)(2,1)S(1)}, u32[]{:S(2)}, u32[]{:S(2)}) collective-permute-start(bf16[4,2,24,1536]{3,2,0,1:T(8,128)(2,1)S(1)} %fusion.16), channel_id=1, source_target_pairs={{0,4},{1,5},{2,6},{3,7},{4,0},{5,1},{6,2},{7,3},{8,12},{9,13},{10,... | collective-permute-start | bytes 1769480 | tf_op jit(solution)/shard_map/ppermute | solution.py:139
  655.9 21.5 %collective-permute-start.88 = (bf16[4,2,24,896]{3,2,1,0:T(8,128)(2,1)S(1)}, bf16[4,2,24,896]{3,2,1,0:T(8,128)(2,1)S(1)}, u32[]{:S(2)}, u32[]{:S(2)}) collective-permute-start(bf16[4,2,24,896]{3,2,1,0:T(8,128)(2,1)S(1)} %fusion.27), channel_id=1, source_target_pairs={{0,4},{1,5},{2,6},{3,7},{4,0},{5,1},{6,2},{7,3},{8,12},{9,13},{10,... | collective-permute-start | bytes 1032200 | tf_op jit(solution)/shard_map/ppermute | solution.py:139
  668.8 75.5 %collective-permute-start.52 = (bf16[4,2,24,1152]{3,2,0,1:T(8,128)(2,1)}, bf16[4,2,24,1152]{3,2,0,1:T(8,128)(2,1)}, u32[]{:S(2)}, u32[]{:S(2)}) collective-permute-start(bf16[4,2,24,1152]{3,2,0,1:T(8,128)(2,1)} %fusion.24), channel_id=1, source_target_pairs={{0,1},{1,0},{2,3},{3,2},{4,5},{5,4},{6,7},{7,6},{8,9},{9,8},{10,11... | collective-permute-start | bytes 1327112 | tf_op jit(solution)/shard_map/ppermute | solution.py:139
  672.0 14.4 %collective-permute-start.71 = (bf16[4,24,1536]{2,1,0:T(8,128)(2,1)}, bf16[4,24,1536]{2,1,0:T(8,128)(2,1)}, u32[]{:S(2)}, u32[]{:S(2)}) collective-permute-start(bf16[4,24,1536]{2,1,0:T(8,128)(2,1)} %fusion.30), channel_id=1, source_target_pairs={{0,1},{1,0},{2,3},{3,2},{4,5},{5,4},{6,7},{7,6},{8,9},{9,8},{10,11... | collective-permute-start | bytes 884744 | tf_op jit(solution)/shard_map/ppermute | solution.py:139
  690.7 19.5 %collective-permute-start.91 = (bf16[24,896]{0,1:T(8,128)(2,1)S(1)}, bf16[24,896]{0,1:T(8,128)(2,1)S(1)}, u32[]{:S(2)}, u32[]{:S(2)}) collective-permute-start(bf16[24,896]{0,1:T(8,128)(2,1)S(1)} %get-tuple-element.262), channel_id=1, source_target_pairs={{0,16},{1,17},{2,18},{3,19},{4,20},{5,21},{6,22},{7,23},{8,24},{9,... | collective-permute-start | bytes 129032 | tf_op jit(solution)/shard_map/ppermute | solution.py:139
  691.8 18.5 %collective-permute-start.90 = (bf16[24,896]{0,1:T(8,128)(2,1)S(1)}, bf16[24,896]{0,1:T(8,128)(2,1)S(1)}, u32[]{:S(2)}, u32[]{:S(2)}) collective-permute-start(bf16[24,896]{0,1:T(8,128)(2,1)S(1)} %get-tuple-element.260), channel_id=1, source_target_pairs={{0,8},{1,9},{2,10},{3,11},{4,12},{5,13},{6,14},{7,15},{8,16},{9,17... | collective-permute-start | bytes 129032 | tf_op jit(solution)/shard_map/ppermute | solution.py:139
  696.1 28.7 %collective-permute-start.80 = (bf16[24,1536]{1,0:T(8,128)(2,1)}, bf16[24,1536]{1,0:T(8,128)(2,1)S(1)}, u32[]{:S(2)}, u32[]{:S(2)}) collective-permute-start(bf16[24,1536]{1,0:T(8,128)(2,1)} %get-tuple-element.279), channel_id=1, source_target_pairs={{0,24},{1,25},{2,26},{3,27},{4,28},{5,29},{6,30},{7,31},{8,0},{9,1... | collective-permute-start | bytes 221192 | tf_op jit(solution)/shard_map/ppermute | solution.py:139
  710.3 17.8 %collective-permute-start.79 = (bf16[24,1536]{1,0:T(8,128)(2,1)S(1)}, bf16[24,1536]{1,0:T(8,128)(2,1)S(1)}, u32[]{:S(2)}, u32[]{:S(2)}) collective-permute-start(bf16[24,1536]{1,0:T(8,128)(2,1)S(1)} %get-tuple-element.280), channel_id=1, source_target_pairs={{0,16},{1,17},{2,18},{3,19},{4,20},{5,21},{6,22},{7,23},{8,24},{9,... | collective-permute-start | bytes 221192 | tf_op jit(solution)/shard_map/ppermute | solution.py:139
  710.3 17.8 %collective-permute-start.78 = (bf16[24,1536]{1,0:T(8,128)(2,1)S(1)}, bf16[24,1536]{1,0:T(8,128)(2,1)S(1)}, u32[]{:S(2)}, u32[]{:S(2)}) collective-permute-start(bf16[24,1536]{1,0:T(8,128)(2,1)S(1)} %get-tuple-element.278), channel_id=1, source_target_pairs={{0,8},{1,9},{2,10},{3,11},{4,12},{5,13},{6,14},{7,15},{8,16},{9,17... | collective-permute-start | bytes 221192 | tf_op jit(solution)/shard_map/ppermute | solution.py:139
  718.6 94.3 %all-to-all-start.1 = ((f32[24,32,96]{2,0,1:T(8,128)}), f32[24,32,96]{2,0,1:T(8,128)}, u32[]{:S(2)}, u32[]{:S(2)}) async-start(f32[24,32,96]{2,0,1:T(8,128)} %copy.281), calls=%async_computation.1 | async-start | bytes 786432 | tf_op jit(solution)/shard_map/all_to_all | solution.py:987
  732.5 14.3 %collective-permute-start.58 = (bf16[4,2,24,1152]{3,2,0,1:T(8,128)(2,1)S(1)}, bf16[4,2,24,1152]{3,2,0,1:T(8,128)(2,1)S(1)}, u32[]{:S(2)}, u32[]{:S(2)}) collective-permute-start(bf16[4,2,24,1152]{3,2,0,1:T(8,128)(2,1)S(1)} %copy-done.45), channel_id=1, source_target_pairs={{0,4},{1,5},{2,6},{3,7},{4,0},{5,1},{6,2},{7,3},{8,12},{9,13},{10,... | collective-permute-start | bytes 1327112 | tf_op jit(solution)/shard_map/ppermute | solution.py:139
  (140 other events, 1475.9 us)

commit v2 on v0

--- a/solution.py
+++ b/solution.py
@@ -1,8 +1,14 @@
+import math
 from functools import partial
 
 import jax
 import jax.numpy as jnp
+import ml_dtypes
+import numpy as np
 from jax import lax
+from jax.experimental import pallas as pl
+from jax.experimental.pallas import tpu as pltpu
+from jax.sharding import Mesh
 from jax.sharding import PartitionSpec as P
 
 HEADS = 12
@@ -102,6 +108,964 @@
 def grid_shape(size_sets, index):
     pixels = size_sets[index][0]
     return (pixels.shape[1], pixels.shape[2], -1)
+
+
+AXES = ("z", "x", "core", "y")
+CHIPS = ("z", "x", "y")
+NT = (((1,), (1,)), ((), ()))
+NN = (((1,), (0,)), ((), ()))
+BF = jnp.bfloat16
+F32 = jnp.float32
+VMEM_BYTES = 58 << 20
+
+
+def shift(value, axis, steps):
+    count = lax.axis_size(axis)
+    pairs = [(source, (source + steps) % count) for source in range(count)]
+    return lax.ppermute(value, axis, pairs)
+
+
+def chip_sizes():
+    return tuple(lax.axis_size(axis) for axis in CHIPS)
+
+
+def gather_rows(value, token=None):
+    rows, cols = value.shape
+    z, x, y = chip_sizes()
+    chips = z * x * y
+    copies = jnp.broadcast_to(value[None], (chips, rows, cols)).reshape(chips * rows, cols)
+    mine = lax.all_to_all(copies, CHIPS, split_axis=0, concat_axis=0, tiled=True)
+    mine = mine if token is None else after(mine, token)
+    other = shift(mine, "core", 1)
+    parts = [part.reshape(z, x, 1, y, rows, cols) for part in (mine, other)]
+    first = lax.axis_index("core") == 0
+    both = jnp.concatenate(
+        [jnp.where(first, parts[0], parts[1]), jnp.where(first, parts[1], parts[0])], 2
+    )
+    return both.reshape(2 * chips * rows, cols)
+
+
+def scatter_rows(away, own):
+    z, x, y = chip_sizes()
+    chips = z * x * y
+    both = (own.astype(F32) + shift(away, "core", 1).astype(F32)).astype(BF)
+    got = lax.all_to_all(both, CHIPS, split_axis=0, concat_axis=0, tiled=True)
+    return jnp.sum(got.reshape(chips, own.shape[0] // chips, own.shape[1]).astype(F32), 0)
+
+
+def store_by_core(core, acc, away_ref, own_ref, count):
+    rows = acc.shape[0] // count // 2
+    for pair in range(count):
+        at = slice(pair * rows, (pair + 1) * rows)
+        for side, ref in ((core, own_ref), (1 - core, away_ref)):
+            first = pl.multiple_of((2 * pair + side) * rows, rows)
+            ref[at, :] = acc[pl.ds(first, rows), :].astype(BF)
+
+
+def interp_table(n_out, n_in):
+    places = np.arange(n_out) * ((n_in - 1) / (n_out - 1))
+    return np.maximum(0.0, 1.0 - np.abs(places[:, None] - np.arange(n_in)[None, :]))
+
+
+def resize_table(patch):
+    basis = interp_table(patch, BASE)
+    table = np.linalg.solve(basis @ basis.T, basis)
+    return np.kron(table, table).astype(np.float32)
+
+
+def place_table(grid):
+    table = interp_table(grid, 7)
+    full = np.kron(table, table).astype(np.float32)
+    high = full.astype(ml_dtypes.bfloat16)
+    low = (full - high.astype(np.float32)).astype(ml_dtypes.bfloat16)
+    return np.concatenate([high, low, np.zeros((grid * grid, 30), ml_dtypes.bfloat16)], 1)
+
+
+def dot(left, right, dims):
+    return lax.dot_general(left, right, dims, preferred_element_type=F32)
+
+
+def estimate(flops, nbytes, share=32):
+    return pl.CostEstimate(
+        flops=int(flops) // share, bytes_accessed=int(nbytes) // share, transcendentals=0
+    )
+
+
+def normed(values):
+    centred = values - jnp.mean(values, -1, keepdims=True)
+    scale = lax.rsqrt(jnp.mean(centred * centred, -1, keepdims=True) + 1e-06)
+    return centred * scale, scale
+
+
+def norm_back(d_out, gain, hat, scale):
+    d_hat = d_out * gain
+    return scale * (
+        d_hat
+        - jnp.mean(d_hat, -1, keepdims=True)
+        - hat * jnp.mean(d_hat * hat, -1, keepdims=True)
+    )
+
+
+def embed_kernel(*refs, pieces, at, depth, spot):
+    pixel_refs, (tab_ref, weight_ref, gain_ref, *rest) = refs[:pieces], refs[pieces:]
+    x0_ref, h1_ref = rest
+    base = dot(tab_ref[...], weight_ref[:, spot : spot + tab_ref.shape[1]], NT)
+
+    def body(pixel_ref):
+        x0 = base + dot(pixel_ref[...], weight_ref[:, at : at + depth], NT)
+        x0_ref[...] = x0
+        h1_ref[...] = (normed(x0)[0] * gain_ref[...]).astype(BF)
+
+    for piece, pixel_ref in enumerate(pixel_refs):
+        pl.when(pl.program_id(1) == piece)(partial(body, pixel_ref))
+
+
+def embed(pieces, tab, weight, at, spot, gain, images):
+    count, depth = len(pieces), pieces[0].shape[1]
+    block = tab.shape[0] // count
+    rows, width = images * tab.shape[0], weight.shape[0]
+    still = lambda array: pl.BlockSpec(array.shape, lambda i, j: (0, 0))
+    moving = lambda cols: pl.BlockSpec((block, cols), lambda i, j: (i * count + j, 0))
+    outs = [(width, F32), (width, BF)]
+    return pl.pallas_call(
+        partial(embed_kernel, pieces=count, at=at, depth=depth, spot=spot),
+        out_shape=tuple(jax.ShapeDtypeStruct((rows, cols), kind) for cols, kind in outs),
+        grid=(images, count),
+        in_specs=[pl.BlockSpec((block, depth), lambda i, j: (i, 0))] * count
+        + [pl.BlockSpec((block, tab.shape[1]), lambda i, j: (j, 0)), still(weight), still(gain)],
+        out_specs=[moving(cols) for cols, _ in outs],
+        compiler_params=pltpu.CompilerParams(vmem_limit_bytes=VMEM_BYTES),
+        cost_estimate=estimate(2 * rows * width * width, rows * width * 8, 1),
+        name="embed",
+    )(*pieces, tab, weight, gain)
+
+
+def head_split(first, values):
+    zero = jnp.zeros((), values.dtype)
+    return jnp.where(first, values, zero), jnp.where(first, zero, values)
+
+
+def attend_pair(rows_ref, n_query, out_ref, log_ref, between=None):
+    lane = lax.broadcasted_iota(jnp.int32, (1, 128), 1)
+    first = lane < HEAD_DIM
+    one = jnp.ones((), BF)
+    values = rows_ref[:, 256:]
+    keys = head_split(first, rows_ref[:, 128:256])
+    sided = (jnp.where(first, values, one).T, jnp.where(first, one, values).T)
+    query = rows_ref[:n_query, :128] * jnp.asarray(HEAD_DIM**-0.5, BF)
+    scores = [dot(keys[head], query, NT) for head in range(2)]
+    if between is not None:
+        between()
+    tops, probs, mixed = [], [], []
+    for head in range(2):
+        tops.append(jnp.max(scores[head], 0, keepdims=True))
+        probs.append(jnp.exp(scores[head] - tops[head]).astype(BF))
+        mixed.append(dot(sided[head], probs[head], NN))
+    outs = []
+    for head in range(2):
+        at = HEAD_DIM * (1 - head)
+        total = mixed[head][at : at + 1]
+        own = HEAD_DIM * head
+        outs.append(mixed[head][own : own + HEAD_DIM] / total)
+        log_ref[0, 0, head : head + 1, :] = tops[head] + jnp.log(total)
+    out_ref[...] = jnp.concatenate(outs, 0).T.astype(BF)
+
+
+def attend_kernel(h1_ref, weight_ref, qkv_ref, out_ref, log_ref, held, *, items, n_query):
+    step = pl.program_id(0)
+
+    def project():
+        rows = dot(h1_ref[...], weight_ref[...], NN).astype(BF)
+        qkv_ref[...] = rows
+        held[step % 2] = rows
+
+    def attend(between=None):
+        attend_pair(held.at[(step + 1) % 2], n_query, out_ref, log_ref, between)
+
+    @pl.when(step == 0)
+    def _():
+        project()
+
+    @pl.when((step > 0) & (step < items))
+    def _():
+        attend(project)
+
+    @pl.when(step == items)
+    def _():
+        attend()
+
+
+def attend_pairs(h1, weight, images, n_query):
+    rows, width = h1.shape
+    count = rows // images
+    pairs = weight.shape[1] // 384
+    items = images * pairs
+    now = lambda s: jnp.minimum(s, items - 1)
+    last = lambda s: jnp.maximum(s - 1, 0)
+    return pl.pallas_call(
+        partial(attend_kernel, items=items, n_query=n_query),
+        out_shape=(
+            jax.ShapeDtypeStruct((rows, pairs * 384), BF),
+            jax.ShapeDtypeStruct((images * n_query, pairs * 128), BF),
+            jax.ShapeDtypeStruct((images, pairs, 2, n_query), F32),
+        ),
+        grid=(items + 1,),
+        in_specs=[
+            pl.BlockSpec((count, width), lambda s: (now(s) // pairs, 0)),
+            pl.BlockSpec((width, 384), lambda s: (0, now(s) % pairs)),
+        ],
+        out_specs=[
+            pl.BlockSpec((count, 384), lambda s: (now(s) // pairs, now(s) % pairs)),
+            pl.BlockSpec((n_query, 128), lambda s: (last(s) // pairs, last(s) % pairs)),
+            pl.BlockSpec(
+                (1, 1, 2, n_query), lambda s: (last(s) // pairs, last(s) % pairs, 0, 0)
+            ),
+        ],
+        scratch_shapes=[pltpu.VMEM((2, count, 384), BF)],
+        compiler_params=pltpu.CompilerParams(vmem_limit_bytes=VMEM_BYTES),
+        cost_estimate=estimate(
+            2 * items * count * (n_query * 1200 + width * 384), rows * width * 8, 1
+        ),
+        name="attend",
+    )(h1, weight)
+
+
+def attend_back_pair(q_ref, kv_ref, do_ref, o_ref, log_ref):
+    lane = lax.broadcasted_iota(jnp.int32, (1, 128), 1)
+    first = lane < HEAD_DIM
+    scale = jnp.asarray(HEAD_DIM**-0.5, BF)
+    keys_all = kv_ref[:, 128:256]
+    keys = head_split(first, keys_all)
+    values = head_split(first, kv_ref[:, 256:])
+    query = q_ref[:, :128] * scale
+    d_out = do_ref[...]
+    queries = head_split(first, query)
+    d_outs = head_split(first, d_out)
+    keys_t = tuple(part.T for part in head_split(first, keys_all * scale))
+    both = (d_out.astype(F32) * o_ref[...].astype(F32)).T
+    d_query, d_keys, d_values = 0.0, 0.0, 0.0
+    for head in range(2):
+        row = jnp.sum(both[HEAD_DIM * head : HEAD_DIM * (head + 1)], 0, keepdims=True)
+        scores = dot(keys[head], query, NT)
+        probs = jnp.exp(scores - log_ref[0, 0, head : head + 1, :])
+        d_probs = dot(values[head], d_out, NT)
+        d_scores = (probs * (d_probs - row)).astype(BF)
+        d_keys = d_keys + dot(d_scores, queries[head], NN)
+        d_values = d_values + dot(probs.astype(BF), d_outs[head], NN)
+        d_query = d_query + dot(keys_t[head], d_scores, NN)
+    return d_query.astype(BF), d_keys.astype(BF), d_values.astype(BF)
+
+
+def attend_back_kernel(q_ref, kv_ref, do_ref, o_ref, log_ref, d_ref):
+    parts = attend_back_pair(q_ref, kv_ref, do_ref, o_ref, log_ref)
+    rows = parts[0].shape[1]
+    d_ref[:rows, :128] = parts[0].T
+    d_ref[rows:, :128] = jnp.zeros((d_ref.shape[0] - rows, 128), BF)
+    for index, part in enumerate(parts[1:], 1):
+        d_ref[:, 128 * index : 128 * (index + 1)] = part
+
+
+def attend_back_apart(query, keys, d_out, out, log, pairs, n_query, n_key):
+    over_q = lambda cols: pl.BlockSpec((n_query, cols), lambda h: (0, h))
+    over_k = lambda cols: pl.BlockSpec((n_key, cols), lambda h: (0, h))
+    return pl.pallas_call(
+        attend_back_kernel,
+        out_shape=jax.ShapeDtypeStruct((n_key, pairs * 384), BF),
+        grid=(pairs,),
+        in_specs=[
+            over_q(384),
+            over_k(384),
+            over_q(128),
+            over_q(128),
+            pl.BlockSpec((1, 1, 2, n_query), lambda h: (0, h, 0, 0)),
+        ],
+        out_specs=over_k(384),
+        compiler_params=pltpu.CompilerParams(vmem_limit_bytes=VMEM_BYTES),
+        cost_estimate=estimate(2 * pairs * n_query * n_key * 2400, (n_query + n_key) * pairs * 1024),
+        name="attend_back_apart",
+    )(query, keys, d_out, out, log)
+
+
+def attend_back_grad_kernel(
+    core_ref, qkv_ref, do_ref, o_ref, log_ref, h1_ref, h1_a_ref, d_a_ref,
+    d_ref, away_ref, own_ref, acc, turned, *, images, blocks
+):
+    image = pl.program_id(1)
+
+    @pl.when(image == 0)
+    def _():
+        acc[...] = dot(d_a_ref[...].T, h1_a_ref[...], NN)
+
+    d_query, d_keys, d_values = attend_back_pair(qkv_ref, qkv_ref, do_ref, o_ref, log_ref)
+    d_ref[:, :128] = d_query.T
+    d_ref[:, 128:256] = d_keys
+    d_ref[:, 256:] = d_values
+    d_turned = jnp.concatenate([d_query, d_keys.T, d_values.T], 0)
+    acc[...] += dot(d_turned, h1_ref[...], NN)
+
+    @pl.when(image == images - 1)
+    def _():
+        turned[...] = acc[...].T
+        store_by_core(core_ref[0], turned, away_ref, own_ref, blocks)
+
+
+def attend_back_grad(qkv, d_out, out, log, h1, h1_a, d_a, core, pairs, images, count, blocks):
+    width = h1.shape[1]
+    rows_a = h1_a.shape[0]
+    over = lambda cols: pl.BlockSpec((count, cols), lambda h, i: (i, h))
+    grad = pl.BlockSpec((width // 2, 384), lambda h, i: (0, h))
+    return pl.pallas_call(
+        partial(attend_back_grad_kernel, images=images, blocks=blocks),
+        out_shape=(
+            jax.ShapeDtypeStruct((images * count, pairs * 384), BF),
+            jax.ShapeDtypeStruct((width // 2, pairs * 384), BF),
+            jax.ShapeDtypeStruct((width // 2, pairs * 384), BF),
+        ),
+        grid=(pairs, images),
+        in_specs=[
+            pl.BlockSpec(memory_space=pltpu.SMEM),
+            over(384),
+            over(128),
+            over(128),
+            pl.BlockSpec((1, 1, 2, count), lambda h, i: (i, h, 0, 0)),
+            pl.BlockSpec((count, width), lambda h, i: (i, 0)),
+            pl.BlockSpec((rows_a, width), lambda h, i: (0, 0)),
+            pl.BlockSpec((rows_a, 384), lambda h, i: (0, h)),
+        ],
+        out_specs=[over(384), grad, grad],
+        scratch_shapes=[
+            pltpu.VMEM((384, width), F32),
+            pltpu.VMEM((width, 384), F32),
+        ],
+        compiler_params=pltpu.CompilerParams(vmem_limit_bytes=VMEM_BYTES),
+        cost_estimate=estimate(
+            images * 2 * pairs * count * count * 2800, images * count * pairs * 2048
+        ),
+        name="attend_back",
+    )(core, qkv, d_out, out, log, h1, h1_a, d_a)
+
+
+def gelu_parts(inner):
+    scaled = inner * (0.5**0.5)
+    upper = 0.5 * lax.erf(scaled) + 0.5
+    bell = jnp.exp2(scaled * scaled * -math.log2(math.e) - 0.5 * math.log2(2.0 * math.pi))
+    return upper, inner * bell
+
+
+def mlp_kernel(
+    x0_ref, mixed0_ref, mixed1_ref, wout_ref, gain_ref, wup_ref,
+    x1_ref, slope_ref, xsum_ref, asum_ref, *, per
+):
+    mixed = jnp.concatenate([mixed0_ref[...], mixed1_ref[...]], 1)
+    x1 = x0_ref[...] + dot(mixed, wout_ref[...], NN)
+    x1_ref[...] = x1
+    h2 = (normed(x1)[0] * gain_ref[...]).astype(BF)
+
+    @pl.when(pl.program_id(0) % per == 0)
+    def _():
+        xsum_ref[...] = jnp.zeros_like(xsum_ref)
+        asum_ref[...] = jnp.zeros_like(asum_ref)
+
+    xsum_ref[0] += jnp.sum(x1, 0, keepdims=True)
+    width = 512
+    for first in range(0, wup_ref.shape[1], width):
+        cols = slice(first, first + width)
+        inner = dot(h2, wup_ref[:, cols], NN)
+        upper, slope = gelu_parts(inner)
+        slope_ref[:, cols] = (upper + slope).astype(BF)
+        asum_ref[0, :, cols] += jnp.sum(inner * upper, 0, keepdims=True)
+
+
+def mlp(x0, mixed, w_up_out, gain, images, block):
+    rows, width = x0.shape
+    hidden = w_up_out.shape[1] - width
+    per = rows // images // block
+    return pl.pallas_call(
+        partial(mlp_kernel, per=per),
+        out_shape=(
+            jax.ShapeDtypeStruct((rows, width), F32),
+            jax.ShapeDtypeStruct((rows, hidden), BF),
+            jax.ShapeDtypeStruct((images, 1, width), F32),
+            jax.ShapeDtypeStruct((images, 1, hidden), F32),
+        ),
+        grid=(rows // block,),
+        in_specs=[
+            pl.BlockSpec((block, width), lambda i: (i, 0)),
+            pl.BlockSpec((block, width // 2), lambda i: (i, 0)),
+            pl.BlockSpec((block, width // 2), lambda i: (i, 0)),
+            pl.BlockSpec((width, width), lambda i: (0, hidden // width)),
+            pl.BlockSpec((1, width), lambda i: (0, 0)),
+            pl.BlockSpec((width, hidden), lambda i: (0, 0)),
+        ],
+        out_specs=[
+            pl.BlockSpec((block, width), lambda i: (i, 0)),
+            pl.BlockSpec((block, hidden), lambda i: (i, 0)),
+            pl.BlockSpec((1, 1, width), lambda i: (i // per, 0, 0)),
+            pl.BlockSpec((1, 1, hidden), lambda i: (i // per, 0, 0)),
+        ],
+        compiler_params=pltpu.CompilerParams(vmem_limit_bytes=VMEM_BYTES),
+        cost_estimate=estimate(4 * rows * width * (hidden + width), rows * hidden * 4),
+        name="mlp",
+    )(x0, *mixed, w_up_out, gain, w_up_out)
+
+
+def head_kernel(
+    xsum_ref, asum_ref, sums_a_ref, down_ref, head_ref, label_ref, alive_ref, once_ref, whole_ref,
+    total_ref, loss_ref, rows_ref, dx2_ref, dact_ref, *, classes, own
+):
+    width, hidden = down_ref.shape
+    fill = loss_ref.shape[0] - own - 1
+
+    def stacked(ref, cols):
+        rows = [ref[image] for image in range(own)] + [sums_a_ref[:, cols]]
+        return jnp.concatenate(rows + [jnp.zeros((fill, rows[0].shape[1]), F32)], 0)
+
+    xsum = stacked(xsum_ref, slice(0, width))
+    asum = stacked(asum_ref, slice(width, width + hidden))
+    high = asum.astype(BF)
+    low = (asum - high.astype(F32)).astype(BF)
+    whole = whole_ref[...]
+    down = down_ref[...]
+    pooled = (xsum + (dot(high, down, NT) + dot(low, down, NT))) / whole
+    pooled_low = pooled.astype(BF)
+    head = head_ref[...]
+    place = lax.broadcasted_iota(jnp.int32, (1, head.shape[1]), 1)
+    logits = jnp.where(place < classes, dot(pooled_low, head, NN), -1e30)
+    top = jnp.max(logits, -1, keepdims=True)
+    norm_log = top + jnp.log(jnp.sum(jnp.exp(logits - top), -1, keepdims=True))
+    hot = place == label_ref[...]
+    true_logit = jnp.sum(jnp.where(hot, logits, 0.0), -1, keepdims=True)
+    loss_ref[...] = jnp.broadcast_to(norm_log - true_logit, loss_ref.shape)
+    soft = jnp.exp(logits - norm_log) - hot.astype(F32)
+    d_logits = (soft * alive_ref[...] / total_ref[...]).astype(BF)
+    d_x2 = dot(d_logits, head, NT) / whole
+    d_mix = d_x2.astype(BF)
+    d_act = dot(d_mix, down, NN)
+    for image in range(own + 1):
+        dx2_ref[image] = d_x2[image : image + 1]
+        dact_ref[image] = d_act[image : image + 1]
+    once = once_ref[...]
+    rows_ref[:, :hidden] = high
+    rows_ref[:, hidden : hidden + width] = pooled_low
+    rows_ref[:, hidden + width : hidden + 2 * width] = (d_mix * once).astype(BF)
+    rows_ref[:, hidden + 2 * width :] = (d_logits * once).astype(BF)
+
+
+def head_step(xsum, asum, sums_a, w_down_head, labels, alive, once, whole, total, classes):
+    own, _, width = xsum.shape
+    hidden = asum.shape[2]
+    rows = labels.shape[0]
+    padded = w_down_head.shape[1] - hidden
+    spec = lambda shape, *place: pl.BlockSpec(shape, lambda i: place or (0,) * len(shape))
+    shapes = (
+        ((rows, 128), F32),
+        ((rows, hidden + 2 * width + padded), BF),
+        ((own + 1, 1, width), F32),
+        ((own + 1, 1, hidden), F32),
+    )
+    return pl.pallas_call(
+        partial(head_kernel, classes=classes, own=own),
+        out_shape=tuple(jax.ShapeDtypeStruct(*shape) for shape in shapes),
+        grid=(1,),
+        in_specs=[
+            spec(xsum.shape),
+            spec(asum.shape),
+            spec(sums_a.shape),
+            spec((width, hidden), 0, 0),
+            spec((width, padded), 0, hidden // padded),
+            spec((rows, 1)),
+            spec((rows, 1)),
+            spec((rows, 1)),
+            spec((rows, 1)),
+            spec((1, 1)),
+        ],
+        out_specs=[spec(shape[0]) for shape in shapes],
+        compiler_params=pltpu.CompilerParams(vmem_limit_bytes=VMEM_BYTES),
+        cost_estimate=estimate(1 << 32, 8 << 20),
+        name="head",
+    )(xsum, asum, sums_a, w_down_head, w_down_head, labels, alive, once, whole, total)
+
+
+def mlp_back_kernel(*refs, steps):
+    parts = (refs[0:6], refs[6:12])
+    wout_ref, gain_ref, wup_ref = refs[12:15]
+    outs = (refs[15:18], refs[18:21])
+    grad_ref, ggain_ref = refs[21:23]
+    up_acc, out_acc = refs[23:25]
+    step = pl.program_id(0)
+
+    def body(inputs, outputs, begin):
+        slope_ref, dact_ref, x1_ref, dx2_ref, *mixed_refs = inputs
+        dx1_ref, *dmixed_refs = outputs
+        gain = gain_ref[...]
+        hat, scale = normed(x1_ref[...])
+        h2_t = (hat * gain).astype(BF).T
+        d_h2 = 0.0
+        width = 768
+        for first in range(0, slope_ref.shape[1], width):
+            cols = slice(first, first + width)
+            d_inner = (slope_ref[:, cols].astype(F32) * dact_ref[0, :, cols]).astype(BF)
+            d_h2 = d_h2 + dot(d_inner, wup_ref[:, cols], NT)
+            grad = dot(h2_t, d_inner, NN)
+            up_acc[:, cols] = grad if begin else up_acc[:, cols] + grad
+        gain_grad = jnp.sum(d_h2 * hat, 0, keepdims=True)
+        ggain_ref[...] = gain_grad if begin else ggain_ref[...] + gain_grad
+        d_x1 = dx2_ref[0] + norm_back(d_h2, gain, hat, scale)
+        dx1_ref[...] = d_x1
+        d_attn = d_x1.astype(BF)
+        mixed = jnp.concatenate([mixed_ref[...] for mixed_ref in mixed_refs], 1)
+        grad = dot(mixed.T, d_attn, NN)
+        out_acc[...] = grad if begin else out_acc[...] + grad
+        d_mixed = dot(d_attn, wout_ref[...], NT).astype(BF)
+        half = mixed_refs[0].shape[1]
+        for index, dmixed_ref in enumerate(dmixed_refs):
+            dmixed_ref[...] = d_mixed[:, index * half : (index + 1) * half]
+
+    @pl.when(step == 0)
+    def _():
+        body(parts[1], outs[1], True)
+
+    @pl.when(step > 0)
+    def _():
+        body(parts[0], outs[0], False)
+
+    @pl.when(step == steps)
+    def _():
+        hidden = up_acc.shape[1]
+        grad_ref[:, :hidden] = up_acc[...].astype(BF)
+        grad_ref[:, hidden:] = out_acc[...].astype(BF)
+
+
+def mlp_back(part_b, part_a, w_up_out, gain, images, block):
+    rows, width = part_b[2].shape
+    rows_a = part_a[2].shape[0]
+    hidden = part_b[0].shape[1]
+    steps = rows // block
+    per = steps // images
+    at = lambda i: jnp.maximum(i - 1, 0)
+    moving = lambda cols: pl.BlockSpec((block, cols), lambda i: (at(i), 0))
+    still = lambda shape: pl.BlockSpec(shape, lambda i: (0,) * len(shape))
+    image = lambda cols: pl.BlockSpec((1, 1, cols), lambda i: (at(i) // per, 0, 0))
+    last = lambda cols: pl.BlockSpec((1, 1, cols), lambda i: (images, 0, 0))
+    half = width // 2
+    outs = []
+    for count in (rows, rows_a):
+        outs += [
+            jax.ShapeDtypeStruct((count, width), F32),
+            jax.ShapeDtypeStruct((count, half), BF),
+            jax.ShapeDtypeStruct((count, half), BF),
+        ]
+    return pl.pallas_call(
+        partial(mlp_back_kernel, steps=steps),
+        out_shape=(
+            *outs,
+            jax.ShapeDtypeStruct((width, hidden + width), BF),
+            jax.ShapeDtypeStruct((1, width), F32),
+        ),
+        grid=(steps + 1,),
+        in_specs=[
+            moving(hidden), image(hidden), moving(width), image(width), moving(half), moving(half),
+            still((rows_a, hidden)), last(hidden), still((rows_a, width)),
+            last(width), still((rows_a, half)), still((rows_a, half)),
+            pl.BlockSpec((width, width), lambda i: (0, hidden // width)),
+            still((1, width)),
+            still((width, hidden)),
+        ],
+        out_specs=[
+            moving(width), moving(half), moving(half),
+            still((rows_a, width)), still((rows_a, half)), still((rows_a, half)),
+            still((width, hidden + width)), still((1, width)),
+        ],
+        scratch_shapes=[pltpu.VMEM((width, hidden), F32), pltpu.VMEM((width, width), F32)],
+        compiler_params=pltpu.CompilerParams(vmem_limit_bytes=VMEM_BYTES),
+        cost_estimate=estimate(
+            4 * (rows + rows_a) * width * (hidden + width), (rows + rows_a) * hidden * 4
+        ),
+        name="mlp_back",
+    )(*part_b, *part_a, w_up_out, gain, w_up_out)
+
+
+def embed_back_kernel(core_ref, *refs, steps, groups, pieces, blocks, parts_b):
+    n_b, n_a = 3 + pieces + groups, 4 + groups
+    inputs_b, inputs_a = refs[:n_b], refs[n_b : n_b + n_a]
+    gain_ref, gain_grad_ref, *rest = refs[n_b + n_a :]
+    weight_refs = rest[:groups]
+    away_ref, own_ref, acc_b, acc_a, acc_tab, gain_acc = rest[groups:]
+    step = pl.program_id(0)
+
+    def body(inputs, acc, parts, pixel_ref):
+        x0_ref, dx1_ref, tab_ref = inputs[:3]
+        gain = gain_ref[...]
+        count = x0_ref.shape[0] // parts
+        turned = []
+        for part in range(parts):
+            rows = slice(part * count, (part + 1) * count)
+            hat, scale = normed(x0_ref[rows])
+            d_h1 = 0.0
+            for ref, weight_ref in zip(inputs[-groups:], weight_refs):
+                d_h1 = d_h1 + dot(ref[rows], weight_ref[...], NT)
+            gain_acc[0:1] += jnp.sum(d_h1 * hat, 0, keepdims=True)
+            d_x0 = dx1_ref[rows] + norm_back(d_h1, gain, hat, scale)
+            turned.append(d_x0.astype(BF).T)
+        turned = jnp.concatenate(turned, 1)
+        acc_tab[...] += dot(turned, tab_ref[...], NN)
+        acc[:, : pixel_ref.shape[1]] += dot(turned, pixel_ref[...], NN)
+
+    @pl.when(step == 0)
+    def _():
+        for acc in (acc_b, acc_a, acc_tab, gain_acc):
+            acc[...] = jnp.zeros_like(acc)
+        gain_acc[1:2] = gain_grad_ref[...]
+        body(inputs_a, acc_a, 1, inputs_a[3])
+
+    for piece in range(pieces):
+
+        @pl.when((step > 0) & ((step - 1) % pieces == piece))
+        def _(piece=piece):
+            body(inputs_b, acc_b, parts_b, inputs_b[3 + piece])
+
+    @pl.when(step == steps)
+    def _():
+        place = lax.broadcasted_iota(jnp.int32, (8, 128), 1)
+        row = lax.broadcasted_iota(jnp.int32, (8, 128), 0)
+        spots = jnp.where((place == 126 + row) & (row < 2), 1.0, 0.0).astype(BF)
+        acc_tab[...] += lax.dot_general(
+            gain_acc[...].astype(BF), spots, ROWS_DIM, preferred_element_type=F32
+        )
+        at = 0
+        for acc in (acc_b, acc_a, acc_tab):
+            cols = slice(at, at + acc.shape[1])
+            at += acc.shape[1]
+            store_by_core(core_ref[0], acc, away_ref.at[:, cols], own_ref.at[:, cols], blocks)
+
+
+def embed_back(
+    x0_b, dx1_b, tab_b, pixels_b, d_b, x0_a, dx1_a, tab_a, pixels_a, d_a, gain, gain_grad, w_qkv,
+    core, blocks, images, depths
+):
+    rows, width = x0_b.shape
+    pieces = len(pixels_b)
+    steps = images * pieces
+    block = rows // steps
+    at = lambda i: jnp.maximum(i - 1, 0)
+    moving = lambda array: pl.BlockSpec((block, array.shape[1]), lambda i: (at(i), 0))
+    still = lambda shape: pl.BlockSpec(shape, lambda i: (0,) * len(shape))
+    inputs_a = (x0_a, dx1_a, tab_a, pixels_a, *d_a)
+    grad = (width // 2, sum(depths) + 128)
+    return pl.pallas_call(
+        partial(
+            embed_back_kernel, steps=steps, groups=len(d_b), pieces=pieces, blocks=blocks,
+            parts_b=max(1, block // 256),
+        ),
+        out_shape=(jax.ShapeDtypeStruct(grad, BF), jax.ShapeDtypeStruct(grad, BF)),
+        grid=(steps + 1,),
+        in_specs=[pl.BlockSpec(memory_space=pltpu.SMEM)]
+        + [moving(x0_b), moving(dx1_b)]
+        + [pl.BlockSpec((block, 128), lambda i: (at(i) % pieces, 0))]
+        + [
+            pl.BlockSpec((block, array.shape[1]), lambda i: (at(i) // pieces, 0))
+            for array in pixels_b
+        ]
+        + [moving(array) for array in d_b]
+        + [still(array.shape) for array in inputs_a]
+        + [still((1, width)), still((1, width))]
+        + [still(weight.shape) for weight in w_qkv],
+        out_specs=[still(grad), still(grad)],
+        scratch_shapes=[pltpu.VMEM((width, depth), F32) for depth in (*depths, 128)]
+        + [pltpu.VMEM((8, width), F32)],
+        compiler_params=pltpu.CompilerParams(vmem_limit_bytes=VMEM_BYTES),
+        cost_estimate=estimate(2 * rows * width * (3 * width + 640), rows * 10000),
+        name="embed_back",
+    )(core, x0_b, dx1_b, tab_b, *pixels_b, *d_b, *inputs_a, gain, gain_grad, *w_qkv)
+
+
+def after(value, *others):
+    return lax.optimization_barrier((value, *others))[0]
+
+
+def padded_cols(array, width):
+    return jnp.pad(array, ((0, 0), (0, width - array.shape[1])))
+
+
+def round_up(count, unit):
+    return -(-count // unit) * unit
+
+
+def fast_step(
+    pixels_a, pixels_b, labels_a, labels_b, live_a, live_b, masters, firsts, seconds
+):
+    qkv_w, out_w, mlp_w, kern_w, pos_w, head_w, gains = masters
+    seq = lax.axis_size("y")
+    row = lax.axis_index("y")
+    count_all = seq * lax.axis_size("z") * lax.axis_size("x") * 2
+    flat_index = lax.axis_index(AXES)
+    lead = (row == 0).astype(F32)
+    width = HEADS * HEAD_DIM
+    hidden = mlp_w.shape[2]
+    classes = head_w.shape[1]
+    classes_up = round_up(classes, 1024)
+    rows_own = qkv_w.shape[0]
+    rows_kern = kern_w.shape[0]
+    groups = 2
+    span = width // groups
+    pairs = span // 128
+
+    images_a, rows_a, grid_a, depth_a = pixels_a.shape
+    images_b, rows_b, grid_b, depth_b = pixels_b.shape
+    own_b = images_b // seq
+    parts_b, tabs_b, slices = [], [], []
+    table_b = jnp.asarray(place_table(grid_b))
+    table_a = jnp.asarray(place_table(grid_a))
+    span_b, span_a = rows_b * grid_b, rows_a * grid_a
+    for step in range(seq):
+        part = lax.dynamic_slice_in_dim(
+            pixels_b, ((row + step) % seq) * own_b, own_b, 0
+        )
+        part = part.reshape(own_b * rows_b * grid_b, depth_b)
+        slices.append(part)
+        parts_b.append(shift(part, "y", step) if step else part)
+        tabs_b.append(lax.dynamic_slice_in_dim(table_b, ((row - step) % seq) * span_b, span_b, 0))
+    tab_a = lax.dynamic_slice_in_dim(table_a, row * span_a, span_a, 0)
+    whole_a, whole_b = grid_a * grid_a, grid_b * grid_b
+
+    alive_a = live_a.astype(F32)[:, None]
+    counts = jnp.stack([lead * jnp.sum(alive_a), lead * jnp.sum(live_b.astype(F32))]).astype(BF)
+    lanes = round_up(rows_kern + 2, 128)
+    sent = jnp.concatenate(
+        [
+            kern_w.astype(BF).T,
+            jnp.broadcast_to(counts[None], (width, 2)),
+            jnp.zeros((width, lanes - rows_kern - 2), BF),
+        ],
+        1,
+    )
+    sent = after(sent, *slices)
+    got = lax.all_to_all(sent, AXES, split_axis=0, concat_axis=0, tiled=True)
+    got, tab_a, tab_b, *parts_b = lax.optimization_barrier(
+        (got, tab_a, jnp.concatenate(tabs_b, 0), *parts_b)
+    )
+    got = got.reshape(count_all, rows_own, lanes)
+    counts = got[:, 0, rows_kern : rows_kern + 2]
+    got = got.astype(F32)
+    kern_cols = got[:, :, :rows_kern].transpose(1, 0, 2).reshape(rows_own, 3, BASE * BASE)
+
+    def group_cols(array, group):
+        shaped = array.reshape(rows_own, 3, groups, pairs, 128)[:, :, group]
+        return shaped.transpose(0, 2, 1, 3).reshape(rows_own, 3 * span)
+
+    qkv_low = qkv_w.astype(BF)
+    w_groups = [lax.all_gather(group_cols(qkv_low, 0), AXES, axis=0, tiled=True)]
+
+    tables = [resize_table(PATCH_B), resize_table(PATCH_A)]
+    sizes = [3 * table.shape[0] for table in tables]
+    resized = [
+        jnp.einsum("dck,pk->dcp", kern_cols, jnp.asarray(table), precision=HIGH).reshape(
+            rows_own, -1
+        )
+        for table in tables
+    ]
+    depths = [round_up(size, 128) for size in sizes]
+    spot = sum(depths)
+    pos_t = pos_w.astype(BF).T
+    edge = jnp.zeros((rows_own, 28), BF)
+    small = jnp.concatenate(
+        [padded_cols(piece.astype(BF), depth) for piece, depth in zip(resized, depths)]
+        + [pos_t, pos_t, edge, gains.astype(BF).T],
+        1,
+    )
+    w_small = gather_rows(small)
+    second = group_cols(qkv_low, 1)
+    w_up_out = lax.all_gather(
+        after(jnp.concatenate([mlp_w[0].astype(BF), out_w.astype(BF)], 1), got),
+        AXES, axis=0, tiled=True,
+    )
+    w_down_head = lax.all_gather(
+        after(
+            jnp.concatenate([mlp_w[1].astype(BF), padded_cols(head_w.astype(BF), classes_up)], 1),
+            w_small,
+        ),
+        AXES, axis=0, tiled=True,
+    )
+
+    gain_rows = w_small[:, spot + 126 :].T.astype(F32)
+    gain1, gain2 = gain_rows[0:1], gain_rows[1:2]
+    flat_a = pixels_a.reshape(span_a, depth_a)
+    block = min(512, whole_b)
+    x0_a, h1_a = embed([flat_a], tab_a, w_small, depths[0], spot, gain1, 1)
+    h1_all = jnp.concatenate([h1_a] + [shift(h1_a, "y", step) for step in range(1, seq)], 0)
+    x0_b, h1_b = embed(
+        [after(parts_b[0], h1_a), *parts_b[1:]], tab_b, w_small, 0, spot, gain1, own_b
+    )
+    h1_b, h1_all = lax.optimization_barrier((h1_b, h1_all))
+    outs_a, outs_b = [], []
+    ready = h1_b
+    for group in range(groups):
+        if group:
+            w_groups.append(gather_rows(after(second, h1_a), ready))
+        outs_b.append(attend_pairs(after(h1_b, ready), w_groups[group], own_b, whole_b))
+        ready = outs_b[-1][0]
+    for group in range(groups):
+        outs_a.append(attend_pairs(after(h1_all, ready), w_groups[group], 1, span_a))
+    qkvs_a, qkvs_b = [out[0] for out in outs_a], [out[0] for out in outs_b]
+    mixed_a, mixed_b = [out[1] for out in outs_a], [out[1] for out in outs_b]
+
+    x1_a, slope_a, xsum_a, asum_a = mlp(x0_a, mixed_a, w_up_out, gain2, 1, span_a)
+    sums_a = jnp.concatenate([xsum_a[0], asum_a[0]], 1)
+    sums_a = sum([shift(sums_a, "y", step) for step in range(1, seq)], sums_a)
+    x1_b, slope_b, xsum_b, asum_b = mlp(after(x0_b, x1_a), mixed_b, w_up_out, gain2, own_b, block)
+
+    counts, labels_a, labels_b, live_b, alive_a = lax.optimization_barrier(
+        (counts, labels_a, labels_b, live_b, alive_a, h1_b)
+    )[:5]
+    count = jnp.sum(counts.astype(F32), 0, keepdims=True)
+    total = jnp.maximum(jnp.sum(count), 1.0)
+    rows_up = round_up(own_b + 1, 8)
+    fill = rows_up - own_b - 1
+    stack = lambda first, last: jnp.pad(
+        jnp.concatenate([first, last], 0), ((0, fill), (0, 0))
+    )
+    mine = lambda array: lax.dynamic_slice_in_dim(array, row * own_b, own_b, 0)[:, None]
+    labels = stack(mine(labels_b), labels_a[:, None])
+    alive_b = mine(live_b).astype(F32)
+    alive = stack(alive_b, alive_a)
+    once = stack(jnp.ones((own_b, 1), F32), lead.reshape(1, 1))
+    whole = np.ones((rows_up, 1), np.float32)
+    whole[:own_b], whole[own_b] = whole_b, whole_a
+    losses, rows_out, d_x2, d_act = head_step(
+        xsum_b, asum_b, sums_a, w_down_head, labels, alive, once, jnp.asarray(whole),
+        total.reshape(1, 1), classes,
+    )
+    loss_sums = jnp.stack(
+        [lead * jnp.sum(alive_a * losses[own_b : own_b + 1, :1]),
+         jnp.sum(alive_b * losses[:own_b, :1])]
+    )
+
+    image_rows = lax.all_gather(rows_out[: round_up(own_b + 1, 4)], AXES, axis=0, tiled=True)
+
+    d_x1_b, d0_b, d1_b, d_x1_a, d0_a, d1_a, grad_up_out, grad_gain2 = mlp_back(
+        (slope_b, d_act, x1_b, d_x2, *mixed_b),
+        (slope_a, d_act, x1_a, d_x2, *mixed_a),
+        w_up_out, gain2, own_b, block,
+    )
+    d_mixed_a, d_mixed_b = (d0_a, d1_a), (d0_b, d1_b)
+
+    d_alls, d_groups_a = [], []
+    for group in range(groups):
+        d_all = attend_back_apart(
+            qkvs_a[group], qkvs_a[group], d_mixed_a[group], mixed_a[group],
+            outs_a[group][2], pairs, span_a, seq * span_a,
+        )
+        own = d_all[:span_a].astype(F32)
+        for step in range(1, seq):
+            own = own + shift(
+                d_all[step * span_a : (step + 1) * span_a], "y", seq - step
+            ).astype(F32)
+        d_alls.append(d_all)
+        d_groups_a.append(own.astype(BF))
+    own_up_out = lax.psum_scatter(
+        after(grad_up_out, image_rows, *d_alls), AXES, scatter_dimension=0, tiled=True
+    ).astype(F32)
+    core = lax.axis_index("core").reshape(1).astype(jnp.int32)
+    blocks = lax.axis_size("z") * lax.axis_size("x")
+    d_groups_b, own_groups = [], []
+    ready = d_alls[-1]
+    for group in range(groups):
+        got, away, own = attend_back_grad(
+            qkvs_b[group],
+            after(d_mixed_b[group], ready),
+            mixed_b[group], outs_b[group][2],
+            h1_b, h1_all, d_alls[group], core, pairs, own_b, whole_b, blocks,
+        )
+        if group:
+            away, own, own_groups[-1] = lax.optimization_barrier((away, own, own_groups[-1]))
+        else:
+            away, own, *d_groups_a = lax.optimization_barrier((away, own, *d_groups_a))
+        d_groups_b.append(got)
+        own_groups.append(scatter_rows(away, own))
+        ready = got
+    away, own = embed_back(
+        x0_b, after(d_x1_b, ready), tab_b, parts_b, d_groups_b,
+        x0_a, d_x1_a, tab_a, flat_a, d_groups_a,
+        gain1, grad_gain2, w_groups, core, blocks, own_b, depths,
+    )
+    away, own, own_up_out, *own_groups = lax.optimization_barrier(
+        (away, own, own_up_out, *own_groups)
+    )
+    own_qkv = jnp.stack(own_groups, 1).reshape(rows_own, groups * pairs, 3, 128)
+    own_qkv = own_qkv.transpose(0, 2, 1, 3).reshape(rows_own, 3 * width)
+    own_small = scatter_rows(away, own)
+    kern_t = jnp.zeros((rows_own, 3, BASE * BASE), F32)
+    for table, size, at in zip(tables, sizes, (0, depths[0])):
+        piece = own_small[:, at : at + size].reshape(rows_own, 3, -1)
+        kern_t = kern_t + jnp.einsum("dcp,pk->dck", piece, jnp.asarray(table), precision=HIGH)
+    own_pos = own_small[:, spot : spot + 49] + own_small[:, spot + 49 : spot + 98]
+    kern_t = kern_t.reshape(rows_own, count_all, rows_kern)
+    own_pos = own_pos.T
+    own_gain = own_small[:, -2:].T
+
+    columns = lambda lo: lax.dynamic_slice_in_dim(
+        image_rows[:, lo : lo + width], flat_index * rows_own, rows_own, 1
+    )
+    own_down = lax.dot_general(
+        columns(hidden + width), image_rows[:, :hidden], ROWS_DIM, preferred_element_type=F32
+    )
+    own_head = lax.dot_general(
+        columns(hidden),
+        image_rows[:, hidden + 2 * width : hidden + 2 * width + classes],
+        ROWS_DIM,
+        preferred_element_type=F32,
+    )
+    own_up, own_out = own_up_out[:, :hidden], own_up_out[:, hidden:]
+    square_sum = sum(
+        jnp.sum(piece * piece)
+        for piece in (own_up_out, own_down, own_head, own_qkv, kern_t, own_pos, own_gain)
+    )
+
+    sums = jnp.concatenate([square_sum.reshape(1), loss_sums])
+    sent = jnp.concatenate(
+        [
+            kern_t.transpose(1, 0, 2),
+            jnp.broadcast_to(sums[None, None], (count_all, rows_own, 3)),
+            jnp.zeros((count_all, rows_own, lanes - rows_kern - 3), F32),
+        ],
+        2,
+    )
+    got = lax.all_to_all(sent, AXES, split_axis=0, concat_axis=0, tiled=True)
+    own_kern = got[:, :, :rows_kern].reshape(count_all * rows_own, rows_kern).T
+    sums = jnp.sum(got[:, 0, rows_kern : rows_kern + 3], 0)
+    grad_norm = jnp.sqrt(sums[0])
+    factor = jnp.minimum(1.0, CLIP / (grad_norm + 1e-06))
+    own_mlp = jnp.stack([own_up, own_down], 0)
+    owned = (own_qkv, own_out, own_mlp, own_kern, own_pos, own_head, own_gain)
+    done = [adamw(masters[i], firsts[i], seconds[i], owned[i] * factor, RATES[i]) for i in range(7)]
+    size_stats = sums[1:] / jnp.maximum(count[0], 1.0)
+    return (
+        *(item[0] for item in done),
+        *(item[1] for item in done),
+        *(item[2] for item in done),
+        size_stats,
+        grad_norm,
+    )
+
+
+def fits_fast(mesh, pixels_a, pixels_b):
+    dp, seq = mesh.shape["dp"], mesh.shape["seq"]
+    images_b, rows_b, grid_b, _ = pixels_b.shape
+    rows_a, grid_a = pixels_a.shape[1:3]
+    return (
+        dp % 8 == 0
+        and rows_b % seq == 0
+        and rows_a % seq == 0
+        and images_b % (dp * seq) == 0
+        and images_b // dp <= 256
+        and pixels_a.shape[0] == dp
+        and grid_b * grid_b % 256 == 0
+        and rows_a // seq * grid_a % 32 == 0
+    )
+
+
+def fast_on_device(*args):
+    return fast_step(*args[:6], args[6:13], args[13:20], args[20:27])
 
 
 def on_device(
@@ -327,64 +1291,31 @@
     )
 
 
+def specs(row, col):
+    both = (*row, *col)
+    owned = (
+        P(both, None), P(both, None), P(None, both, None), P(both, None), P(None, both),
+        P(both, None), P(None, both),
+    )
+    images = P(row, col, None, None)
+    return (images, images, P(row), P(row), P(row), P(row), *owned * 3), (*owned * 3, P(), P())
+
+
 def solution(mesh):
-    placed = (
-        P("dp", "seq", None, None),
-        P("dp", "seq", None, None),
-        P("dp"),
-        P("dp"),
-        P("dp"),
-        P("dp"),
-        P(("dp", "seq"), None),
-        P(("dp", "seq"), None),
-        P(None, ("dp", "seq"), None),
-        P(("dp", "seq"), None),
-        P(None, ("dp", "seq")),
-        P(("dp", "seq"), None),
-        P(None, ("dp", "seq")),
-        P(("dp", "seq"), None),
-        P(("dp", "seq"), None),
-        P(None, ("dp", "seq"), None),
-        P(("dp", "seq"), None),
-        P(None, ("dp", "seq")),
-        P(("dp", "seq"), None),
-        P(None, ("dp", "seq")),
-        P(("dp", "seq"), None),
-        P(("dp", "seq"), None),
-        P(None, ("dp", "seq"), None),
-        P(("dp", "seq"), None),
-        P(None, ("dp", "seq")),
-        P(("dp", "seq"), None),
-        P(None, ("dp", "seq")),
-    )
-    return jax.shard_map(
-        on_device,
-        mesh=mesh,
-        in_specs=placed,
-        out_specs=(
-            P(("dp", "seq"), None),
-            P(("dp", "seq"), None),
-            P(None, ("dp", "seq"), None),
-            P(("dp", "seq"), None),
-            P(None, ("dp", "seq")),
-            P(("dp", "seq"), None),
-            P(None, ("dp", "seq")),
-            P(("dp", "seq"), None),
-            P(("dp", "seq"), None),
-            P(None, ("dp", "seq"), None),
-            P(("dp", "seq"), None),
-            P(None, ("dp", "seq")),
-            P(("dp", "seq"), None),
-            P(None, ("dp", "seq")),
-            P(("dp", "seq"), None),
-            P(("dp", "seq"), None),
-            P(None, ("dp", "seq"), None),
-            P(("dp", "seq"), None),
-            P(None, ("dp", "seq")),
-            P(("dp", "seq"), None),
-            P(None, ("dp", "seq")),
-            P(),
-            P(),
-        ),
-        check_vma=False,
-    )
+    dp, seq = mesh.shape["dp"], mesh.shape["seq"]
+
+    def run(*args):
+        if fits_fast(mesh, args[0], args[1]):
+            split = Mesh(mesh.devices.reshape(4, dp // 8, 2, seq), AXES)
+            placed, given = specs(AXES[:3], AXES[3:])
+            step = jax.shard_map(
+                fast_on_device, mesh=split, in_specs=placed, out_specs=given, check_vma=False
+            )
+        else:
+            placed, given = specs(("dp",), ("seq",))
+            step = jax.shard_map(
+                on_device, mesh=mesh, in_specs=placed, out_specs=given, check_vma=False
+            )
+        return step(*args)
+
+    return run

time: 2190 us -> 511 us (0.23)
  waiting for transfers between devices: 704 us -> 48.3 us
  matrix products: 600 us -> 5.55 us
  local copies, waits for them, and re-layouts: 329 us -> 27.7 us
  Pallas kernels: 0 us -> 288 us
  other arithmetic: 264 us -> 34.4 us
  blocking collectives: 250 us -> 31.8 us
  starting transfers between devices: 2.41 us -> 45.9 us
    dot_general x51 -> x6, matrix products: 600 us -> 5.55 us  [the longest x1 1.64 us: fast_step(): lax.dot_general(columns(hidden + width), image_rows[:, :hidden], ROWS_DIM...]
    reduce_scatter x5 -> x1, waiting for transfers between devices: 437 us -> 0.02 us  [fast_step(): lax.psum_scatter(after(grad_up_out, image_rows, *d_alls), AXES, scatter_d...]
    pallas_call x0 -> x15, Pallas kernels: none -> 288 us  [the longest x2 86.9 us: attend_back_grad(): pl.pallas_call(partial(attend_back_grad_kernel, images=images, blocks=blo...]
    ppermute x2 -> x10, waiting for transfers between devices: 267 us -> 7.66 us  [shift(): return lax.ppermute(value, axis, pairs)]
    all_gather x2 -> x0, blocking collectives: 131 us -> none  [the longest x1 66.1 us: on_device(): lax.all_gather(gains.astype(bf16), ('dp', 'seq'), axis=1, tiled=True)]
    reshape x13 -> x8, local copies, waits for them, and re-layouts: 106 us -> 2.82 us  [the longest x1 1.31 us: fast_step(): part = part.reshape(own_b * rows_b * grid_b, depth_b)]
    convert_element_type x13 -> x12, other arithmetic: 108 us -> 12.2 us  [the longest x3 4.59 us: scatter_rows(): both = (own.astype(F32) + shift(away, 'core', 1).astype(F32)).astype(BF)]
    psum x3 -> x0, blocking collectives: 81.3 us -> none  [the longest x1 39.6 us: on_device(): grad_norm = jnp.sqrt(lax.psum(square_sum, ('dp', 'seq')))]
  transfers between devices with their start and end apart: 13 -> 21, of which waited for: 5 -> 8; matrix products, arithmetic and copies ran while one was open for 33% -> 9% of each run, Pallas kernels for 0% -> 55%
where the time goes in v2:
time: 511 us; the launch traced here: 505 us
  Pallas kernels  288 us (56%)
  waiting for transfers between devices  48.3 us (9%)
  starting transfers between devices  45.9 us (9%)
  other arithmetic  34.4 us (7%)
  blocking collectives  31.8 us (6%)
  local copies, waits for them, and re-layouts  27.7 us (5%)
  between operations  24 us (5%)
  matrix products  5.55 us (1%)
    pallas_call x2, Pallas kernels, attend_back_grad(): pl.pallas_call(partial(attend_back_grad_kernel, images=images, blocks=blo...  86.9 us
    pallas_call x4, Pallas kernels, attend_pairs(): pl.pallas_call(partial(attend_kernel, items=items, n_query=n_query), out_...  63.9 us
    pallas_call x1, Pallas kernels, mlp_back(): pl.pallas_call(partial(mlp_back_kernel, steps=steps), out_shape=(*outs, j...  43.7 us
    pallas_call x2, Pallas kernels, mlp(): pl.pallas_call(partial(mlp_kernel, per=per), out_shape=(jax.ShapeDtypeStr...  35.6 us
    all_to_all x1, blocking collectives, gather_rows(): lax.all_to_all(copies, CHIPS, split_axis=0, concat_axis=0, tiled=True)  31.8 us
    pallas_call x1, Pallas kernels, embed_back(): pl.pallas_call(partial(embed_back_kernel, steps=steps, groups=len(d_b), p...  24.1 us
    all_to_all x2, waiting for transfers between devices, fast_step(): got = lax.all_to_all(sent, AXES, split_axis=0, concat_axis=0, tiled=True)  23.8 us
    all_to_all x3, starting transfers between devices, scatter_rows(): got = lax.all_to_all(both, CHIPS, split_axis=0, concat_axis=0, tiled=True)  17.9 us
  transfers between devices with their start and end apart: 21, of which 8 were waited for; matrix products, arithmetic and copies ran while one was open for 9% of the time, Pallas kernels for 55%

profile of v2, /device:TPU:1, one launch (start us, length us, event | category | flops | bytes accessed | tf_op | source)
XLA Modules:
  0.0 505.2 jit_solution(6814960813946032350)
XLA Ops:
  10.9 2.7 constant_dynamic-slice_fusion.3
  13.6 1.3 copy.195
  14.9 2.1 collective-permute-start
  20.1 5.6 %all-to-all-start = ((bf16[32,24,128]{2,1,0:T(8,128)(2,1)}), bf16[32,24,128]{2,1,0:T(8,128)(2,1)S(1)}, u32[]{:S(2)}, u32[]{:S(2)}) async-start(bf16[32,24,128]{2,1,0:T(8,128)(2,1)} %bitcast.7), calls=%async_computation | async-start | bytes 393216 | tf_op jit(solution)/shard_map/all_to_all | solution.py:843
  26.8 1.5 constant_dynamic-slice_fusion.2.refs_1_.refs_9_
  29.2 10.6 %all-to-all-done = bf16[32,24,128]{2,1,0:T(8,128)(2,1)S(1)} async-done(((bf16[32,24,128]{2,1,0:T(8,128)(2,1)}), bf16[32,24,128]{2,1,0:T(8,128)(2,1)S(1)}, u32[]{:S(2)}, u32[]{:S(2)}) %all-to-all-start) | async-done | bytes 196640 | tf_op jit(solution)/shard_map/all_to_all | solution.py:843
  41.6 31.8 %all_to_all.62 = bf16[16,24,1024]{2,1,0:T(8,128)(2,1)S(1)} all-to-all(bf16[16,24,1024]{2,1,0:T(8,128)(2,1)S(1)} %broadcast_in_dim.23), channel_id=1, replica_groups=mesh['z'=4,'x'=2,'core'=2,'y'=2] {'z','x','y'}, dimensions={0} | all-to-all | bytes 1572864 | tf_op jit(solution)/shard_map/all_to_all | solution.py:137
  73.4 2.1 collective-permute-start.1
  78.9 3.2 embed.2
  82.5 2.3 copy.204.refs_1_.refs_4_
  85.7 4.0 all-to-all-start.2
  90.0 9.4 %embed.3 = (f32[2048,768]{1,0:T(8,128)}, bf16[2048,768]{1,0:T(8,128)(2,1)}) custom-call(bf16[1024,432]{1,0:T(8,128)(2,1)} %bitcast.101, bf16[1024,432]{1,0:T(8,128)(2,1)} %copy.204.refs_1_.refs_4_, bf16[1024,128]{1,0:T(8,128)(2,1)} %pad_maximum_fusion.3.refs_2_, bf16[768,1024]{1,0:T(8,128)(2,1)} %bitcast.97, f32[1,768]{1,0:T(1,128)} %get-tuple-element.315.refs_3_.refs_4_.refs_13_), custom_call_target="tpu_custom_call" | custom-call | flops 2415919104 | bytes 12582912 | tf_op jit(solution)/shard_map/embed/pallas_call | solution.py:230
  100.5 24.9 %attend.4 = (bf16[2048,1152]{1,0:T(8,128)(2,1)}, bf16[2048,384]{1,0:T(8,128)(2,1)}, f32[2,3,2,1024]{3,2,1,0:T(2,128)}) custom-call(bf16[2048,768]{1,0:T(8,128)(2,1)} %get-tuple-element.119.h1_ref, bf16[768,1152]{1,0:T(8,128)(2,1)} %all-gather.6.cloned.1.call-done.weight_ref.refs_15_), custom_call_target="tpu_custom_call" | custom-call | flops 18723373056 | bytes 12582912 | tf_op jit(solution)/shard_map/attend/pallas_call | solution.py:305
  131.0 1.4 pad_maximum_fusion
  132.4 25.2 %attend.5 = (bf16[2048,1152]{1,0:T(8,128)(2,1)}, bf16[2048,384]{1,0:T(8,128)(2,1)}, f32[2,3,2,1024]{3,2,1,0:T(2,128)}) custom-call(bf16[2048,768]{1,0:T(8,128)(2,1)} %get-tuple-element.119.h1_ref, bf16[768,1152]{1,0:T(8,128)(2,1)} %bitcast.98), custom_call_target="tpu_custom_call" | custom-call | flops 18723373056 | bytes 12582912 | tf_op jit(solution)/shard_map/attend/pallas_call | solution.py:305
  157.6 6.7 %attend.7 = (bf16[576,1152]{1,0:T(8,128)(2,1)}, bf16[288,384]{1,0:T(8,128)(2,1)}, f32[1,3,2,288]{3,2,1,0:T(2,128)}) custom-call(bf16[576,768]{1,0:T(8,128)(2,1)} %pad_maximum_fusion.2.h1_ref.h1_a_ref, bf16[768,1152]{1,0:T(8,128)(2,1)} %bitcast.99), custom_call_target="tpu_custom_call" | custom-call | flops 2213609472 | bytes 3538944 | tf_op jit(solution)/shard_map/attend/pallas_call | solution.py:305
  164.3 7.1 %attend.6 = (bf16[576,1152]{1,0:T(8,128)(2,1)}, bf16[288,384]{1,0:T(8,128)(2,1)}, f32[1,3,2,288]{3,2,1,0:T(2,128)}) custom-call(bf16[576,768]{1,0:T(8,128)(2,1)} %pad_maximum_fusion.2.h1_ref.h1_a_ref, bf16[768,1152]{1,0:T(8,128)(2,1)} %all-gather.6.cloned.1.call-done.weight_ref.refs_15_), custom_call_target="tpu_custom_call" | custom-call | flops 2213609472 | bytes 3538944 | tf_op jit(solution)/shard_map/attend/pallas_call | solution.py:305
  171.4 7.7 %mlp.2 = (f32[288,768]{1,0:T(8,128)}, bf16[288,3072]{1,0:T(8,128)(2,1)}, f32[1,1,768]{2,1,0:T(1,128)}, f32[1,1,3072]{2,1,0:T(1,128)}) custom-call(f32[288,768]{1,0:T(8,128)} %get-tuple-element.113.x0_ref.refs_7_, bf16[288,384]{1,0:T(8,128)(2,1)} %get-tuple-element.124.mixed0_ref.refs_10_.o_ref, ...), custom_call_target="tpu_custom_call" | custom-call | flops 106168320 | bytes 110592 | tf_op jit(solution)/shard_map/mlp/pallas_call | solution.py:483
  179.8 1.8 collective-permute-start.4
  181.6 27.9 %mlp.3 = (f32[2048,768]{1,0:T(8,128)}, bf16[2048,3072]{1,0:T(8,128)(2,1)}, f32[2,1,768]{2,1,0:T(1,128)}, f32[2,1,3072]{2,1,0:T(1,128)}) custom-call(f32[2048,768]{1,0:T(8,128)} %get-tuple-element.127.x0_ref.refs_0_, bf16[2048,384]{1,0:T(8,128)(2,1)} %get-tuple-element.128.mixed0_ref.refs_4_.o_ref, ...), custom_call_target="tpu_custom_call" | custom-call | flops 754974720 | bytes 786432 | tf_op jit(solution)/shard_map/mlp/pallas_call | solution.py:483
  210.1 10.5 %all-gather.10.cloned.1.call-done.down_ref.head_ref = bf16[768,4096]{1,0:T(8,128)(2,1)} async-done(((bf16[24,4096]{1,0:T(8,128)(2,1)}), bf16[768,4096]{1,0:T(8,128)(2,1)}) %all-gather.10.cloned.1.call-update) | async-done | bytes 6291472 | tf_op jit(solution)/shard_map/all_gather | solution.py:882
  220.6 7.9 %head.1 = (f32[8,128]{1,0:T(8,128)}, bf16[8,5632]{1,0:T(8,128)(2,1)}, f32[3,1,768]{2,1,0:T(1,128)}, f32[3,1,3072]{2,1,0:T(1,128)}) custom-call(f32[2,1,768]{2,1,0:T(1,128)} %get-tuple-element.131.xsum_ref, f32[2,1,3072]{2,1,0:T(1,128)} %get-tuple-element.132.asum_ref, f32[1,3840]{1,0:T(1,128)} %fusion.27.sums_a_ref, ...), custom_call_target="tpu_custom_call" | custom-call | flops 134217728 | bytes 262144 | tf_op jit(solution)/shard_map/head/pallas_call | solution.py:566
  228.5 1.5 slice_bitcast_fusion.6
  230.1 43.7 %mlp_back.1 = (f32[2048,768]{1,0:T(8,128)}, bf16[2048,384]{1,0:T(8,128)(2,1)}, bf16[2048,384]{1,0:T(8,128)(2,1)}, f32[288,768]{1,0:T(8,128)}, bf16[288,384]{1,0:...) custom-call(bf16[2048,3072]{1,0:T(8,128)(2,1)} %get-tuple-element.130.refs_0_, ...), custom_call_target="tpu_custom_call" | custom-call | flops 861143040 | bytes 897024 | tf_op jit(solution)/shard_map/mlp_back/pallas_call | solution.py:658
  273.9 6.5 %attend_back_apart.3.d_a_ref = bf16[576,1152]{1,0:T(8,128)(2,1)} custom-call(bf16[576,1152]{1,0:T(8,128)(2,1)} %get-tuple-element.153.q_ref.kv_ref, bf16[576,1152]{1,0:T(8,128)(2,1)} %get-tuple-element.153.q_ref.kv_ref, bf16[288,384]{1,0:T(8,128)(2,1)} %get-tuple-element.154.do_ref, bf16[288,384]{1,0:T(8,128)(2,1)} %get-tuple-element.124.mixed0_ref.refs_10_.o_ref, ...), custom_call_target="tpu_custom_call" | custom-call | flops 74649600 | bytes 82944 | tf_op jit(solution)/shard_map/attend_back_apart/pallas_call | solution.py:371
  280.4 2.0 slice.136
  283.6 6.4 %attend_back_apart.2.d_a_ref = bf16[576,1152]{1,0:T(8,128)(2,1)} custom-call(bf16[576,1152]{1,0:T(8,128)(2,1)} %get-tuple-element.148.q_ref.kv_ref, bf16[576,1152]{1,0:T(8,128)(2,1)} %get-tuple-element.148.q_ref.kv_ref, bf16[288,384]{1,0:T(8,128)(2,1)} %get-tuple-element.149.do_ref, bf16[288,384]{1,0:T(8,128)(2,1)} %get-tuple-element.125.mixed1_ref.refs_11_.o_ref, ...), custom_call_target="tpu_custom_call" | custom-call | flops 74649600 | bytes 82944 | tf_op jit(solution)/shard_map/attend_back_apart/pallas_call | solution.py:371
  289.9 2.6 reshape.279
  295.0 43.5 %attend_back.2 = (bf16[2048,1152]{1,0:T(8,128)(2,1)}, bf16[384,1152]{1,0:T(8,128)(2,1)}, bf16[384,1152]{1,0:T(8,128)(2,1)}) custom-call(s32[1]{0:T(128)} %bitcast.core_ref, bf16[2048,1152]{1,0:T(8,128)(2,1)} %get-tuple-element.118.qkv_ref, bf16[2048,384]{1,0:T(8,128)(2,1)} %get-tuple-element.151.do_ref, ...), custom_call_target="tpu_custom_call" | custom-call | flops 1101004800 | bytes 393216 | tf_op jit(solution)/shard_map/attend_back/pallas_call | solution.py:417
  338.6 2.3 add_convert_fusion.4.refs_11_
  340.9 2.3 add_convert_fusion.3.refs_12_
  343.9 2.1 collective-permute-done.7
  347.0 4.2 all-to-all-start.3
  351.3 43.4 %attend_back.3 = (bf16[2048,1152]{1,0:T(8,128)(2,1)}, bf16[384,1152]{1,0:T(8,128)(2,1)}, bf16[384,1152]{1,0:T(8,128)(2,1)}) custom-call(s32[1]{0:T(128)} %bitcast.core_ref, bf16[2048,1152]{1,0:T(8,128)(2,1)} %get-tuple-element.122.qkv_ref, bf16[2048,384]{1,0:T(8,128)(2,1)} %get-tuple-element.157.do_ref, ...), custom_call_target="tpu_custom_call" | custom-call | flops 1101004800 | bytes 393216 | tf_op jit(solution)/shard_map/attend_back/pallas_call | solution.py:417
  395.5 2.3 collective-permute-done.8
  399.0 6.9 %all-to-all-start.4 = ((bf16[16,24,1152]{2,1,0:T(8,128)(2,1)}), bf16[16,24,1152]{2,1,0:T(8,128)(2,1)S(1)}, u32[]{:S(2)}, u32[]{:S(2)}) async-start(bf16[16,24,1152]{2,1,0:T(8,128)(2,1)} %bitcast.43), calls=%async_computation.5 | async-start | bytes 1769472 | tf_op jit(solution)/shard_map/all_to_all | solution.py:152
  405.9 24.1 %embed_back.1 = (bf16[384,1024]{1,0:T(8,128)(2,1)}, bf16[384,1024]{1,0:T(8,128)(2,1)}) custom-call(s32[1]{0:T(128)} %bitcast.core_ref, f32[2048,768]{1,0:T(8,128)} %get-tuple-element.127.x0_ref.refs_0_, f32[2048,768]{1,0:T(8,128)} %get-tuple-element.160.refs_1_, bf16[1024,128]{1,0:T(8,128)(2,1)} %pad_maximum_fusion.3.refs_2_, bf16[1024,432]{1,0:T(8,128)(2,1)} %bitcast.102, ...), custom_call_target="tpu_custom_call" | custom-call | flops 289406976 | bytes 640000 | tf_op jit(solution)/shard_map/embed_back/pallas_call | solution.py:755
  431.8 2.1 collective-permute-done.9
  433.9 2.3 add_convert_fusion.2
  436.2 6.7 %all-to-all-start.5 = ((bf16[16,24,1024]{2,1,0:T(8,128)(2,1)}), bf16[16,24,1024]{2,1,0:T(8,128)(2,1)S(1)}, u32[]{:S(2)}, u32[]{:S(2)}) async-start(bf16[16,24,1024]{2,1,0:T(8,128)(2,1)} %bitcast.44), calls=%async_computation.6 | async-start | bytes 1572864 | tf_op jit(solution)/shard_map/all_to_all | solution.py:152
  445.0 1.3 multiply_reduce_fusion.6
  446.3 1.5 multiply_reduce_fusion.4
  447.8 1.6 multiply_reduce_fusion.2
  453.8 6.2 %all-to-all-done.5 = bf16[16,24,1024]{2,1,0:T(8,128)(2,1)S(1)} async-done(((bf16[16,24,1024]{2,1,0:T(8,128)(2,1)}), bf16[16,24,1024]{2,1,0:T(8,128)(2,1)S(1)}, u32[]{:S(2)}, u32[]{:S(2)}) %all-to-all-start.5) | async-done | bytes 786464 | tf_op jit(solution)/shard_map/all_to_all | solution.py:152
  467.5 7.3 %all-to-all-start.6 = ((f32[32,24,128]{2,1,0:T(8,128)}), f32[32,24,128]{2,1,0:T(8,128)S(1)}, u32[]{:S(2)}, u32[]{:S(2)}) async-start(f32[32,24,128]{2,1,0:T(8,128)} %copy.217), calls=%async_computation.7 | async-start | bytes 786432 | tf_op jit(solution)/shard_map/all_to_all | solution.py:1033
  474.8 13.2 %all-to-all-done.6 = f32[32,24,128]{2,1,0:T(8,128)S(1)} async-done(((f32[32,24,128]{2,1,0:T(8,128)}), f32[32,24,128]{2,1,0:T(8,128)S(1)}, u32[]{:S(2)}, u32[]{:S(2)}) %all-to-all-start.6) | async-done | bytes 393248 | tf_op jit(solution)/shard_map/all_to_all | solution.py:1033
  492.6 2.1 multiply_subtract_fusion.2
  495.7 1.5 multiply_subtract_fusion
  (218 shorter events, 43.9 us)
Async XLA Ops:
  7.2 120.8 %copy-start = (s32[4]{0:T(128)S(1)}, s32[4]{0:T(128)}, u32[]{:S(2)}) copy-start(s32[4]{0:T(128)} %param.35) | copy-start | bytes 52
  7.2 93.2 %all-gather.6.cloned.1.call-start = ((), (), s32[]{:S(2)}) async-start(), calls=%async_computation.8 | async-start | bytes 1824768 | tf_op jit(solution)/shard_map/all_gather | solution.py:857
  9.1 162.3 %all-gather.8.cloned.1.call-start = ((), (), s32[]{:S(2)}) async-start(), calls=%async_computation.9 | async-start | bytes 6082560 | tf_op jit(solution)/shard_map/all_gather | solution.py:878
  13.6 4.1 copy-start.39
  13.6 5.4 %copy-start.11 = (f32[96,768]{1,0:T(8,128)S(1)}, f32[96,768]{1,0:T(8,128)}, u32[]{:S(2)}) copy-start(f32[96,768]{1,0:T(8,128)} %param.41) | copy-start | bytes 884740
  14.9 13.4 %copy-start.35 = (f32[2,24]{1,0:T(2,128)S(1)}, f32[2,24]{1,0:T(2,128)}, u32[]{:S(2)}) copy-start(f32[2,24]{1,0:T(2,128)} %param.44) | copy-start | bytes 580
  14.9 14.3 %copy-start.30 = (f32[49,24]{0,1:T(8,128)S(1)}, f32[49,24]{0,1:T(8,128)}, u32[]{:S(2)}) copy-start(f32[49,24]{0,1:T(8,128)} %param.42) | copy-start | bytes 14116
  14.9 24.9 %collective-permute-start = (bf16[1024,432]{0,1:T(8,128)(2,1)}, bf16[1024,432]{0,1:T(8,128)(2,1)S(1)}, u32[]{:S(2)}, u32[]{:S(2)}) collective-permute-start(bf16[1024,432]{0,1:T(8,128)(2,1)} %copy.195), channel_id=1, source_target_pairs={{0,1},{1,0},{2,3},{3,2},{4,5},{5,4},{6,7},{7,6},{8,9},{9,8},{10,11... | collective-permute-start | bytes 2654216 | tf_op jit(solution)/shard_map/ppermute | solution.py:125
  19.3 20.9 %copy-start.8 = (f32[100,1024,1]{1,0,2:T(8,128)S(1)}, f32[100,1024,1]{1,0,2:T(8,128)}, u32[]{:S(2)}) copy-start(f32[100,1024,1]{1,0,2:T(8,128)} %constant.216) | copy-start | bytes 1228804
  20.1 19.7 %all-to-all-start = ((bf16[32,24,128]{2,1,0:T(8,128)(2,1)}), bf16[32,24,128]{2,1,0:T(8,128)(2,1)S(1)}, u32[]{:S(2)}, u32[]{:S(2)}) async-start(bf16[32,24,128]{2,1,0:T(8,128)(2,1)} %bitcast.7), calls=%async_computation | async-start | bytes 393216 | tf_op jit(solution)/shard_map/all_to_all | solution.py:843
  25.7 195.0 %all-gather.10.cloned.1.call-start = ((), (), s32[]{:S(2)}) async-start(), calls=%async_computation.10 | async-start | bytes 6488064 | tf_op jit(solution)/shard_map/all_gather | solution.py:882
  25.8 14.9 %copy-start.6 = (f32[144,1024,1]{1,0,2:T(8,128)S(1)}, f32[144,1024,1]{1,0,2:T(8,128)}, u32[]{:S(2)}) copy-start(f32[144,1024,1]{1,0,2:T(8,128)} %constant.215) | copy-start | bytes 1769476
  40.7 34.8 %copy-start.20 = (f32[24,1000]{1,0:T(8,128)S(1)}, f32[24,1000]{1,0:T(8,128)}, u32[]{:S(2)}) copy-start(f32[24,1000]{1,0:T(8,128)} %param.43) | copy-start | bytes 288004
  73.4 4.0 collective-permute-start.1
  82.1 17.3 %collective-permute-start.2 = (bf16[288,768]{1,0:T(8,128)(2,1)}, bf16[288,768]{1,0:T(8,128)(2,1)S(1)}, u32[]{:S(2)}, u32[]{:S(2)}) collective-permute-start(bf16[288,768]{1,0:T(8,128)(2,1)} %get-tuple-element.108), channel_id=1, source_target_pairs={{0,1},{1,0},{2,3},{3,2},{4,5},{5,4},{6,7},{7,6},{8,9},{9,8},{10,11... | collective-permute-start | bytes 1327112 | tf_op jit(solution)/shard_map/ppermute | solution.py:125
  85.7 39.6 %all-to-all-start.2 = ((bf16[16,24,1152]{2,1,0:T(8,128)(2,1)}), bf16[16,24,1152]{2,1,0:T(8,128)(2,1)S(1)}, u32[]{:S(2)}, u32[]{:S(2)}) async-start(bf16[16,24,1152]{2,1,0:T(8,128)(2,1)} %broadcast_in_dim.48), calls=%async_computation.2 | async-start | bytes 1769472 | tf_op jit(solution)/shard_map/all_to_all | solution.py:137
  89.7 9.7 %copy-start.19 = (bf16[288,768]{1,0:T(8,128)(2,1)S(1)}, bf16[288,768]{1,0:T(8,128)(2,1)}, u32[]{:S(2)}) copy-start(bf16[288,768]{1,0:T(8,128)(2,1)} %get-tuple-element.108) | copy-start | bytes 1327108
  89.7 200.2 %all-gather.12.cloned.1.call-start = ((), (), s32[]{:S(2)}) async-start(), calls=%async_computation.12 | async-start | bytes 1486848 | tf_op jit(solution)/shard_map/all_gather | solution.py:943
  125.3 5.4 %collective-permute-start.3 = (bf16[384,1152]{1,0:T(8,128)(2,1)S(1)}, bf16[384,1152]{1,0:T(8,128)(2,1)S(1)}, u32[]{:S(2)}, u32[]{:S(2)}) collective-permute-start(bf16[384,1152]{1,0:T(8,128)(2,1)S(1)} %bitcast.106), channel_id=1, source_target_pairs={{0,2},{2,0},{1,3},{3,1},{4,6},{6,4},{5,7},{7,5},{8,10},{10,8},{9,1... | collective-permute-start | bytes 2654216 | tf_op jit(solution)/shard_map/ppermute | solution.py:125
  179.8 29.7 %collective-permute-start.4 = (f32[1,3840]{1,0:T(1,128)S(1)}, f32[1,3840]{1,0:T(1,128)S(1)}, u32[]{:S(2)}, u32[]{:S(2)}) collective-permute-start(f32[1,3840]{1,0:T(1,128)S(1)} %pad_maximum_fusion.6), channel_id=1, source_target_pairs={{0,1},{1,0},{2,3},{3,2},{4,5},{5,4},{6,7},{7,6},{8,9},{9,8},{10,11... | collective-permute-start | bytes 46088 | tf_op jit(solution)/shard_map/ppermute | solution.py:125
  181.6 27.9 %copy-start.31 = (f32[1,1,3072]{2,1,0:T(1,128)S(1)}, f32[1,1,3072]{2,1,0:T(1,128)}, u32[]{:S(2)}) copy-start(f32[1,1,3072]{2,1,0:T(1,128)} %get-tuple-element.134) | copy-start | bytes 36868
  181.6 27.9 %copy-start.34 = (f32[1,1,768]{2,1,0:T(1,128)S(1)}, f32[1,1,768]{2,1,0:T(1,128)}, u32[]{:S(2)}) copy-start(f32[1,1,768]{2,1,0:T(1,128)} %get-tuple-element.133) | copy-start | bytes 9220
  230.1 200.1 %reduce-scatter.2.cloned.1.call-start = ((), (), s32[]{:S(2)}) async-start(), calls=%async_computation.11 | async-start | bytes 6082560 | tf_op jit(solution)/shard_map/reduce_scatter | solution.py:965
  282.4 56.2 %collective-permute-start.5 = (bf16[288,1152]{1,0:T(8,128)(2,1)}, bf16[288,1152]{1,0:T(8,128)(2,1)}, u32[]{:S(2)}, u32[]{:S(2)}) collective-permute-start(bf16[288,1152]{1,0:T(8,128)(2,1)} %slice.136), channel_id=1, source_target_pairs={{0,1},{1,0},{2,3},{3,2},{4,5},{5,4},{6,7},{7,6},{8,9},{9,8},{10,11... | collective-permute-start | bytes 1990664 | tf_op jit(solution)/shard_map/ppermute | solution.py:125
  294.8 46.1 %collective-permute-start.6 = (bf16[288,1152]{1,0:T(8,128)(2,1)}, bf16[288,1152]{1,0:T(8,128)(2,1)}, u32[]{:S(2)}, u32[]{:S(2)}) collective-permute-start(bf16[288,1152]{1,0:T(8,128)(2,1)} %slice.138), channel_id=1, source_target_pairs={{0,1},{1,0},{2,3},{3,2},{4,5},{5,4},{6,7},{7,6},{8,9},{9,8},{10,11... | collective-permute-start | bytes 1990664 | tf_op jit(solution)/shard_map/ppermute | solution.py:125
  295.0 43.5 %copy-start.3 = (bf16[576,1152]{1,0:T(8,128)(2,1)S(1)}, bf16[576,1152]{1,0:T(8,128)(2,1)}, u32[]{:S(2)}) copy-start(bf16[576,1152]{1,0:T(8,128)(2,1)} %attend_back_apart.3.d_a_ref) | copy-start | bytes 3981316
  338.5 4.6 copy-start.38
  338.5 7.4 %copy-start.15 = (bf16[384,1152]{1,0:T(8,128)(2,1)S(1)}, bf16[384,1152]{1,0:T(8,128)(2,1)}, u32[]{:S(2)}) copy-start(bf16[384,1152]{1,0:T(8,128)(2,1)} %get-tuple-element.174) | copy-start | bytes 2654212
  343.2 2.7 collective-permute-start.7
  347.0 47.6 %all-to-all-start.3 = ((bf16[16,24,1152]{2,1,0:T(8,128)(2,1)}), bf16[16,24,1152]{2,1,0:T(8,128)(2,1)S(1)}, u32[]{:S(2)}, u32[]{:S(2)}) async-start(bf16[16,24,1152]{2,1,0:T(8,128)(2,1)} %bitcast.42), calls=%async_computation.4 | async-start | bytes 1769472 | tf_op jit(solution)/shard_map/all_to_all | solution.py:152
  394.8 3.0 collective-permute-start.8
  399.0 31.0 %all-to-all-start.4 = ((bf16[16,24,1152]{2,1,0:T(8,128)(2,1)}), bf16[16,24,1152]{2,1,0:T(8,128)(2,1)S(1)}, u32[]{:S(2)}, u32[]{:S(2)}) async-start(bf16[16,24,1152]{2,1,0:T(8,128)(2,1)} %bitcast.43), calls=%async_computation.5 | async-start | bytes 1769472 | tf_op jit(solution)/shard_map/all_to_all | solution.py:152
  431.1 2.8 collective-permute-start.9
  436.2 23.8 %all-to-all-start.5 = ((bf16[16,24,1024]{2,1,0:T(8,128)(2,1)}), bf16[16,24,1024]{2,1,0:T(8,128)(2,1)S(1)}, u32[]{:S(2)}, u32[]{:S(2)}) async-start(bf16[16,24,1024]{2,1,0:T(8,128)(2,1)} %bitcast.44), calls=%async_computation.6 | async-start | bytes 1572864 | tf_op jit(solution)/shard_map/all_to_all | solution.py:152
  449.5 12.3 %copy-start.7 = (f32[144,1024,1]{1,0,2:T(8,128)S(1)}, f32[144,1024,1]{1,0,2:T(8,128)}, u32[]{:S(2)}) copy-start(f32[144,1024,1]{1,0,2:T(8,128)} %constant.215) | copy-start | bytes 1769476
  449.6 12.7 %copy-start.9 = (f32[100,1024,1]{1,0,2:T(8,128)S(1)}, f32[100,1024,1]{1,0,2:T(8,128)}, u32[]{:S(2)}) copy-start(f32[100,1024,1]{1,0,2:T(8,128)} %constant.216) | copy-start | bytes 1228804
  467.5 20.5 %all-to-all-start.6 = ((f32[32,24,128]{2,1,0:T(8,128)}), f32[32,24,128]{2,1,0:T(8,128)S(1)}, u32[]{:S(2)}, u32[]{:S(2)}) async-start(f32[32,24,128]{2,1,0:T(8,128)} %copy.217), calls=%async_computation.7 | async-start | bytes 786432 | tf_op jit(solution)/shard_map/all_to_all | solution.py:1033
  488.5 3.2 copy-start.21
  488.6 3.2 copy-start.22
  488.6 3.2 copy-start.26
  488.6 3.2 copy-start.27
  488.8 3.8 copy-start.13
  489.6 5.0 copy-start.12
  489.7 4.9 copy-start.24
  489.7 4.9 copy-start.25
  492.5 3.2 copy-start.10
  492.5 3.2 copy-start.17
  492.6 3.2 copy-start.18
  (13 other events, 24.8 us)
Sparse Core Ops, SparseCore 0:
  11.6 60.7 all-gather.5
  75.8 73.3 all-gather.7
  152.6 67.9 all-gather.9
  230.2 53.3 all-gather.11
  292.7 126.3 reduce-scatter.1

commit v3 on v2

--- a/solution.py
+++ b/solution.py
@@ -117,6 +117,7 @@
 BF = jnp.bfloat16
 F32 = jnp.float32
 VMEM_BYTES = 58 << 20
+QUERY_SCALE = HEAD_DIM**-0.5 * math.log2(math.e)
 
 
 def shift(value, axis, steps):
@@ -129,13 +130,12 @@
     return tuple(lax.axis_size(axis) for axis in CHIPS)
 
 
-def gather_rows(value, token=None):
+def gather_rows(value):
     rows, cols = value.shape
     z, x, y = chip_sizes()
     chips = z * x * y
     copies = jnp.broadcast_to(value[None], (chips, rows, cols)).reshape(chips * rows, cols)
     mine = lax.all_to_all(copies, CHIPS, split_axis=0, concat_axis=0, tiled=True)
-    mine = mine if token is None else after(mine, token)
     other = shift(mine, "core", 1)
     parts = [part.reshape(z, x, 1, y, rows, cols) for part in (mine, other)]
     first = lax.axis_index("core") == 0
@@ -146,11 +146,12 @@
 
 
 def scatter_rows(away, own):
-    z, x, y = chip_sizes()
-    chips = z * x * y
     both = (own.astype(F32) + shift(away, "core", 1).astype(F32)).astype(BF)
-    got = lax.all_to_all(both, CHIPS, split_axis=0, concat_axis=0, tiled=True)
-    return jnp.sum(got.reshape(chips, own.shape[0] // chips, own.shape[1]).astype(F32), 0)
+    return lax.all_to_all(both, CHIPS, split_axis=0, concat_axis=0, tiled=True)
+
+
+def block_sum(got, rows):
+    return jnp.sum(got.reshape(-1, rows, got.shape[1]).astype(F32), 0)
 
 
 def store_by_core(core, acc, away_ref, own_ref, count):
@@ -252,14 +253,14 @@
     values = rows_ref[:, 256:]
     keys = head_split(first, rows_ref[:, 128:256])
     sided = (jnp.where(first, values, one).T, jnp.where(first, one, values).T)
-    query = rows_ref[:n_query, :128] * jnp.asarray(HEAD_DIM**-0.5, BF)
+    query = rows_ref[:n_query, :128]
     scores = [dot(keys[head], query, NT) for head in range(2)]
     if between is not None:
         between()
     tops, probs, mixed = [], [], []
     for head in range(2):
         tops.append(jnp.max(scores[head], 0, keepdims=True))
-        probs.append(jnp.exp(scores[head] - tops[head]).astype(BF))
+        probs.append(jnp.exp2(scores[head] - tops[head]).astype(BF))
         mixed.append(dot(sided[head], probs[head], NN))
     outs = []
     for head in range(2):
@@ -267,7 +268,7 @@
         total = mixed[head][at : at + 1]
         own = HEAD_DIM * head
         outs.append(mixed[head][own : own + HEAD_DIM] / total)
-        log_ref[0, 0, head : head + 1, :] = tops[head] + jnp.log(total)
+        log_ref[0, 0, head : head + 1, :] = tops[head] + jnp.log2(total)
     out_ref[...] = jnp.concatenate(outs, 0).T.astype(BF)
 
 
@@ -275,7 +276,9 @@
     step = pl.program_id(0)
 
     def project():
-        rows = dot(h1_ref[...], weight_ref[...], NN).astype(BF)
+        lane = lax.broadcasted_iota(jnp.int32, (1, 384), 1)
+        scale = jnp.where(lane < 128, QUERY_SCALE, 1.0)
+        rows = (dot(h1_ref[...], weight_ref[...], NN) * scale).astype(BF)
         qkv_ref[...] = rows
         held[step % 2] = rows
 
@@ -295,10 +298,9 @@
         attend()
 
 
-def attend_pairs(h1, weight, images, n_query):
+def attend_pairs(h1, weight, first, pairs, images, n_query):
     rows, width = h1.shape
     count = rows // images
-    pairs = weight.shape[1] // 384
     items = images * pairs
     now = lambda s: jnp.minimum(s, items - 1)
     last = lambda s: jnp.maximum(s - 1, 0)
@@ -312,7 +314,7 @@
         grid=(items + 1,),
         in_specs=[
             pl.BlockSpec((count, width), lambda s: (now(s) // pairs, 0)),
-            pl.BlockSpec((width, 384), lambda s: (0, now(s) % pairs)),
+            pl.BlockSpec((width, 384), lambda s: (0, first + now(s) % pairs)),
         ],
         out_specs=[
             pl.BlockSpec((count, 384), lambda s: (now(s) // pairs, now(s) % pairs)),
@@ -337,7 +339,7 @@
     keys_all = kv_ref[:, 128:256]
     keys = head_split(first, keys_all)
     values = head_split(first, kv_ref[:, 256:])
-    query = q_ref[:, :128] * scale
+    query = q_ref[:, :128]
     d_out = do_ref[...]
     queries = head_split(first, query)
     d_outs = head_split(first, d_out)
@@ -347,13 +349,13 @@
     for head in range(2):
         row = jnp.sum(both[HEAD_DIM * head : HEAD_DIM * (head + 1)], 0, keepdims=True)
         scores = dot(keys[head], query, NT)
-        probs = jnp.exp(scores - log_ref[0, 0, head : head + 1, :])
+        probs = jnp.exp2(scores - log_ref[0, 0, head : head + 1, :])
         d_probs = dot(values[head], d_out, NT)
         d_scores = (probs * (d_probs - row)).astype(BF)
         d_keys = d_keys + dot(d_scores, queries[head], NN)
         d_values = d_values + dot(probs.astype(BF), d_outs[head], NN)
         d_query = d_query + dot(keys_t[head], d_scores, NN)
-    return d_query.astype(BF), d_keys.astype(BF), d_values.astype(BF)
+    return d_query.astype(BF), (d_keys * math.log(2.0)).astype(BF), d_values.astype(BF)
 
 
 def attend_back_kernel(q_ref, kv_ref, do_ref, o_ref, log_ref, d_ref):
@@ -476,9 +478,8 @@
         asum_ref[0, :, cols] += jnp.sum(inner * upper, 0, keepdims=True)
 
 
-def mlp(x0, mixed, w_up_out, gain, images, block):
+def mlp(x0, mixed, w_all, hidden, gain, images, block):
     rows, width = x0.shape
-    hidden = w_up_out.shape[1] - width
     per = rows // images // block
     return pl.pallas_call(
         partial(mlp_kernel, per=per),
@@ -493,9 +494,9 @@
             pl.BlockSpec((block, width), lambda i: (i, 0)),
             pl.BlockSpec((block, width // 2), lambda i: (i, 0)),
             pl.BlockSpec((block, width // 2), lambda i: (i, 0)),
-            pl.BlockSpec((width, width), lambda i: (0, hidden // width)),
+            pl.BlockSpec((width, width), lambda i: (0, 3)),
             pl.BlockSpec((1, width), lambda i: (0, 0)),
-            pl.BlockSpec((width, hidden), lambda i: (0, 0)),
+            pl.BlockSpec((width, hidden), lambda i: (0, 4 * width // hidden)),
         ],
         out_specs=[
             pl.BlockSpec((block, width), lambda i: (i, 0)),
@@ -506,7 +507,7 @@
         compiler_params=pltpu.CompilerParams(vmem_limit_bytes=VMEM_BYTES),
         cost_estimate=estimate(4 * rows * width * (hidden + width), rows * hidden * 4),
         name="mlp",
-    )(x0, *mixed, w_up_out, gain, w_up_out)
+    )(x0, *mixed, w_all, gain, w_all)
 
 
 def head_kernel(
@@ -526,7 +527,8 @@
     low = (asum - high.astype(F32)).astype(BF)
     whole = whole_ref[...]
     down = down_ref[...]
-    pooled = (xsum + (dot(high, down, NT) + dot(low, down, NT))) / whole
+    both = dot(jnp.concatenate([high, low], 0), down, NT)
+    pooled = (xsum + (both[: both.shape[0] // 2] + both[both.shape[0] // 2 :])) / whole
     pooled_low = pooled.astype(BF)
     head = head_ref[...]
     place = lax.broadcasted_iota(jnp.int32, (1, head.shape[1]), 1)
@@ -600,19 +602,21 @@
         gain = gain_ref[...]
         hat, scale = normed(x1_ref[...])
         h2_t = (hat * gain).astype(BF).T
-        d_h2 = 0.0
         width = 768
-        for first in range(0, slope_ref.shape[1], width):
-            cols = slice(first, first + width)
-            d_inner = (slope_ref[:, cols].astype(F32) * dact_ref[0, :, cols]).astype(BF)
-            d_h2 = d_h2 + dot(d_inner, wup_ref[:, cols], NT)
-            grad = dot(h2_t, d_inner, NN)
-            up_acc[:, cols] = grad if begin else up_acc[:, cols] + grad
+        cuts = [slice(first, first + width) for first in range(0, slope_ref.shape[1], width)]
+        d_inner = [
+            (slope_ref[:, cols].astype(F32) * dact_ref[0, :, cols]).astype(BF) for cols in cuts
+        ]
+        d_h2 = sum(dot(part, wup_ref[:, cols], NT) for part, cols in zip(d_inner, cuts))
         gain_grad = jnp.sum(d_h2 * hat, 0, keepdims=True)
         ggain_ref[...] = gain_grad if begin else ggain_ref[...] + gain_grad
-        d_x1 = dx2_ref[0] + norm_back(d_h2, gain, hat, scale)
-        dx1_ref[...] = d_x1
-        d_attn = d_x1.astype(BF)
+        rows = x1_ref.shape[0] // len(cuts)
+        for index, (part, cols) in enumerate(zip(d_inner, cuts)):
+            share = slice(index * rows, (index + 1) * rows)
+            grad = dot(h2_t, part, NN)
+            up_acc[:, cols] = grad if begin else up_acc[:, cols] + grad
+            dx1_ref[share] = dx2_ref[0] + norm_back(d_h2[share], gain, hat[share], scale[share])
+        d_attn = dx1_ref[...].astype(BF)
         mixed = jnp.concatenate([mixed_ref[...] for mixed_ref in mixed_refs], 1)
         grad = dot(mixed.T, d_attn, NN)
         out_acc[...] = grad if begin else out_acc[...] + grad
@@ -636,7 +640,7 @@
         grad_ref[:, hidden:] = out_acc[...].astype(BF)
 
 
-def mlp_back(part_b, part_a, w_up_out, gain, images, block):
+def mlp_back(part_b, part_a, w_all, gain, images, block):
     rows, width = part_b[2].shape
     rows_a = part_a[2].shape[0]
     hidden = part_b[0].shape[1]
@@ -667,9 +671,9 @@
             moving(hidden), image(hidden), moving(width), image(width), moving(half), moving(half),
             still((rows_a, hidden)), last(hidden), still((rows_a, width)),
             last(width), still((rows_a, half)), still((rows_a, half)),
-            pl.BlockSpec((width, width), lambda i: (0, hidden // width)),
+            pl.BlockSpec((width, width), lambda i: (0, 3)),
             still((1, width)),
-            still((width, hidden)),
+            pl.BlockSpec((width, hidden), lambda i: (0, 4 * width // hidden)),
         ],
         out_specs=[
             moving(width), moving(half), moving(half),
@@ -682,18 +686,18 @@
             4 * (rows + rows_a) * width * (hidden + width), (rows + rows_a) * hidden * 4
         ),
         name="mlp_back",
-    )(*part_b, *part_a, w_up_out, gain, w_up_out)
-
-
-def embed_back_kernel(core_ref, *refs, steps, groups, pieces, blocks, parts_b):
-    n_b, n_a = 3 + pieces + groups, 4 + groups
+    )(*part_b, *part_a, w_all, gain, w_all)
+
+
+def embed_back_kernel(core_ref, *refs, steps, groups, pieces, blocks, parts_b, parts_a):
+    n_b, n_a = 3 + pieces + groups, 4 + groups * parts_a
     inputs_b, inputs_a = refs[:n_b], refs[n_b : n_b + n_a]
     gain_ref, gain_grad_ref, *rest = refs[n_b + n_a :]
     weight_refs = rest[:groups]
     away_ref, own_ref, acc_b, acc_a, acc_tab, gain_acc = rest[groups:]
     step = pl.program_id(0)
 
-    def body(inputs, acc, parts, pixel_ref):
+    def body(inputs, acc, parts, pixel_ref, terms):
         x0_ref, dx1_ref, tab_ref = inputs[:3]
         gain = gain_ref[...]
         count = x0_ref.shape[0] // parts
@@ -702,8 +706,12 @@
             rows = slice(part * count, (part + 1) * count)
             hat, scale = normed(x0_ref[rows])
             d_h1 = 0.0
-            for ref, weight_ref in zip(inputs[-groups:], weight_refs):
-                d_h1 = d_h1 + dot(ref[rows], weight_ref[...], NT)
+            for group, weight_ref in enumerate(weight_refs):
+                term_refs = inputs[len(inputs) - (groups - group) * terms :][:terms]
+                d_qkv = term_refs[0][rows]
+                if terms > 1:
+                    d_qkv = sum(ref[rows].astype(F32) for ref in term_refs).astype(BF)
+                d_h1 = d_h1 + dot(d_qkv, weight_ref[...], NT)
             gain_acc[0:1] += jnp.sum(d_h1 * hat, 0, keepdims=True)
             d_x0 = dx1_ref[rows] + norm_back(d_h1, gain, hat, scale)
             turned.append(d_x0.astype(BF).T)
@@ -716,13 +724,13 @@
         for acc in (acc_b, acc_a, acc_tab, gain_acc):
             acc[...] = jnp.zeros_like(acc)
         gain_acc[1:2] = gain_grad_ref[...]
-        body(inputs_a, acc_a, 1, inputs_a[3])
+        body(inputs_a, acc_a, 1, inputs_a[3], parts_a)
 
     for piece in range(pieces):
 
         @pl.when((step > 0) & ((step - 1) % pieces == piece))
         def _(piece=piece):
-            body(inputs_b, acc_b, parts_b, inputs_b[3 + piece])
+            body(inputs_b, acc_b, parts_b, inputs_b[3 + piece], 1)
 
     @pl.when(step == steps)
     def _():
@@ -740,7 +748,7 @@
 
 
 def embed_back(
-    x0_b, dx1_b, tab_b, pixels_b, d_b, x0_a, dx1_a, tab_a, pixels_a, d_a, gain, gain_grad, w_qkv,
+    x0_b, dx1_b, tab_b, pixels_b, d_b, x0_a, dx1_a, tab_a, pixels_a, d_a, gain, gain_grad, w_all,
     core, blocks, images, depths
 ):
     rows, width = x0_b.shape
@@ -750,12 +758,13 @@
     at = lambda i: jnp.maximum(i - 1, 0)
     moving = lambda array: pl.BlockSpec((block, array.shape[1]), lambda i: (at(i), 0))
     still = lambda shape: pl.BlockSpec(shape, lambda i: (0,) * len(shape))
-    inputs_a = (x0_a, dx1_a, tab_a, pixels_a, *d_a)
+    inputs_a = (x0_a, dx1_a, tab_a, pixels_a, *sum(d_a, ()))
+    rows_a = x0_a.shape[0]
     grad = (width // 2, sum(depths) + 128)
     return pl.pallas_call(
         partial(
             embed_back_kernel, steps=steps, groups=len(d_b), pieces=pieces, blocks=blocks,
-            parts_b=max(1, block // 256),
+            parts_b=max(1, block // 256), parts_a=len(d_a[0]),
         ),
         out_shape=(jax.ShapeDtypeStruct(grad, BF), jax.ShapeDtypeStruct(grad, BF)),
         grid=(steps + 1,),
@@ -767,16 +776,122 @@
             for array in pixels_b
         ]
         + [moving(array) for array in d_b]
-        + [still(array.shape) for array in inputs_a]
+        + [still((rows_a, array.shape[1])) for array in inputs_a]
         + [still((1, width)), still((1, width))]
-        + [still(weight.shape) for weight in w_qkv],
+        + [
+            pl.BlockSpec((width, array.shape[1]), partial(lambda group, i: (0, group), group))
+            for group, array in enumerate(d_b)
+        ],
         out_specs=[still(grad), still(grad)],
         scratch_shapes=[pltpu.VMEM((width, depth), F32) for depth in (*depths, 128)]
         + [pltpu.VMEM((8, width), F32)],
         compiler_params=pltpu.CompilerParams(vmem_limit_bytes=VMEM_BYTES),
         cost_estimate=estimate(2 * rows * width * (3 * width + 640), rows * 10000),
         name="embed_back",
-    )(core, x0_b, dx1_b, tab_b, *pixels_b, *d_b, *inputs_a, gain, gain_grad, *w_qkv)
+    )(core, x0_b, dx1_b, tab_b, *pixels_b, *d_b, *inputs_a, gain, gain_grad, *[w_all] * len(d_b))
+
+
+def resize_back_kernel(got_ref, table_b_ref, table_a_ref, sums_ref, sent_ref, small_ref, *, rows, at):
+    owners, _, lanes = sent_ref.shape
+    total = jnp.zeros(small_ref.shape, F32)
+    for block in range(got_ref.shape[0] // rows):
+        total = total + got_ref[block * rows : (block + 1) * rows].astype(F32)
+    small_ref[...] = total
+    parts, square = [], 0.0
+    for channel in range(3):
+        part = 0.0
+        for table_ref, first in ((table_b_ref, 0), (table_a_ref, at)):
+            size = table_ref.shape[0]
+            part = part + lax.dot_general(
+                total[:, first + channel * size : first + (channel + 1) * size],
+                table_ref[...],
+                NN,
+                precision=HIGH,
+                preferred_element_type=F32,
+            )
+        square = square + jnp.sum(part * part)
+        parts.append(part)
+    width = BASE * BASE * 3 // owners
+    kern = jnp.concatenate(parts + [jnp.zeros((rows, lanes), F32)], 1)
+    lane = lax.broadcasted_iota(jnp.int32, (1, lanes), 1)
+    last = total[:, total.shape[1] - lanes :]
+    pos = jnp.where(lane < 49, last + pltpu.roll(last, lanes - 49, 1), 0.0)
+    last = jnp.where(lane < 126, pos, last)
+    small_ref[:, total.shape[1] - lanes :] = last
+    square = square + jnp.sum(last * last) + jnp.sum(jnp.where(lane == 0, sums_ref[...], 0.0))
+    beside = jnp.where(lane == width, square, 0.0)
+    for index in (1, 2):
+        beside = beside + jnp.where(lane == width + index, pltpu.roll(sums_ref[...], width, 1), 0.0)
+    for owner in range(owners):
+        sent_ref[owner] = jnp.where(
+            lane < width, kern[:, owner * width : owner * width + lanes], beside
+        )
+
+
+def resize_back(got, tables, sums, rows, at, owners, lanes):
+    cols = got.shape[1]
+    return pl.pallas_call(
+        partial(resize_back_kernel, rows=rows, at=at),
+        out_shape=(
+            jax.ShapeDtypeStruct((owners, rows, lanes), F32),
+            jax.ShapeDtypeStruct((rows, cols), F32),
+        ),
+        in_specs=[pl.BlockSpec(memory_space=pltpu.VMEM)] * 4,
+        out_specs=[pl.BlockSpec(memory_space=pltpu.VMEM)] * 2,
+        compiler_params=pltpu.CompilerParams(vmem_limit_bytes=VMEM_BYTES),
+        cost_estimate=estimate(1 << 28, 4 << 20),
+        name="resize_back",
+    )(got, *tables, sums)
+
+
+def update_kernel(got_ref, small_ref, qkv_ref, out_ref, up_ref, down_ref, head_ref, count_ref, *refs, width):
+    masters, firsts, seconds = refs[0:7], refs[7:14], refs[14:21]
+    new, new_firsts, new_seconds = refs[21:28], refs[28:35], refs[35:42]
+    norm_ref, stat_ref = refs[42:]
+    owners, rows, lanes = got_ref.shape
+    sums = got_ref[0, 0:1, :]
+    for owner in range(1, owners):
+        sums = sums + got_ref[owner, 0:1, :]
+    lane = lax.broadcasted_iota(jnp.int32, (1, lanes), 1)
+    norm = jnp.sqrt(jnp.sum(jnp.where(lane == width, sums, 0.0), 1, keepdims=True))
+    factor = jnp.minimum(1.0, CLIP / (norm + 1e-06))
+    sums = pltpu.roll(sums, lanes - width, 1)
+    ratio = sums / jnp.maximum(count_ref[...], 1.0)
+    norm_ref[...] = norm
+    stat_ref[...] = ratio[:, 1:3]
+    kern = jnp.concatenate([got_ref[owner] for owner in range(owners)], 0).T[:width]
+    small = small_ref[:, small_ref.shape[1] - lanes :]
+    grads = (
+        (Ellipsis, qkv_ref[...]),
+        (Ellipsis, out_ref[...]),
+        (0, up_ref[...]),
+        (1, down_ref[...]),
+        (Ellipsis, kern),
+        (Ellipsis, small[:, :49]),
+        (Ellipsis, head_ref[...]),
+        (Ellipsis, small[:, 126:128].T),
+    )
+    for index, (at, grad) in zip((0, 1, 2, 2, 3, 4, 5, 6), grads):
+        new[index][at], new_firsts[index][at], new_seconds[index][at] = adamw(
+            masters[index][at], firsts[index][at], seconds[index][at], grad * factor, RATES[index]
+        )
+
+
+def update(got, small, grads, count, masters, firsts, seconds, width):
+    full = pl.BlockSpec(memory_space=pltpu.VMEM)
+    shapes = [jax.ShapeDtypeStruct(array.shape, F32) for array in masters]
+    inputs = (got, small, *grads, count, *masters, *firsts, *seconds)
+    return pl.pallas_call(
+        partial(update_kernel, width=width),
+        out_shape=(
+            *shapes * 3, jax.ShapeDtypeStruct((1, 1), F32), jax.ShapeDtypeStruct((1, 2), F32)
+        ),
+        in_specs=[full] * len(inputs),
+        out_specs=[full] * 23,
+        compiler_params=pltpu.CompilerParams(vmem_limit_bytes=VMEM_BYTES),
+        cost_estimate=estimate(1 << 28, 16 << 20),
+        name="update",
+    )(*inputs)
 
 
 def after(value, *others):
@@ -854,7 +969,14 @@
         return shaped.transpose(0, 2, 1, 3).reshape(rows_own, 3 * span)
 
     qkv_low = qkv_w.astype(BF)
-    w_groups = [lax.all_gather(group_cols(qkv_low, 0), AXES, axis=0, tiled=True)]
+    w_all = lax.all_gather(
+        jnp.concatenate(
+            [group_cols(qkv_low, group) for group in range(groups)]
+            + [out_w.astype(BF), mlp_w[0].astype(BF)],
+            1,
+        ),
+        AXES, axis=0, tiled=True,
+    )
 
     tables = [resize_table(PATCH_B), resize_table(PATCH_A)]
     sizes = [3 * table.shape[0] for table in tables]
@@ -874,11 +996,6 @@
         1,
     )
     w_small = gather_rows(small)
-    second = group_cols(qkv_low, 1)
-    w_up_out = lax.all_gather(
-        after(jnp.concatenate([mlp_w[0].astype(BF), out_w.astype(BF)], 1), got),
-        AXES, axis=0, tiled=True,
-    )
     w_down_head = lax.all_gather(
         after(
             jnp.concatenate([mlp_w[1].astype(BF), padded_cols(head_w.astype(BF), classes_up)], 1),
@@ -900,19 +1017,19 @@
     outs_a, outs_b = [], []
     ready = h1_b
     for group in range(groups):
-        if group:
-            w_groups.append(gather_rows(after(second, h1_a), ready))
-        outs_b.append(attend_pairs(after(h1_b, ready), w_groups[group], own_b, whole_b))
+        outs_b.append(
+            attend_pairs(after(h1_b, ready), w_all, group * pairs, pairs, own_b, whole_b)
+        )
         ready = outs_b[-1][0]
     for group in range(groups):
-        outs_a.append(attend_pairs(after(h1_all, ready), w_groups[group], 1, span_a))
+        outs_a.append(attend_pairs(after(h1_all, ready), w_all, group * pairs, pairs, 1, span_a))
     qkvs_a, qkvs_b = [out[0] for out in outs_a], [out[0] for out in outs_b]
     mixed_a, mixed_b = [out[1] for out in outs_a], [out[1] for out in outs_b]
 
-    x1_a, slope_a, xsum_a, asum_a = mlp(x0_a, mixed_a, w_up_out, gain2, 1, span_a)
+    x1_a, slope_a, xsum_a, asum_a = mlp(x0_a, mixed_a, w_all, hidden, gain2, 1, span_a)
     sums_a = jnp.concatenate([xsum_a[0], asum_a[0]], 1)
     sums_a = sum([shift(sums_a, "y", step) for step in range(1, seq)], sums_a)
-    x1_b, slope_b, xsum_b, asum_b = mlp(after(x0_b, x1_a), mixed_b, w_up_out, gain2, own_b, block)
+    x1_b, slope_b, xsum_b, asum_b = mlp(after(x0_b, x1_a), mixed_b, w_all, hidden, gain2, own_b, block)
 
     counts, labels_a, labels_b, live_b, alive_a = lax.optimization_barrier(
         (counts, labels_a, labels_b, live_b, alive_a, h1_b)
@@ -940,12 +1057,12 @@
          jnp.sum(alive_b * losses[:own_b, :1])]
     )
 
-    image_rows = lax.all_gather(rows_out[: round_up(own_b + 1, 4)], AXES, axis=0, tiled=True)
+    image_rows = lax.all_gather(rows_out, AXES, axis=0, tiled=True)
 
     d_x1_b, d0_b, d1_b, d_x1_a, d0_a, d1_a, grad_up_out, grad_gain2 = mlp_back(
         (slope_b, d_act, x1_b, d_x2, *mixed_b),
         (slope_a, d_act, x1_a, d_x2, *mixed_a),
-        w_up_out, gain2, own_b, block,
+        w_all, gain2, own_b, block,
     )
     d_mixed_a, d_mixed_b = (d0_a, d1_a), (d0_b, d1_b)
 
@@ -955,13 +1072,11 @@
             qkvs_a[group], qkvs_a[group], d_mixed_a[group], mixed_a[group],
             outs_a[group][2], pairs, span_a, seq * span_a,
         )
-        own = d_all[:span_a].astype(F32)
-        for step in range(1, seq):
-            own = own + shift(
-                d_all[step * span_a : (step + 1) * span_a], "y", seq - step
-            ).astype(F32)
         d_alls.append(d_all)
-        d_groups_a.append(own.astype(BF))
+        d_groups_a += [
+            shift(d_all[step * span_a : (step + 1) * span_a], "y", seq - step)
+            for step in range(1, seq)
+        ]
     own_up_out = lax.psum_scatter(
         after(grad_up_out, image_rows, *d_alls), AXES, scatter_dimension=0, tiled=True
     ).astype(F32)
@@ -983,25 +1098,23 @@
         d_groups_b.append(got)
         own_groups.append(scatter_rows(away, own))
         ready = got
+    moved = seq - 1
+    d_groups_a = [
+        (d_all, *d_groups_a[group * moved : (group + 1) * moved])
+        for group, d_all in enumerate(d_alls)
+    ]
     away, own = embed_back(
         x0_b, after(d_x1_b, ready), tab_b, parts_b, d_groups_b,
         x0_a, d_x1_a, tab_a, flat_a, d_groups_a,
-        gain1, grad_gain2, w_groups, core, blocks, own_b, depths,
+        gain1, grad_gain2, w_all, core, blocks, own_b, depths,
     )
     away, own, own_up_out, *own_groups = lax.optimization_barrier(
         (away, own, own_up_out, *own_groups)
     )
-    own_qkv = jnp.stack(own_groups, 1).reshape(rows_own, groups * pairs, 3, 128)
+    own_qkv = jnp.stack([block_sum(got, rows_own) for got in own_groups], 1)
+    own_qkv = own_qkv.reshape(rows_own, groups * pairs, 3, 128)
     own_qkv = own_qkv.transpose(0, 2, 1, 3).reshape(rows_own, 3 * width)
-    own_small = scatter_rows(away, own)
-    kern_t = jnp.zeros((rows_own, 3, BASE * BASE), F32)
-    for table, size, at in zip(tables, sizes, (0, depths[0])):
-        piece = own_small[:, at : at + size].reshape(rows_own, 3, -1)
-        kern_t = kern_t + jnp.einsum("dcp,pk->dck", piece, jnp.asarray(table), precision=HIGH)
-    own_pos = own_small[:, spot : spot + 49] + own_small[:, spot + 49 : spot + 98]
-    kern_t = kern_t.reshape(rows_own, count_all, rows_kern)
-    own_pos = own_pos.T
-    own_gain = own_small[:, -2:].T
+    small_parts = scatter_rows(away, own)
 
     columns = lambda lo: lax.dynamic_slice_in_dim(
         image_rows[:, lo : lo + width], flat_index * rows_own, rows_own, 1
@@ -1017,35 +1130,22 @@
     )
     own_up, own_out = own_up_out[:, :hidden], own_up_out[:, hidden:]
     square_sum = sum(
-        jnp.sum(piece * piece)
-        for piece in (own_up_out, own_down, own_head, own_qkv, kern_t, own_pos, own_gain)
-    )
-
-    sums = jnp.concatenate([square_sum.reshape(1), loss_sums])
-    sent = jnp.concatenate(
-        [
-            kern_t.transpose(1, 0, 2),
-            jnp.broadcast_to(sums[None, None], (count_all, rows_own, 3)),
-            jnp.zeros((count_all, rows_own, lanes - rows_kern - 3), F32),
-        ],
-        2,
+        jnp.sum(piece * piece) for piece in (own_up_out, own_down, own_head, own_qkv)
+    )
+    sums = padded_cols(jnp.concatenate([square_sum.reshape(1), loss_sums])[None], lanes)
+    sent, own_small = resize_back(
+        small_parts, [jnp.asarray(table) for table in tables], sums, rows_own, depths[0],
+        count_all, lanes,
     )
     got = lax.all_to_all(sent, AXES, split_axis=0, concat_axis=0, tiled=True)
-    own_kern = got[:, :, :rows_kern].reshape(count_all * rows_own, rows_kern).T
-    sums = jnp.sum(got[:, 0, rows_kern : rows_kern + 3], 0)
-    grad_norm = jnp.sqrt(sums[0])
-    factor = jnp.minimum(1.0, CLIP / (grad_norm + 1e-06))
-    own_mlp = jnp.stack([own_up, own_down], 0)
-    owned = (own_qkv, own_out, own_mlp, own_kern, own_pos, own_head, own_gain)
-    done = [adamw(masters[i], firsts[i], seconds[i], owned[i] * factor, RATES[i]) for i in range(7)]
-    size_stats = sums[1:] / jnp.maximum(count[0], 1.0)
-    return (
-        *(item[0] for item in done),
-        *(item[1] for item in done),
-        *(item[2] for item in done),
-        size_stats,
-        grad_norm,
-    )
+    counts = padded_cols(jnp.pad(count, ((0, 0), (1, 0))), lanes)
+    turn = lambda arrays: [array.T if at == 4 else array for at, array in enumerate(arrays)]
+    *done, grad_norm, size_stats = update(
+        got, own_small, (own_qkv, own_out, own_up, own_down, own_head), counts,
+        turn(masters), turn(firsts), turn(seconds), rows_kern,
+    )
+    done = [item for at in (0, 7, 14) for item in turn(done[at : at + 7])]
+    return (*done, size_stats.reshape(2), grad_norm.reshape(()))
 
 
 def fits_fast(mesh, pixels_a, pixels_b):

time: 511 us -> 497 us (0.973)
  other arithmetic: 34.4 us -> 20.8 us
  starting transfers between devices: 45.9 us -> 38.4 us
  waiting for transfers between devices: 48.3 us -> 55.4 us
  local copies, waits for them, and re-layouts: 27.7 us -> 21.3 us
  Pallas kernels: 288 us -> 294 us
    all_gather x3 -> x2, waiting for transfers between devices: 0.02 us -> 13.8 us  [the longest x1 10.2 us: fast_step(): lax.all_gather(jnp.concatenate([group_cols(qkv_low, group) for group in r...]
    all_gather x1, waiting for transfers between devices: 10.5 us -> 0.01 us  [fast_step(): lax.all_gather(after(jnp.concatenate([mlp_w[1].astype(BF), padded_cols(he...]
    pallas_call x0 -> x2, Pallas kernels: none -> 9.35 us  [the longest x1 5.48 us: update(): pl.pallas_call(partial(update_kernel, width=width), out_shape=(*shapes *...]
    sub x7 -> x0, other arithmetic: 7.43 us -> none  [adamw(): return (weight - rate * (step_dir + 0.1 * weight), first, second)]
    ppermute x10 -> x9, waiting for transfers between devices: 7.66 us -> 14.5 us  [shift(): return lax.ppermute(value, axis, pairs)]
    all_to_all x4 -> x3, starting transfers between devices: 21.8 us -> 18.1 us  [scatter_rows(): return lax.all_to_all(both, CHIPS, split_axis=0, concat_axis=0, tiled=True)]
    ppermute x10 -> x9, starting transfers between devices: 10.7 us -> 7.35 us  [shift(): return lax.ppermute(value, axis, pairs)]
  transfers between devices with their start and end apart: 21 -> 18, of which waited for: 8 -> 9; matrix products, arithmetic and copies ran while one was open for 9% -> 8% of each run, Pallas kernels for 55% -> 56%
where the time goes in v3:
time: 497 us; the launch traced here: 493 us
  Pallas kernels  294 us (59%)
  waiting for transfers between devices  55.4 us (11%)
  starting transfers between devices  38.4 us (8%)
  blocking collectives  35.9 us (7%)
  local copies, waits for them, and re-layouts  21.3 us (4%)
  other arithmetic  20.8 us (4%)
  between operations  20.5 us (4%)
  matrix products  6.58 us (1%)
    pallas_call x2, Pallas kernels, attend_back_grad(): pl.pallas_call(partial(attend_back_grad_kernel, images=images, blocks=blo...  86.1 us
    pallas_call x4, Pallas kernels, attend_pairs(): pl.pallas_call(partial(attend_kernel, items=items, n_query=n_query), out_...  63 us
    pallas_call x1, Pallas kernels, mlp_back(): pl.pallas_call(partial(mlp_back_kernel, steps=steps), out_shape=(*outs, j...  42.1 us
    all_to_all x1, blocking collectives, gather_rows(): lax.all_to_all(copies, CHIPS, split_axis=0, concat_axis=0, tiled=True)  35.9 us
    pallas_call x2, Pallas kernels, mlp(): pl.pallas_call(partial(mlp_kernel, per=per), out_shape=(jax.ShapeDtypeStr...  35.8 us
    pallas_call x1, Pallas kernels, embed_back(): pl.pallas_call(partial(embed_back_kernel, steps=steps, groups=len(d_b), p...  24.6 us
    all_to_all x2, waiting for transfers between devices, fast_step(): got = lax.all_to_all(sent, AXES, split_axis=0, concat_axis=0, tiled=True)  22.7 us
    all_to_all x3, starting transfers between devices, scatter_rows(): return lax.all_to_all(both, CHIPS, split_axis=0, concat_axis=0, tiled=True)  18.1 us
  transfers between devices with their start and end apart: 18, of which 9 were waited for; matrix products, arithmetic and copies ran while one was open for 8% of the time, Pallas kernels for 56%

profile of v3, /device:TPU:1, one launch (start us, length us, event | category | flops | bytes accessed | tf_op | source)
XLA Modules:
  0.0 492.6 jit_solution(3643518590233548249)
XLA Ops:
  10.9 1.2 constant_dynamic-slice_fusion.3
  12.6 2.1 collective-permute-start
  17.8 5.6 %all-to-all-start = ((bf16[32,24,128]{2,1,0:T(8,128)(2,1)}), bf16[32,24,128]{2,1,0:T(8,128)(2,1)S(1)}, u32[]{:S(2)}, u32[]{:S(2)}) async-start(bf16[32,24,128]{2,1,0:T(8,128)(2,1)} %bitcast.7), calls=%async_computation | async-start | bytes 393216 | tf_op jit(solution)/shard_map/all_to_all | solution.py:958
  24.4 1.5 constant_dynamic-slice_fusion.2.refs_1_.refs_9_
  26.8 12.3 %all-to-all-done = bf16[32,24,128]{2,1,0:T(8,128)(2,1)S(1)} async-done(((bf16[32,24,128]{2,1,0:T(8,128)(2,1)}), bf16[32,24,128]{2,1,0:T(8,128)(2,1)S(1)}, u32[]{:S(2)}, u32[]{:S(2)}) %all-to-all-start) | async-done | bytes 196640 | tf_op jit(solution)/shard_map/all_to_all | solution.py:958
  40.9 35.9 %all_to_all.61 = bf16[16,24,1024]{2,1,0:T(8,128)(2,1)S(1)} all-to-all(bf16[16,24,1024]{2,1,0:T(8,128)(2,1)S(1)} %broadcast_in_dim.37), channel_id=1, replica_groups=mesh['z'=4,'x'=2,'core'=2,'y'=2] {'z','x','y'}, dimensions={0} | all-to-all | bytes 1572864 | tf_op jit(solution)/shard_map/all_to_all | solution.py:138
  76.8 1.2 collective-permute-start.1
  78.7 2.3 collective-permute-done.1
  82.6 3.2 embed.2
  87.2 1.4 copy.130.refs_1_.refs_4_
  88.5 9.5 %embed.3 = (f32[2048,768]{1,0:T(8,128)}, bf16[2048,768]{1,0:T(8,128)(2,1)}) custom-call(bf16[1024,432]{1,0:T(8,128)(2,1)} %bitcast.81, bf16[1024,432]{1,0:T(8,128)(2,1)} %copy.130.refs_1_.refs_4_, bf16[1024,128]{1,0:T(8,128)(2,1)} %pad_maximum_fusion.3.refs_2_, bf16[768,1024]{1,0:T(8,128)(2,1)} %bitcast.80, f32[1,768]{1,0:T(1,128)} %get-tuple-element.246.refs_3_.refs_4_.refs_15_), custom_call_target="tpu_custom_call" | custom-call | flops 2415919104 | bytes 12582912 | tf_op jit(solution)/shard_map/embed/pallas_call | solution.py:231
  98.0 7.6 %collective-permute-done.2 = bf16[288,768]{1,0:T(8,128)(2,1)S(1)} collective-permute-done((bf16[288,768]{1,0:T(8,128)(2,1)}, bf16[288,768]{1,0:T(8,128)(2,1)S(1)}, u32[]{:S(2)}, u32[]{:S(2)}) %collective-permute-start.2) | collective-permute-done | bytes 442400 | tf_op jit(solution)/shard_map/ppermute | solution.py:126
  109.7 10.2 %all-gather.4.cloned.1.call-done.weight_ref.wout_ref.wup_ref.refs_12_.refs_14_.refs_17_.refs_18_ = bf16[768,6144]{1,0:T(8,128)(2,1)} async-done(((bf16[24,6144]{1,0:T(8,128)(2,1)}), bf16[768,6144]{1,0:T(8,128)(2,1)}) %all-gather.4.cloned.1.call-update) | async-done | bytes 9437200 | tf_op jit(solution)/shard_map/all_gather | solution.py:972
  119.8 24.8 %attend.4 = (bf16[2048,1152]{1,0:T(8,128)(2,1)}, bf16[2048,384]{1,0:T(8,128)(2,1)}, f32[2,3,2,1024]{3,2,1,0:T(2,128)}) custom-call(bf16[2048,768]{1,0:T(8,128)(2,1)} %get-tuple-element.142.h1_ref, bf16[768,6144]{1,0:T(8,128)(2,1)} %all-gather.4.cloned.1.call-done.weight_ref.wout_ref.wup_ref.refs_12_.refs_14_.refs_17_.refs_18_), custom_call_target="tpu_custom_call" | custom-call | flops 18723373056 | bytes 12582912 | tf_op jit(solution)/shard_map/attend/pallas_call | solution.py:307
  144.7 25.1 %attend.5 = (bf16[2048,1152]{1,0:T(8,128)(2,1)}, bf16[2048,384]{1,0:T(8,128)(2,1)}, f32[2,3,2,1024]{3,2,1,0:T(2,128)}) custom-call(bf16[2048,768]{1,0:T(8,128)(2,1)} %get-tuple-element.142.h1_ref, bf16[768,6144]{1,0:T(8,128)(2,1)} %all-gather.4.cloned.1.call-done.weight_ref.wout_ref.wup_ref.refs_12_.refs_14_.refs_17_.refs_18_), custom_call_target="tpu_custom_call" | custom-call | flops 18723373056 | bytes 12582912 | tf_op jit(solution)/shard_map/attend/pallas_call | solution.py:307
  169.8 6.3 %attend.7 = (bf16[576,1152]{1,0:T(8,128)(2,1)}, bf16[288,384]{1,0:T(8,128)(2,1)}, f32[1,3,2,288]{3,2,1,0:T(2,128)}) custom-call(bf16[576,768]{1,0:T(8,128)(2,1)} %pad_maximum_fusion.1.h1_ref.h1_a_ref, bf16[768,6144]{1,0:T(8,128)(2,1)} %all-gather.4.cloned.1.call-done.weight_ref.wout_ref.wup_ref.refs_12_.refs_14_.refs_17_.refs_18_), custom_call_target="tpu_custom_call" | custom-call | flops 2213609472 | bytes 3538944 | tf_op jit(solution)/shard_map/attend/pallas_call | solution.py:307
  176.1 6.7 %attend.6 = (bf16[576,1152]{1,0:T(8,128)(2,1)}, bf16[288,384]{1,0:T(8,128)(2,1)}, f32[1,3,2,288]{3,2,1,0:T(2,128)}) custom-call(bf16[576,768]{1,0:T(8,128)(2,1)} %pad_maximum_fusion.1.h1_ref.h1_a_ref, bf16[768,6144]{1,0:T(8,128)(2,1)} %all-gather.4.cloned.1.call-done.weight_ref.wout_ref.wup_ref.refs_12_.refs_14_.refs_17_.refs_18_), custom_call_target="tpu_custom_call" | custom-call | flops 2213609472 | bytes 3538944 | tf_op jit(solution)/shard_map/attend/pallas_call | solution.py:307
  182.9 8.0 %mlp.2 = (f32[288,768]{1,0:T(8,128)}, bf16[288,3072]{1,0:T(8,128)(2,1)}, f32[1,1,768]{2,1,0:T(1,128)}, f32[1,1,3072]{2,1,0:T(1,128)}) custom-call(f32[288,768]{1,0:T(8,128)} %get-tuple-element.136.x0_ref.refs_7_, bf16[288,384]{1,0:T(8,128)(2,1)} %get-tuple-element.145.mixed0_ref.refs_10_.o_ref, ...), custom_call_target="tpu_custom_call" | custom-call | flops 106168320 | bytes 110592 | tf_op jit(solution)/shard_map/mlp/pallas_call | solution.py:484
  191.6 27.9 %mlp.3 = (f32[2048,768]{1,0:T(8,128)}, bf16[2048,3072]{1,0:T(8,128)(2,1)}, f32[2,1,768]{2,1,0:T(1,128)}, f32[2,1,3072]{2,1,0:T(1,128)}) custom-call(f32[2048,768]{1,0:T(8,128)} %get-tuple-element.148.x0_ref.refs_0_, bf16[2048,384]{1,0:T(8,128)(2,1)} %get-tuple-element.149.mixed0_ref.refs_4_.o_ref, ...), custom_call_target="tpu_custom_call" | custom-call | flops 754974720 | bytes 786432 | tf_op jit(solution)/shard_map/mlp/pallas_call | solution.py:484
  220.1 7.2 %head.1 = (f32[8,128]{1,0:T(8,128)}, bf16[8,5632]{1,0:T(8,128)(2,1)}, f32[3,1,768]{2,1,0:T(1,128)}, f32[3,1,3072]{2,1,0:T(1,128)}) custom-call(f32[2,1,768]{2,1,0:T(1,128)} %get-tuple-element.152.xsum_ref, f32[2,1,3072]{2,1,0:T(1,128)} %get-tuple-element.153.asum_ref, f32[1,3840]{1,0:T(1,128)} %fusion.14.sums_a_ref, ...), custom_call_target="tpu_custom_call" | custom-call | flops 134217728 | bytes 262144 | tf_op jit(solution)/shard_map/head/pallas_call | solution.py:568
  227.5 42.1 %mlp_back.1 = (f32[2048,768]{1,0:T(8,128)}, bf16[2048,384]{1,0:T(8,128)(2,1)}, bf16[2048,384]{1,0:T(8,128)(2,1)}, f32[288,768]{1,0:T(8,128)}, bf16[288,384]{1,0:...) custom-call(bf16[2048,3072]{1,0:T(8,128)(2,1)} %get-tuple-element.151.refs_0_, ...), custom_call_target="tpu_custom_call" | custom-call | flops 861143040 | bytes 897024 | tf_op jit(solution)/shard_map/mlp_back/pallas_call | solution.py:662
  269.6 6.5 %attend_back_apart.3.d_a_ref.refs_11_ = bf16[576,1152]{1,0:T(8,128)(2,1)} custom-call(bf16[576,1152]{1,0:T(8,128)(2,1)} %get-tuple-element.174.q_ref.kv_ref, bf16[576,1152]{1,0:T(8,128)(2,1)} %get-tuple-element.174.q_ref.kv_ref, bf16[288,384]{1,0:T(8,128)(2,1)} %get-tuple-element.175.do_ref, bf16[288,384]{1,0:T(8,128)(2,1)} %get-tuple-element.145.mixed0_ref.refs_10_.o_ref, ...), custom_call_target="tpu_custom_call" | custom-call | flops 74649600 | bytes 82944 | tf_op jit(solution)/shard_map/attend_back_apart/pallas_call | solution.py:373
  276.1 6.4 %attend_back_apart.2.d_a_ref.refs_13_ = bf16[576,1152]{1,0:T(8,128)(2,1)} custom-call(bf16[576,1152]{1,0:T(8,128)(2,1)} %get-tuple-element.169.q_ref.kv_ref, bf16[576,1152]{1,0:T(8,128)(2,1)} %get-tuple-element.169.q_ref.kv_ref, bf16[288,384]{1,0:T(8,128)(2,1)} %get-tuple-element.170.do_ref, bf16[288,384]{1,0:T(8,128)(2,1)} %get-tuple-element.146.mixed1_ref.refs_11_.o_ref, ...), custom_call_target="tpu_custom_call" | custom-call | flops 74649600 | bytes 82944 | tf_op jit(solution)/shard_map/attend_back_apart/pallas_call | solution.py:373
  282.5 3.6 all-gather.8.cloned.1.call-done
  286.1 1.3 copy-done.3
  287.4 1.3 copy-done.2
  288.8 1.3 collective-permute-start.4
  290.3 43.0 %attend_back.2 = (bf16[2048,1152]{1,0:T(8,128)(2,1)}, bf16[384,1152]{1,0:T(8,128)(2,1)}, bf16[384,1152]{1,0:T(8,128)(2,1)}) custom-call(s32[1]{0:T(128)} %bitcast.core_ref, bf16[2048,1152]{1,0:T(8,128)(2,1)} %get-tuple-element.141.qkv_ref, bf16[2048,384]{1,0:T(8,128)(2,1)} %get-tuple-element.172.do_ref, ...), custom_call_target="tpu_custom_call" | custom-call | flops 1101004800 | bytes 393216 | tf_op jit(solution)/shard_map/attend_back/pallas_call | solution.py:419
  334.2 2.3 collective-permute-done.6
  336.5 2.3 add_convert_fusion.1
  338.7 4.4 all-to-all-start.2
  343.1 43.1 %attend_back.3 = (bf16[2048,1152]{1,0:T(8,128)(2,1)}, bf16[384,1152]{1,0:T(8,128)(2,1)}, bf16[384,1152]{1,0:T(8,128)(2,1)}) custom-call(s32[1]{0:T(128)} %bitcast.core_ref, bf16[2048,1152]{1,0:T(8,128)(2,1)} %get-tuple-element.143.qkv_ref, bf16[2048,384]{1,0:T(8,128)(2,1)} %get-tuple-element.178.do_ref, ...), custom_call_target="tpu_custom_call" | custom-call | flops 1101004800 | bytes 393216 | tf_op jit(solution)/shard_map/attend_back/pallas_call | solution.py:419
  387.0 2.3 collective-permute-done.7
  389.3 2.3 add_convert_fusion
  391.6 6.9 %all-to-all-start.3 = ((bf16[16,24,1152]{2,1,0:T(8,128)(2,1)}), bf16[16,24,1152]{2,1,0:T(8,128)(2,1)S(1)}, u32[]{:S(2)}, u32[]{:S(2)}) async-start(bf16[16,24,1152]{2,1,0:T(8,128)(2,1)} %bitcast.39), calls=%async_computation.4 | async-start | bytes 1769472 | tf_op jit(solution)/shard_map/all_to_all | solution.py:150
  398.5 24.6 %embed_back.1 = (bf16[384,1024]{1,0:T(8,128)(2,1)}, bf16[384,1024]{1,0:T(8,128)(2,1)}) custom-call(s32[1]{0:T(128)} %bitcast.core_ref, f32[2048,768]{1,0:T(8,128)} %get-tuple-element.148.x0_ref.refs_0_, f32[2048,768]{1,0:T(8,128)} %get-tuple-element.181.refs_1_, bf16[1024,128]{1,0:T(8,128)(2,1)} %pad_maximum_fusion.3.refs_2_, bf16[1024,432]{1,0:T(8,128)(2,1)} %bitcast.82, ...), custom_call_target="tpu_custom_call" | custom-call | flops 289406976 | bytes 640000 | tf_op jit(solution)/shard_map/embed_back/pallas_call | solution.py:764
  425.0 1.2 slice.74
  426.9 1.3 multiply_reduce_fusion.4
  428.2 2.3 add_convert_fusion.2
  430.4 6.8 %all-to-all-start.4 = ((bf16[16,24,1024]{2,1,0:T(8,128)(2,1)}), bf16[16,24,1024]{2,1,0:T(8,128)(2,1)S(1)}, u32[]{:S(2)}, u32[]{:S(2)}) async-start(bf16[16,24,1024]{2,1,0:T(8,128)(2,1)} %bitcast.85), calls=%async_computation.5 | async-start | bytes 1572864 | tf_op jit(solution)/shard_map/all_to_all | solution.py:150
  437.2 1.2 fusion.15
  438.4 2.6 multiply_reduce_fusion.3
  441.0 3.1 multiply_reduce_fusion.2
  450.3 4.3 all-to-all-done.4
  455.5 3.9 resize_back.1
  459.3 7.0 %all-to-all-start.5 = ((f32[32,24,128]{2,1,0:T(8,128)}), f32[32,24,128]{2,1,0:T(8,128)S(1)}, u32[]{:S(2)}, u32[]{:S(2)}) async-start(f32[32,24,128]{2,1,0:T(8,128)} %get-tuple-element.206), calls=%async_computation.6 | async-start | bytes 786432 | tf_op jit(solution)/shard_map/all_to_all | solution.py:1140
  469.2 10.4 %all-to-all-done.5.got_ref = f32[32,24,128]{2,1,0:T(8,128)S(1)} async-done(((f32[32,24,128]{2,1,0:T(8,128)}), f32[32,24,128]{2,1,0:T(8,128)S(1)}, u32[]{:S(2)}, u32[]{:S(2)}) %all-to-all-start.5) | async-done | bytes 393248 | tf_op jit(solution)/shard_map/all_to_all | solution.py:1140
  480.3 5.5 %update.1 = (f32[24,2304]{1,0:T(8,128)}, f32[24,768]{1,0:T(8,128)}, f32[2,24,3072]{2,1,0:T(8,128)}, f32[96,768]{1,0:T(8,128)}, f32[24,49]{1,0:T(8,128)}, /*index...) custom-call(f32[32,24,128]{2,1,0:T(8,128)} %copy-done.8, ...), custom_call_target="tpu_custom_call" | custom-call | flops 8388608 | bytes 524288 | tf_op jit(solution)/shard_map/update/pallas_call | solution.py:884
  (143 shorter events, 29.0 us)
Async XLA Ops:
  7.2 99.7 %copy-start = (s32[4]{0:T(128)S(1)}, s32[4]{0:T(128)}, u32[]{:S(2)}) copy-start(s32[4]{0:T(128)} %param.35) | copy-start | bytes 52
  7.2 2.3 copy-start.6
  7.2 112.6 %all-gather.4.cloned.1.call-start = ((), (), s32[]{:S(2)}) async-start(), calls=%async_computation.7 | async-start | bytes 9732096 | tf_op jit(solution)/shard_map/all_gather | solution.py:972
  9.2 1.7 copy-start.7
  12.0 3.3 copy-start.20
  12.0 4.7 copy-start.9
  12.0 13.9 %copy-start.19 = (f32[2,24]{1,0:T(2,128)S(1)}, f32[2,24]{1,0:T(2,128)}, u32[]{:S(2)}) copy-start(f32[2,24]{1,0:T(2,128)} %refs_6_.1) | copy-start | bytes 580
  12.5 14.3 %copy-start.16 = (f32[49,24]{0,1:T(8,128)S(1)}, f32[49,24]{0,1:T(8,128)}, u32[]{:S(2)}) copy-start(f32[49,24]{0,1:T(8,128)} %param.42) | copy-start | bytes 14116
  12.6 26.6 %collective-permute-start = (bf16[1024,432]{0,1:T(8,128)(2,1)S(1)}, bf16[1024,432]{0,1:T(8,128)(2,1)S(1)}, u32[]{:S(2)}, u32[]{:S(2)}) collective-permute-start(bf16[1024,432]{0,1:T(8,128)(2,1)S(1)} %copy.121), channel_id=1, source_target_pairs={{0,1},{1,0},{2,3},{3,2},{4,5},{5,4},{6,7},{7,6},{8,9},{9,8},{10,11... | collective-permute-start | bytes 2654216 | tf_op jit(solution)/shard_map/ppermute | solution.py:126
  16.8 22.7 %copy-start.14 = (f32[100,1024,1]{1,0,2:T(8,128)S(1)}, f32[100,1024,1]{1,0,2:T(8,128)}, u32[]{:S(2)}) copy-start(f32[100,1024,1]{1,0,2:T(8,128)} %constant.134) | copy-start | bytes 1228804
  17.8 22.3 %copy-start.12 = (f32[144,1024,1]{1,0,2:T(8,128)S(1)}, f32[144,1024,1]{1,0,2:T(8,128)}, u32[]{:S(2)}) copy-start(f32[144,1024,1]{1,0,2:T(8,128)} %constant.133) | copy-start | bytes 1769476
  17.8 21.4 %all-to-all-start = ((bf16[32,24,128]{2,1,0:T(8,128)(2,1)}), bf16[32,24,128]{2,1,0:T(8,128)(2,1)S(1)}, u32[]{:S(2)}, u32[]{:S(2)}) async-start(bf16[32,24,128]{2,1,0:T(8,128)(2,1)} %bitcast.7), calls=%async_computation | async-start | bytes 393216 | tf_op jit(solution)/shard_map/all_to_all | solution.py:958
  23.4 196.8 %all-gather.6.cloned.1.call-start = ((), (), s32[]{:S(2)}) async-start(), calls=%async_computation.8 | async-start | bytes 6488064 | tf_op jit(solution)/shard_map/all_gather | solution.py:999
  40.1 37.9 %copy-start.15 = (f32[24,1000]{1,0:T(8,128)S(1)}, f32[24,1000]{1,0:T(8,128)}, u32[]{:S(2)}) copy-start(f32[24,1000]{1,0:T(8,128)} %refs_5_.1) | copy-start | bytes 288004
  76.8 4.2 collective-permute-start.1
  81.4 1.2 copy-start.4
  81.5 204.6 %all-gather.8.cloned.1.call-start = ((), (), s32[]{:S(2)}) async-start(), calls=%async_computation.9 | async-start | bytes 2973696 | tf_op jit(solution)/shard_map/all_gather | solution.py:1060
  85.8 19.9 %collective-permute-start.2 = (bf16[288,768]{1,0:T(8,128)(2,1)}, bf16[288,768]{1,0:T(8,128)(2,1)S(1)}, u32[]{:S(2)}, u32[]{:S(2)}) collective-permute-start(bf16[288,768]{1,0:T(8,128)(2,1)} %get-tuple-element.131), channel_id=1, source_target_pairs={{0,1},{1,0},{2,3},{3,2},{4,5},{5,4},{6,7},{7,6},{8,9},{9,8},{10,11... | collective-permute-start | bytes 1327112 | tf_op jit(solution)/shard_map/ppermute | solution.py:126
  88.5 17.1 %copy-start.13 = (bf16[288,768]{1,0:T(8,128)(2,1)S(1)}, bf16[288,768]{1,0:T(8,128)(2,1)}, u32[]{:S(2)}) copy-start(bf16[288,768]{1,0:T(8,128)(2,1)} %get-tuple-element.131) | copy-start | bytes 1327108
  191.5 28.0 %collective-permute-start.3 = (f32[1,3840]{1,0:T(1,128)S(1)}, f32[1,3840]{1,0:T(1,128)S(1)}, u32[]{:S(2)}, u32[]{:S(2)}) collective-permute-start(f32[1,3840]{1,0:T(1,128)S(1)} %pad_maximum_fusion.5), channel_id=1, source_target_pairs={{0,1},{1,0},{2,3},{3,2},{4,5},{5,4},{6,7},{7,6},{8,9},{9,8},{10,11... | collective-permute-start | bytes 46088 | tf_op jit(solution)/shard_map/ppermute | solution.py:126
  191.6 27.9 %copy-start.17 = (f32[1,1,3072]{2,1,0:T(1,128)S(1)}, f32[1,1,3072]{2,1,0:T(1,128)}, u32[]{:S(2)}) copy-start(f32[1,1,3072]{2,1,0:T(1,128)} %get-tuple-element.155) | copy-start | bytes 36868
  191.6 27.9 %copy-start.18 = (f32[1,1,768]{2,1,0:T(1,128)S(1)}, f32[1,1,768]{2,1,0:T(1,128)}, u32[]{:S(2)}) copy-start(f32[1,1,768]{2,1,0:T(1,128)} %get-tuple-element.154) | copy-start | bytes 9220
  227.4 195.7 %reduce-scatter.2.cloned.1.call-start = ((), (), s32[]{:S(2)}) async-start(), calls=%async_computation.10 | async-start | bytes 6082560 | tf_op jit(solution)/shard_map/reduce_scatter | solution.py:1080
  286.1 1.3 copy-start.3
  287.4 1.3 copy-start.2
  288.8 44.5 %collective-permute-start.4 = (bf16[288,1152]{1,0:T(8,128)(2,1)S(1)}, bf16[288,1152]{1,0:T(8,128)(2,1)S(1)}, u32[]{:S(2)}, u32[]{:S(2)}) collective-permute-start(bf16[288,1152]{1,0:T(8,128)(2,1)S(1)} %slice.87), channel_id=1, source_target_pairs={{0,1},{1,0},{2,3},{3,2},{4,5},{5,4},{6,7},{7,6},{8,9},{9,8},{10,11... | collective-permute-start | bytes 1990664 | tf_op jit(solution)/shard_map/ppermute | solution.py:126
  290.0 43.3 %collective-permute-start.5 = (bf16[288,1152]{1,0:T(8,128)(2,1)S(1)}, bf16[288,1152]{1,0:T(8,128)(2,1)S(1)}, u32[]{:S(2)}, u32[]{:S(2)}) collective-permute-start(bf16[288,1152]{1,0:T(8,128)(2,1)S(1)} %slice.88), channel_id=1, source_target_pairs={{0,1},{1,0},{2,3},{3,2},{4,5},{5,4},{6,7},{7,6},{8,9},{9,8},{10,11... | collective-permute-start | bytes 1990664 | tf_op jit(solution)/shard_map/ppermute | solution.py:126
  333.3 5.4 %copy-start.10 = (bf16[288,1152]{1,0:T(8,128)(2,1)}, bf16[288,1152]{1,0:T(8,128)(2,1)S(1)}, u32[]{:S(2)}) copy-start(bf16[288,1152]{1,0:T(8,128)(2,1)S(1)} %collective-permute-done.4.refs_12_) | copy-start | bytes 1990660
  333.3 5.4 %copy-start.11 = (bf16[288,1152]{1,0:T(8,128)(2,1)}, bf16[288,1152]{1,0:T(8,128)(2,1)S(1)}, u32[]{:S(2)}) copy-start(bf16[288,1152]{1,0:T(8,128)(2,1)S(1)} %collective-permute-done.5.refs_14_) | copy-start | bytes 1990660
  333.3 3.1 collective-permute-start.6
  338.7 47.5 %all-to-all-start.2 = ((bf16[16,24,1152]{2,1,0:T(8,128)(2,1)}), bf16[16,24,1152]{2,1,0:T(8,128)(2,1)S(1)}, u32[]{:S(2)}, u32[]{:S(2)}) async-start(bf16[16,24,1152]{2,1,0:T(8,128)(2,1)} %bitcast.37), calls=%async_computation.3 | async-start | bytes 1769472 | tf_op jit(solution)/shard_map/all_to_all | solution.py:150
  386.3 3.0 collective-permute-start.7
  391.6 32.5 %all-to-all-start.3 = ((bf16[16,24,1152]{2,1,0:T(8,128)(2,1)}), bf16[16,24,1152]{2,1,0:T(8,128)(2,1)S(1)}, u32[]{:S(2)}, u32[]{:S(2)}) async-start(bf16[16,24,1152]{2,1,0:T(8,128)(2,1)} %bitcast.39), calls=%async_computation.4 | async-start | bytes 1769472 | tf_op jit(solution)/shard_map/all_to_all | solution.py:150
  424.1 4.1 collective-permute-start.8
  430.4 24.1 %all-to-all-start.4 = ((bf16[16,24,1024]{2,1,0:T(8,128)(2,1)}), bf16[16,24,1024]{2,1,0:T(8,128)(2,1)S(1)}, u32[]{:S(2)}, u32[]{:S(2)}) async-start(bf16[16,24,1024]{2,1,0:T(8,128)(2,1)} %bitcast.85), calls=%async_computation.5 | async-start | bytes 1572864 | tf_op jit(solution)/shard_map/all_to_all | solution.py:150
  454.5 0.9 copy-start.5
  459.3 20.2 %all-to-all-start.5 = ((f32[32,24,128]{2,1,0:T(8,128)}), f32[32,24,128]{2,1,0:T(8,128)S(1)}, u32[]{:S(2)}, u32[]{:S(2)}) async-start(f32[32,24,128]{2,1,0:T(8,128)} %get-tuple-element.206), calls=%async_computation.6 | async-start | bytes 786432 | tf_op jit(solution)/shard_map/all_to_all | solution.py:1140
  479.6 0.7 copy-start.8
  479.6 6.2 %copy-start.1 = (s32[4]{0:T(128)S(1)}, s32[4]{0:T(128)}, u32[]{:S(2)}) copy-start(s32[4]{0:T(128)} %param.35) | copy-start | bytes 52
Sparse Core Ops, SparseCore 0:
  11.5 108.2 all-gather.3
  123.3 68.1 all-gather.5
  227.5 58.4 all-gather.7
  291.6 127.8 reduce-scatter.1

commit v4 on v3

--- a/solution.py
+++ b/solution.py
@@ -130,19 +130,76 @@
     return tuple(lax.axis_size(axis) for axis in CHIPS)
 
 
-def gather_rows(value):
+def gather_rows(value, beside):
     rows, cols = value.shape
     z, x, y = chip_sizes()
     chips = z * x * y
     copies = jnp.broadcast_to(value[None], (chips, rows, cols)).reshape(chips * rows, cols)
     mine = lax.all_to_all(copies, CHIPS, split_axis=0, concat_axis=0, tiled=True)
+    mine, *beside = lax.optimization_barrier((mine, *beside))
     other = shift(mine, "core", 1)
     parts = [part.reshape(z, x, 1, y, rows, cols) for part in (mine, other)]
     first = lax.axis_index("core") == 0
     both = jnp.concatenate(
         [jnp.where(first, parts[0], parts[1]), jnp.where(first, parts[1], parts[0])], 2
     )
-    return both.reshape(2 * chips * rows, cols)
+    return both.reshape(2 * chips * rows, cols), beside
+
+
+STAGES = (*CHIPS, "core")
+
+
+def stage(held, axis):
+    return [held] + [shift(held, axis, step) for step in range(1, lax.axis_size(axis))]
+
+
+def stage_owners():
+    strides, stride = {}, 1
+    for axis in reversed(AXES):
+        strides[axis] = stride
+        stride = stride * lax.axis_size(axis)
+    shifts = [{}]
+    for axis in STAGES:
+        shifts = [{**known, axis: step} for step in range(lax.axis_size(axis)) for known in shifts]
+    owner = jnp.zeros((stride,), jnp.int32)
+    for axis in AXES:
+        steps = np.array([known[axis] for known in shifts], np.int32)
+        owner = owner + ((lax.axis_index(axis) - steps) % lax.axis_size(axis)) * strides[axis]
+    return owner
+
+
+def place_blocks_kernel(owner_ref, *refs):
+    *pieces, out_ref, sems = refs
+    copies = []
+    for piece in pieces:
+        for index in range(piece.shape[0]):
+            block = len(copies)
+            copies.append(
+                pltpu.make_async_copy(
+                    piece.at[index], out_ref.at[owner_ref[block]], sems.at[block]
+                )
+            )
+    for copy in copies:
+        copy.start()
+    for copy in copies:
+        copy.wait()
+
+
+def place_blocks(pieces, owner):
+    count = owner.shape[0]
+    _, rows, cols = pieces[0].shape
+    out = pl.pallas_call(
+        place_blocks_kernel,
+        out_shape=jax.ShapeDtypeStruct((count, rows, cols), BF),
+        in_specs=[pl.BlockSpec(memory_space=pltpu.SMEM)]
+        + [pl.BlockSpec(memory_space=pl.ANY)] * len(pieces),
+        out_specs=pl.BlockSpec(memory_space=pltpu.VMEM),
+        scratch_shapes=[pltpu.SemaphoreType.DMA((count,))],
+        compiler_params=pltpu.CompilerParams(vmem_limit_bytes=VMEM_BYTES),
+        cost_estimate=estimate(0, count * rows * cols * 4, 1),
+        name="place_blocks",
+    )(owner, *pieces)
+    return out.reshape(count * rows, cols)
 
 
 def scatter_rows(away, own):
@@ -150,17 +207,18 @@
     return lax.all_to_all(both, CHIPS, split_axis=0, concat_axis=0, tiled=True)
 
 
-def block_sum(got, rows):
-    return jnp.sum(got.reshape(-1, rows, got.shape[1]).astype(F32), 0)
-
-
-def store_by_core(core, acc, away_ref, own_ref, count):
-    rows = acc.shape[0] // count // 2
+def block_sum(got):
+    return jnp.sum(got.astype(F32), 0)
+
+
+def store_by_core(core, acc, away_ref, own_ref, cols, count):
+    blocks, rows, _ = own_ref.shape
+    per = blocks // count
     for pair in range(count):
-        at = slice(pair * rows, (pair + 1) * rows)
         for side, ref in ((core, own_ref), (1 - core, away_ref)):
-            first = pl.multiple_of((2 * pair + side) * rows, rows)
-            ref[at, :] = acc[pl.ds(first, rows), :].astype(BF)
+            for block in range(per):
+                first = pl.multiple_of(((2 * pair + side) * per + block) * rows, rows)
+                ref[pair * per + block, :, cols] = acc[pl.ds(first, rows), :].astype(BF)
 
 
 def interp_table(n_out, n_in):
@@ -210,12 +268,16 @@
 def embed_kernel(*refs, pieces, at, depth, spot):
     pixel_refs, (tab_ref, weight_ref, gain_ref, *rest) = refs[:pieces], refs[pieces:]
     x0_ref, h1_ref = rest
-    base = dot(tab_ref[...], weight_ref[:, spot : spot + tab_ref.shape[1]], NT)
+    shares = 2 if tab_ref.shape[0] % 512 == 0 else 1
+    count = tab_ref.shape[0] // shares
 
     def body(pixel_ref):
-        x0 = base + dot(pixel_ref[...], weight_ref[:, at : at + depth], NT)
-        x0_ref[...] = x0
-        h1_ref[...] = (normed(x0)[0] * gain_ref[...]).astype(BF)
+        for share in range(shares):
+            rows = slice(share * count, (share + 1) * count)
+            x0 = dot(tab_ref[rows], weight_ref[:, spot : spot + tab_ref.shape[1]], NT)
+            x0 = x0 + dot(pixel_ref[rows], weight_ref[:, at : at + depth], NT)
+            x0_ref[rows] = x0
+            h1_ref[rows] = (normed(x0)[0] * gain_ref[...]).astype(BF)
 
     for piece, pixel_ref in enumerate(pixel_refs):
         pl.when(pl.program_id(1) == piece)(partial(body, pixel_ref))
@@ -408,20 +470,23 @@
     @pl.when(image == images - 1)
     def _():
         turned[...] = acc[...].T
-        store_by_core(core_ref[0], turned, away_ref, own_ref, blocks)
-
-
-def attend_back_grad(qkv, d_out, out, log, h1, h1_a, d_a, core, pairs, images, count, blocks):
+        store_by_core(core_ref[0], turned, away_ref, own_ref, slice(None), blocks)
+
+
+def attend_back_grad(
+    qkv, d_out, out, log, h1, h1_a, d_a, core, pairs, images, count, blocks, count_y
+):
     width = h1.shape[1]
     rows_a = h1_a.shape[0]
     over = lambda cols: pl.BlockSpec((count, cols), lambda h, i: (i, h))
-    grad = pl.BlockSpec((width // 2, 384), lambda h, i: (0, h))
+    held = (count_y * blocks, width // (2 * count_y * blocks))
+    grad = pl.BlockSpec((*held, 384), lambda h, i: (0, 0, h))
     return pl.pallas_call(
         partial(attend_back_grad_kernel, images=images, blocks=blocks),
         out_shape=(
             jax.ShapeDtypeStruct((images * count, pairs * 384), BF),
-            jax.ShapeDtypeStruct((width // 2, pairs * 384), BF),
-            jax.ShapeDtypeStruct((width // 2, pairs * 384), BF),
+            jax.ShapeDtypeStruct((*held, pairs * 384), BF),
+            jax.ShapeDtypeStruct((*held, pairs * 384), BF),
         ),
         grid=(pairs, images),
         in_specs=[
@@ -511,11 +576,26 @@
 
 
 def head_kernel(
-    xsum_ref, asum_ref, sums_a_ref, down_ref, head_ref, label_ref, alive_ref, once_ref, whole_ref,
-    total_ref, loss_ref, rows_ref, dx2_ref, dact_ref, *, classes, own
+    image_ref, xsum_ref, asum_ref, sums_a_ref, down_ref, head_ref, whole_ref, total_ref,
+    loss_ref, rows_ref, dx2_ref, dact_ref, *, classes, own, slots
 ):
     width, hidden = down_ref.shape
-    fill = loss_ref.shape[0] - own - 1
+    fill = rows_ref.shape[0] - own - 1
+    place_y = image_ref[2 * slots + 2]
+
+    def column(values):
+        row = lax.broadcasted_iota(jnp.int32, (own + 1 + fill, 1), 0)
+        out = jnp.zeros_like(row)
+        for index, value in enumerate(values):
+            out = jnp.where(row == index, value, out)
+        return out
+
+    def of_images(first, last):
+        return column([image_ref[first + place_y * own + i] for i in range(own)] + [image_ref[last]])
+
+    label = of_images(0, 2 * slots)
+    alive = of_images(slots, 2 * slots + 1).astype(F32)
+    once = column([1] * own + [jnp.where(place_y == 0, 1, 0)]).astype(F32)
 
     def stacked(ref, cols):
         rows = [ref[image] for image in range(own)] + [sums_a_ref[:, cols]]
@@ -535,49 +615,49 @@
     logits = jnp.where(place < classes, dot(pooled_low, head, NN), -1e30)
     top = jnp.max(logits, -1, keepdims=True)
     norm_log = top + jnp.log(jnp.sum(jnp.exp(logits - top), -1, keepdims=True))
-    hot = place == label_ref[...]
+    hot = place == label
     true_logit = jnp.sum(jnp.where(hot, logits, 0.0), -1, keepdims=True)
-    loss_ref[...] = jnp.broadcast_to(norm_log - true_logit, loss_ref.shape)
+    loss = (norm_log - true_logit) * alive * once
+    lane = lax.broadcasted_iota(jnp.int32, (1, loss_ref.shape[1]), 1)
+    loss_a, loss_b = loss[own : own + 1], jnp.sum(loss[:own], 0, keepdims=True)
+    loss_ref[...] = jnp.where(lane == 1, loss_a, jnp.where(lane == 2, loss_b, 0.0))
     soft = jnp.exp(logits - norm_log) - hot.astype(F32)
-    d_logits = (soft * alive_ref[...] / total_ref[...]).astype(BF)
+    d_logits = (soft * alive / total_ref[...]).astype(BF)
     d_x2 = dot(d_logits, head, NT) / whole
     d_mix = d_x2.astype(BF)
     d_act = dot(d_mix, down, NN)
     for image in range(own + 1):
         dx2_ref[image] = d_x2[image : image + 1]
         dact_ref[image] = d_act[image : image + 1]
-    once = once_ref[...]
     rows_ref[:, :hidden] = high
     rows_ref[:, hidden : hidden + width] = pooled_low
     rows_ref[:, hidden + width : hidden + 2 * width] = (d_mix * once).astype(BF)
     rows_ref[:, hidden + 2 * width :] = (d_logits * once).astype(BF)
 
 
-def head_step(xsum, asum, sums_a, w_down_head, labels, alive, once, whole, total, classes):
+def head_step(images, xsum, asum, sums_a, w_down_head, whole, total, classes):
     own, _, width = xsum.shape
     hidden = asum.shape[2]
-    rows = labels.shape[0]
+    rows = whole.shape[0]
     padded = w_down_head.shape[1] - hidden
     spec = lambda shape, *place: pl.BlockSpec(shape, lambda i: place or (0,) * len(shape))
     shapes = (
-        ((rows, 128), F32),
+        ((1, 128), F32),
         ((rows, hidden + 2 * width + padded), BF),
         ((own + 1, 1, width), F32),
         ((own + 1, 1, hidden), F32),
     )
     return pl.pallas_call(
-        partial(head_kernel, classes=classes, own=own),
+        partial(head_kernel, classes=classes, own=own, slots=(images.shape[0] - 3) // 2),
         out_shape=tuple(jax.ShapeDtypeStruct(*shape) for shape in shapes),
         grid=(1,),
         in_specs=[
+            pl.BlockSpec(memory_space=pltpu.SMEM),
             spec(xsum.shape),
             spec(asum.shape),
             spec(sums_a.shape),
             spec((width, hidden), 0, 0),
             spec((width, padded), 0, hidden // padded),
-            spec((rows, 1)),
-            spec((rows, 1)),
-            spec((rows, 1)),
             spec((rows, 1)),
             spec((1, 1)),
         ],
@@ -585,7 +665,7 @@
         compiler_params=pltpu.CompilerParams(vmem_limit_bytes=VMEM_BYTES),
         cost_estimate=estimate(1 << 32, 8 << 20),
         name="head",
-    )(xsum, asum, sums_a, w_down_head, w_down_head, labels, alive, once, whole, total)
+    )(images, xsum, asum, sums_a, w_down_head, w_down_head, whole, total)
 
 
 def mlp_back_kernel(*refs, steps):
@@ -744,12 +824,12 @@
         for acc in (acc_b, acc_a, acc_tab):
             cols = slice(at, at + acc.shape[1])
             at += acc.shape[1]
-            store_by_core(core_ref[0], acc, away_ref.at[:, cols], own_ref.at[:, cols], blocks)
+            store_by_core(core_ref[0], acc, away_ref, own_ref, cols, blocks)
 
 
 def embed_back(
     x0_b, dx1_b, tab_b, pixels_b, d_b, x0_a, dx1_a, tab_a, pixels_a, d_a, gain, gain_grad, w_all,
-    core, blocks, images, depths
+    core, blocks, images, depths, count_y
 ):
     rows, width = x0_b.shape
     pieces = len(pixels_b)
@@ -760,7 +840,7 @@
     still = lambda shape: pl.BlockSpec(shape, lambda i: (0,) * len(shape))
     inputs_a = (x0_a, dx1_a, tab_a, pixels_a, *sum(d_a, ()))
     rows_a = x0_a.shape[0]
-    grad = (width // 2, sum(depths) + 128)
+    grad = (count_y * blocks, width // (2 * count_y * blocks), sum(depths) + 128)
     return pl.pallas_call(
         partial(
             embed_back_kernel, steps=steps, groups=len(d_b), pieces=pieces, blocks=blocks,
@@ -794,8 +874,8 @@
 def resize_back_kernel(got_ref, table_b_ref, table_a_ref, sums_ref, sent_ref, small_ref, *, rows, at):
     owners, _, lanes = sent_ref.shape
     total = jnp.zeros(small_ref.shape, F32)
-    for block in range(got_ref.shape[0] // rows):
-        total = total + got_ref[block * rows : (block + 1) * rows].astype(F32)
+    for block in range(got_ref.shape[0]):
+        total = total + got_ref[block].astype(F32)
     small_ref[...] = total
     parts, square = [], 0.0
     for channel in range(3):
@@ -829,7 +909,7 @@
 
 
 def resize_back(got, tables, sums, rows, at, owners, lanes):
-    cols = got.shape[1]
+    cols = got.shape[2]
     return pl.pallas_call(
         partial(resize_back_kernel, rows=rows, at=at),
         out_shape=(
@@ -956,27 +1036,28 @@
     )
     sent = after(sent, *slices)
     got = lax.all_to_all(sent, AXES, split_axis=0, concat_axis=0, tiled=True)
-    got, tab_a, tab_b, *parts_b = lax.optimization_barrier(
-        (got, tab_a, jnp.concatenate(tabs_b, 0), *parts_b)
-    )
+    def group_cols(array, group):
+        shaped = array.reshape(rows_own, 3, groups, pairs, 128)[:, :, group]
+        return shaped.transpose(0, 2, 1, 3).reshape(rows_own, 3 * span)
+
+    qkv_low = qkv_w.astype(BF)
+    held = jnp.concatenate(stage(group_cols(qkv_low, 0)[None], STAGES[0]), 0)
+    held = jnp.concatenate(stage(held, STAGES[1]), 0)
+    packed = jnp.concatenate(
+        [group_cols(qkv_low, group) for group in range(groups)]
+        + [out_w.astype(BF), mlp_w[0].astype(BF)],
+        1,
+    )
+    got, held, packed, tab_a, tab_b, *parts_b = lax.optimization_barrier(
+        (got, held, packed, tab_a, jnp.concatenate(tabs_b, 0), *parts_b)
+    )
+    held = stage(held, STAGES[2])
     got = got.reshape(count_all, rows_own, lanes)
     counts = got[:, 0, rows_kern : rows_kern + 2]
     got = got.astype(F32)
     kern_cols = got[:, :, :rows_kern].transpose(1, 0, 2).reshape(rows_own, 3, BASE * BASE)
 
-    def group_cols(array, group):
-        shaped = array.reshape(rows_own, 3, groups, pairs, 128)[:, :, group]
-        return shaped.transpose(0, 2, 1, 3).reshape(rows_own, 3 * span)
-
-    qkv_low = qkv_w.astype(BF)
-    w_all = lax.all_gather(
-        jnp.concatenate(
-            [group_cols(qkv_low, group) for group in range(groups)]
-            + [out_w.astype(BF), mlp_w[0].astype(BF)],
-            1,
-        ),
-        AXES, axis=0, tiled=True,
-    )
+    w_all = lax.all_gather(packed, AXES, axis=0, tiled=True)
 
     tables = [resize_table(PATCH_B), resize_table(PATCH_A)]
     sizes = [3 * table.shape[0] for table in tables]
@@ -995,7 +1076,8 @@
         + [pos_t, pos_t, edge, gains.astype(BF).T],
         1,
     )
-    w_small = gather_rows(small)
+    w_small, held = gather_rows(small, held)
+    held = jnp.concatenate(held, 0)
     w_down_head = lax.all_gather(
         after(
             jnp.concatenate([mlp_w[1].astype(BF), padded_cols(head_w.astype(BF), classes_up)], 1),
@@ -1009,6 +1091,8 @@
     flat_a = pixels_a.reshape(span_a, depth_a)
     block = min(512, whole_b)
     x0_a, h1_a = embed([flat_a], tab_a, w_small, depths[0], spot, gain1, 1)
+    h1_a, *held = lax.optimization_barrier((h1_a, *stage(held, STAGES[3])))
+    w_first = place_blocks(held, stage_owners())
     h1_all = jnp.concatenate([h1_a] + [shift(h1_a, "y", step) for step in range(1, seq)], 0)
     x0_b, h1_b = embed(
         [after(parts_b[0], h1_a), *parts_b[1:]], tab_b, w_small, 0, spot, gain1, own_b
@@ -1018,7 +1102,10 @@
     ready = h1_b
     for group in range(groups):
         outs_b.append(
-            attend_pairs(after(h1_b, ready), w_all, group * pairs, pairs, own_b, whole_b)
+            attend_pairs(
+                after(h1_b, ready), *((w_all, group * pairs) if group else (w_first, 0)),
+                pairs, own_b, whole_b,
+            )
         )
         ready = outs_b[-1][0]
     for group in range(groups):
@@ -1031,30 +1118,15 @@
     sums_a = sum([shift(sums_a, "y", step) for step in range(1, seq)], sums_a)
     x1_b, slope_b, xsum_b, asum_b = mlp(after(x0_b, x1_a), mixed_b, w_all, hidden, gain2, own_b, block)
 
-    counts, labels_a, labels_b, live_b, alive_a = lax.optimization_barrier(
-        (counts, labels_a, labels_b, live_b, alive_a, h1_b)
-    )[:5]
+    images = jnp.concatenate([labels_b, live_b, labels_a, live_a, row.reshape(1).astype(jnp.int32)])
+    images, counts, h1_b = lax.optimization_barrier((images, counts, h1_b))
     count = jnp.sum(counts.astype(F32), 0, keepdims=True)
     total = jnp.maximum(jnp.sum(count), 1.0)
     rows_up = round_up(own_b + 1, 8)
-    fill = rows_up - own_b - 1
-    stack = lambda first, last: jnp.pad(
-        jnp.concatenate([first, last], 0), ((0, fill), (0, 0))
-    )
-    mine = lambda array: lax.dynamic_slice_in_dim(array, row * own_b, own_b, 0)[:, None]
-    labels = stack(mine(labels_b), labels_a[:, None])
-    alive_b = mine(live_b).astype(F32)
-    alive = stack(alive_b, alive_a)
-    once = stack(jnp.ones((own_b, 1), F32), lead.reshape(1, 1))
     whole = np.ones((rows_up, 1), np.float32)
     whole[:own_b], whole[own_b] = whole_b, whole_a
-    losses, rows_out, d_x2, d_act = head_step(
-        xsum_b, asum_b, sums_a, w_down_head, labels, alive, once, jnp.asarray(whole),
-        total.reshape(1, 1), classes,
-    )
-    loss_sums = jnp.stack(
-        [lead * jnp.sum(alive_a * losses[own_b : own_b + 1, :1]),
-         jnp.sum(alive_b * losses[:own_b, :1])]
+    loss_sums, rows_out, d_x2, d_act = head_step(
+        images, xsum_b, asum_b, sums_a, w_down_head, jnp.asarray(whole), total.reshape(1, 1), classes
     )
 
     image_rows = lax.all_gather(rows_out, AXES, axis=0, tiled=True)
@@ -1089,7 +1161,7 @@
             qkvs_b[group],
             after(d_mixed_b[group], ready),
             mixed_b[group], outs_b[group][2],
-            h1_b, h1_all, d_alls[group], core, pairs, own_b, whole_b, blocks,
+            h1_b, h1_all, d_alls[group], core, pairs, own_b, whole_b, blocks, seq,
         )
         if group:
             away, own, own_groups[-1] = lax.optimization_barrier((away, own, own_groups[-1]))
@@ -1106,12 +1178,12 @@
     away, own = embed_back(
         x0_b, after(d_x1_b, ready), tab_b, parts_b, d_groups_b,
         x0_a, d_x1_a, tab_a, flat_a, d_groups_a,
-        gain1, grad_gain2, w_all, core, blocks, own_b, depths,
+        gain1, grad_gain2, w_all, core, blocks, own_b, depths, seq,
     )
     away, own, own_up_out, *own_groups = lax.optimization_barrier(
         (away, own, own_up_out, *own_groups)
     )
-    own_qkv = jnp.stack([block_sum(got, rows_own) for got in own_groups], 1)
+    own_qkv = jnp.stack([block_sum(got) for got in own_groups], 1)
     own_qkv = own_qkv.reshape(rows_own, groups * pairs, 3, 128)
     own_qkv = own_qkv.transpose(0, 2, 1, 3).reshape(rows_own, 3 * width)
     small_parts = scatter_rows(away, own)
@@ -1132,7 +1204,7 @@
     square_sum = sum(
         jnp.sum(piece * piece) for piece in (own_up_out, own_down, own_head, own_qkv)
     )
-    sums = padded_cols(jnp.concatenate([square_sum.reshape(1), loss_sums])[None], lanes)
+    sums = loss_sums + padded_cols(square_sum.reshape(1, 1), lanes)
     sent, own_small = resize_back(
         small_parts, [jnp.asarray(table) for table in tables], sums, rows_own, depths[0],
         count_all, lanes,

time: 497 us -> 494 us (level)
  blocking collectives: 35.9 us -> 0 us
  starting transfers between devices: 38.4 us -> 52.9 us
  local copies, waits for them, and re-layouts: 21.3 us -> 27.9 us
  waiting for transfers between devices: 55.4 us -> 61.7 us
    all_to_all x1 -> x0, blocking collectives: 35.9 us -> none  [gather_rows(): lax.all_to_all(copies, CHIPS, split_axis=0, concat_axis=0, tiled=True)]
    ppermute x9 -> x15, waiting for transfers between devices: 14.5 us -> 36.6 us  [shift(): return lax.ppermute(value, axis, pairs)]
    all_to_all x2, waiting for transfers between devices: 22.7 us -> 10.4 us  [fast_step(): got = lax.all_to_all(sent, AXES, split_axis=0, concat_axis=0, tiled=True)]
    all_gather x1, waiting for transfers between devices: 10.2 us -> 1.15 us  [fast_step(): w_all = lax.all_gather(packed, AXES, axis=0, tiled=True)]
    ppermute x9 -> x15, starting transfers between devices: 7.35 us -> 15.7 us  [shift(): return lax.ppermute(value, axis, pairs)]
    all_to_all x0 -> x1, starting transfers between devices: none -> 5.17 us  [gather_rows(): lax.all_to_all(copies, CHIPS, split_axis=0, concat_axis=0, tiled=True)]
    pallas_call x1 -> x2, Pallas kernels: 7.24 us -> 10.9 us  [the longest x1 7.21 us: head_step(): pl.pallas_call(partial(head_kernel, classes=classes, own=own, slots=(imag...]
  transfers between devices with their start and end apart: 18 -> 25, of which waited for: 9 -> 12; matrix products, arithmetic and copies ran while one was open for 8% -> 10% of each run, Pallas kernels for 56% -> 57%
where the time goes in v4:
time: 494 us; the launch traced here: 489 us
  Pallas kernels  297 us (60%)
  waiting for transfers between devices  61.7 us (12%)
  starting transfers between devices  52.9 us (11%)
  local copies, waits for them, and re-layouts  27.9 us (6%)
  other arithmetic  21.6 us (4%)
  between operations  19.9 us (4%)
  matrix products  7.56 us (2%)
    pallas_call x2, Pallas kernels, attend_back_grad(): pl.pallas_call(partial(attend_back_grad_kernel, images=images, blocks=blo...  86.1 us
    pallas_call x4, Pallas kernels, attend_pairs(): pl.pallas_call(partial(attend_kernel, items=items, n_query=n_query), out_...  63.1 us
    pallas_call x1, Pallas kernels, mlp_back(): pl.pallas_call(partial(mlp_back_kernel, steps=steps), out_shape=(*outs, j...  42.1 us
    ppermute x15, waiting for transfers between devices, shift(): return lax.ppermute(value, axis, pairs)  36.6 us
    pallas_call x2, Pallas kernels, mlp(): pl.pallas_call(partial(mlp_kernel, per=per), out_shape=(jax.ShapeDtypeStr...  36.1 us
    pallas_call x1, Pallas kernels, embed_back(): pl.pallas_call(partial(embed_back_kernel, steps=steps, groups=len(d_b), p...  24.6 us
    all_to_all x3, starting transfers between devices, scatter_rows(): return lax.all_to_all(both, CHIPS, split_axis=0, concat_axis=0, tiled=True)  18.1 us
    ppermute x15, starting transfers between devices, shift(): return lax.ppermute(value, axis, pairs)  15.7 us
  transfers between devices with their start and end apart: 25, of which 12 were waited for; matrix products, arithmetic and copies ran while one was open for 10% of the time, Pallas kernels for 57%

profile of v4, /device:TPU:1, one launch (start us, length us, event | category | flops | bytes accessed | tf_op | source)
XLA Modules:
  0.0 488.6 jit_solution(3264961830176538565)
XLA Ops:
  9.0 4.2 collective-permute-start.2
  17.5 2.7 constant_dynamic-slice_fusion.3
  21.0 6.3 %all-to-all-start = ((bf16[32,24,128]{2,1,0:T(8,128)(2,1)}), bf16[32,24,128]{2,1,0:T(8,128)(2,1)S(1)}, u32[]{:S(2)}, u32[]{:S(2)}) async-start(bf16[32,24,128]{2,1,0:T(8,128)(2,1)} %bitcast.7), calls=%async_computation | async-start | bytes 393216 | tf_op jit(solution)/shard_map/all_to_all | solution.py:1038
  27.9 1.5 collective-permute-start.4
  29.4 1.4 constant_dynamic-update-slice_fusion.4
  32.5 1.5 pad_maximum_fusion.2
  34.0 1.6 constant_dynamic-slice_fusion.2.refs_1_.refs_9_
  40.3 2.7 collective-permute-done.3
  43.0 8.1 %collective-permute-done.4 = bf16[1024,432]{0,1:T(8,128)(2,1)S(1)} collective-permute-done((bf16[1024,432]{0,1:T(8,128)(2,1)S(1)}, bf16[1024,432]{0,1:T(8,128)(2,1)S(1)}, u32[]{:S(2)}, u32[]{:S(2)}) %collective-permute-start.4) | collective-permute-done | bytes 884768 | tf_op jit(solution)/shard_map/ppermute | solution.py:126
  52.4 1.4 convolution_convert_fusion.1
  55.7 5.2 %all-to-all-start.1 = ((bf16[16,24,1024]{2,1,0:T(8,128)(2,1)}), bf16[16,24,1024]{2,1,0:T(8,128)(2,1)S(1)}, u32[]{:S(2)}, u32[]{:S(2)}) async-start(bf16[16,24,1024]{2,1,0:T(8,128)(2,1)} %broadcast_in_dim.25), calls=%async_computation.1 | async-start | bytes 1572864 | tf_op jit(solution)/shard_map/all_to_all | solution.py:138
  60.9 1.4 collective-permute-start.5
  62.4 17.9 %collective-permute-done.5 = bf16[8,24,1152]{2,1,0:T(8,128)(2,1)} collective-permute-done((bf16[8,24,1152]{2,1,0:T(8,128)(2,1)S(1)}, bf16[8,24,1152]{2,1,0:T(8,128)(2,1)}, u32[]{:S(2)}, u32[]{:S(2)}) %collective-permute-start.5) | collective-permute-done | bytes 442400 | tf_op jit(solution)/shard_map/ppermute | solution.py:126
  80.2 4.8 all-to-all-done.1
  85.0 1.5 collective-permute-start.6
  93.2 3.2 embed.2
  99.5 3.6 place_blocks.1
  103.2 8.8 %embed.3 = (f32[2048,768]{1,0:T(8,128)}, bf16[2048,768]{1,0:T(8,128)(2,1)}) custom-call(bf16[1024,432]{1,0:T(8,128)(2,1)} %bitcast.59, bf16[1024,432]{1,0:T(8,128)(2,1)} %copy.126.refs_1_.refs_4_, bf16[1024,128]{1,0:T(8,128)(2,1)} %pad_maximum_fusion.3.refs_2_, bf16[768,1024]{1,0:T(8,128)(2,1)} %bitcast.58, f32[1,768]{1,0:T(1,128)} %get-tuple-element.258.refs_3_.refs_4_.refs_15_), custom_call_target="tpu_custom_call" | custom-call | flops 2415919104 | bytes 12582912 | tf_op jit(solution)/shard_map/embed/pallas_call | solution.py:293
  112.9 24.9 %attend.4 = (bf16[2048,1152]{1,0:T(8,128)(2,1)}, bf16[2048,384]{1,0:T(8,128)(2,1)}, f32[2,3,2,1024]{3,2,1,0:T(2,128)}) custom-call(bf16[2048,768]{1,0:T(8,128)(2,1)} %get-tuple-element.185.h1_ref, bf16[768,1152]{1,0:T(8,128)(2,1)} %bitcast.67), custom_call_target="tpu_custom_call" | custom-call | flops 18723373056 | bytes 12582912 | tf_op jit(solution)/shard_map/attend/pallas_call | solution.py:369
  140.3 25.1 %attend.5 = (bf16[2048,1152]{1,0:T(8,128)(2,1)}, bf16[2048,384]{1,0:T(8,128)(2,1)}, f32[2,3,2,1024]{3,2,1,0:T(2,128)}) custom-call(bf16[2048,768]{1,0:T(8,128)(2,1)} %get-tuple-element.185.h1_ref, bf16[768,6144]{1,0:T(8,128)(2,1)} %all-gather.4.cloned.1.call-done.weight_ref.wout_ref.wup_ref.refs_12_.refs_14_.refs_17_.refs_18_), custom_call_target="tpu_custom_call" | custom-call | flops 18723373056 | bytes 12582912 | tf_op jit(solution)/shard_map/attend/pallas_call | solution.py:369
  165.3 6.4 %attend.7 = (bf16[576,1152]{1,0:T(8,128)(2,1)}, bf16[288,384]{1,0:T(8,128)(2,1)}, f32[1,3,2,288]{3,2,1,0:T(2,128)}) custom-call(bf16[576,768]{1,0:T(8,128)(2,1)} %pad_maximum_fusion.1.h1_ref.h1_a_ref, bf16[768,6144]{1,0:T(8,128)(2,1)} %all-gather.4.cloned.1.call-done.weight_ref.wout_ref.wup_ref.refs_12_.refs_14_.refs_17_.refs_18_), custom_call_target="tpu_custom_call" | custom-call | flops 2213609472 | bytes 3538944 | tf_op jit(solution)/shard_map/attend/pallas_call | solution.py:369
  171.7 6.8 %attend.6 = (bf16[576,1152]{1,0:T(8,128)(2,1)}, bf16[288,384]{1,0:T(8,128)(2,1)}, f32[1,3,2,288]{3,2,1,0:T(2,128)}) custom-call(bf16[576,768]{1,0:T(8,128)(2,1)} %pad_maximum_fusion.1.h1_ref.h1_a_ref, bf16[768,6144]{1,0:T(8,128)(2,1)} %all-gather.4.cloned.1.call-done.weight_ref.wout_ref.wup_ref.refs_12_.refs_14_.refs_17_.refs_18_), custom_call_target="tpu_custom_call" | custom-call | flops 2213609472 | bytes 3538944 | tf_op jit(solution)/shard_map/attend/pallas_call | solution.py:369
  178.5 7.8 %mlp.2 = (f32[288,768]{1,0:T(8,128)}, bf16[288,3072]{1,0:T(8,128)(2,1)}, f32[1,1,768]{2,1,0:T(1,128)}, f32[1,1,3072]{2,1,0:T(1,128)}) custom-call(f32[288,768]{1,0:T(8,128)} %get-tuple-element.147.x0_ref.refs_7_, bf16[288,384]{1,0:T(8,128)(2,1)} %get-tuple-element.159.mixed0_ref.refs_10_.o_ref, ...), custom_call_target="tpu_custom_call" | custom-call | flops 106168320 | bytes 110592 | tf_op jit(solution)/shard_map/mlp/pallas_call | solution.py:549
  187.7 28.4 %mlp.3 = (f32[2048,768]{1,0:T(8,128)}, bf16[2048,3072]{1,0:T(8,128)(2,1)}, f32[2,1,768]{2,1,0:T(1,128)}, f32[2,1,3072]{2,1,0:T(1,128)}) custom-call(f32[2048,768]{1,0:T(8,128)} %get-tuple-element.162.x0_ref.refs_0_, bf16[2048,384]{1,0:T(8,128)(2,1)} %get-tuple-element.163.mixed0_ref.refs_4_.o_ref, ...), custom_call_target="tpu_custom_call" | custom-call | flops 754974720 | bytes 786432 | tf_op jit(solution)/shard_map/mlp/pallas_call | solution.py:549
  216.8 7.2 %head.1 = (f32[1,128]{1,0:T(1,128)}, bf16[8,5632]{1,0:T(8,128)(2,1)}, f32[3,1,768]{2,1,0:T(1,128)}, f32[3,1,3072]{2,1,0:T(1,128)}) custom-call(s32[11]{0:T(128)} %concatenate.51.image_ref, f32[2,1,768]{2,1,0:T(1,128)} %get-tuple-element.167.xsum_ref, f32[2,1,3072]{2,1,0:T(1,128)} %get-tuple-element.168.asum_ref, f32[1,3840]{1,0:T(1,128)} %fusion.22.sums_a_ref, ...), custom_call_target="tpu_custom_call" | custom-call | flops 134217728 | bytes 262144 | tf_op jit(solution)/shard_map/head/pallas_call | solution.py:650
  224.1 42.1 %mlp_back.1 = (f32[2048,768]{1,0:T(8,128)}, bf16[2048,384]{1,0:T(8,128)(2,1)}, bf16[2048,384]{1,0:T(8,128)(2,1)}, f32[288,768]{1,0:T(8,128)}, bf16[288,384]{1,0:...) custom-call(bf16[2048,3072]{1,0:T(8,128)(2,1)} %get-tuple-element.165.refs_0_, ...), custom_call_target="tpu_custom_call" | custom-call | flops 861143040 | bytes 897024 | tf_op jit(solution)/shard_map/mlp_back/pallas_call | solution.py:742
  266.2 6.6 %attend_back_apart.3.d_a_ref.refs_11_ = bf16[576,1152]{1,0:T(8,128)(2,1)} custom-call(bf16[576,1152]{1,0:T(8,128)(2,1)} %get-tuple-element.186.q_ref.kv_ref, bf16[576,1152]{1,0:T(8,128)(2,1)} %get-tuple-element.186.q_ref.kv_ref, bf16[288,384]{1,0:T(8,128)(2,1)} %get-tuple-element.187.do_ref, bf16[288,384]{1,0:T(8,128)(2,1)} %get-tuple-element.159.mixed0_ref.refs_10_.o_ref, ...), custom_call_target="tpu_custom_call" | custom-call | flops 74649600 | bytes 82944 | tf_op jit(solution)/shard_map/attend_back_apart/pallas_call | solution.py:435
  272.8 6.4 %attend_back_apart.2.d_a_ref.refs_13_ = bf16[576,1152]{1,0:T(8,128)(2,1)} custom-call(bf16[576,1152]{1,0:T(8,128)(2,1)} %get-tuple-element.180.q_ref.kv_ref, bf16[576,1152]{1,0:T(8,128)(2,1)} %get-tuple-element.180.q_ref.kv_ref, bf16[288,384]{1,0:T(8,128)(2,1)} %get-tuple-element.181.do_ref, bf16[288,384]{1,0:T(8,128)(2,1)} %get-tuple-element.160.mixed1_ref.refs_11_.o_ref, ...), custom_call_target="tpu_custom_call" | custom-call | flops 74649600 | bytes 82944 | tf_op jit(solution)/shard_map/attend_back_apart/pallas_call | solution.py:435
  279.1 3.9 all-gather.8.cloned.1.call-done
  287.2 43.0 %attend_back.2 = (bf16[2048,1152]{1,0:T(8,128)(2,1)}, bf16[16,24,1152]{2,1,0:T(8,128)(2,1)}, bf16[16,24,1152]{2,1,0:T(8,128)(2,1)}) custom-call(s32[1]{0:T(128)} %bitcast.core_ref, bf16[2048,1152]{1,0:T(8,128)(2,1)} %get-tuple-element.154.qkv_ref, bf16[2048,384]{1,0:T(8,128)(2,1)} %get-tuple-element.183.do_ref, ...), custom_call_target="tpu_custom_call" | custom-call | flops 1101004800 | bytes 393216 | tf_op jit(solution)/shard_map/attend_back/pallas_call | solution.py:484
  331.2 2.3 collective-permute-done.12
  333.4 2.4 add_convert_fusion.1
  335.8 4.4 all-to-all-start.2
  340.2 43.1 %attend_back.3 = (bf16[2048,1152]{1,0:T(8,128)(2,1)}, bf16[16,24,1152]{2,1,0:T(8,128)(2,1)}, bf16[16,24,1152]{2,1,0:T(8,128)(2,1)}) custom-call(s32[1]{0:T(128)} %bitcast.core_ref, bf16[2048,1152]{1,0:T(8,128)(2,1)} %get-tuple-element.157.qkv_ref, bf16[2048,384]{1,0:T(8,128)(2,1)} %get-tuple-element.190.do_ref, ...), custom_call_target="tpu_custom_call" | custom-call | flops 1101004800 | bytes 393216 | tf_op jit(solution)/shard_map/attend_back/pallas_call | solution.py:484
  384.0 2.3 collective-permute-done.13
  386.3 2.3 add_convert_fusion
  388.6 6.9 %all-to-all-start.3 = ((bf16[16,24,1152]{2,1,0:T(8,128)(2,1)}), bf16[16,24,1152]{2,1,0:T(8,128)(2,1)S(1)}, u32[]{:S(2)}, u32[]{:S(2)}) async-start(bf16[16,24,1152]{2,1,0:T(8,128)(2,1)} %add_convert_fusion), calls=%async_computation.4 | async-start | bytes 1769472 | tf_op jit(solution)/shard_map/all_to_all | solution.py:207
  395.5 24.6 %embed_back.1 = (bf16[16,24,1024]{2,1,0:T(8,128)(2,1)}, bf16[16,24,1024]{2,1,0:T(8,128)(2,1)}) custom-call(s32[1]{0:T(128)} %bitcast.core_ref, f32[2048,768]{1,0:T(8,128)} %get-tuple-element.162.x0_ref.refs_0_, f32[2048,768]{1,0:T(8,128)} %get-tuple-element.193.refs_1_, bf16[1024,128]{1,0:T(8,128)(2,1)} %pad_maximum_fusion.3.refs_2_, ...), custom_call_target="tpu_custom_call" | custom-call | flops 289406976 | bytes 640000 | tf_op jit(solution)/shard_map/embed_back/pallas_call | solution.py:844
  422.0 2.1 collective-permute-done.14
  424.1 2.4 add_convert_fusion.2
  426.5 6.8 %all-to-all-start.4 = ((bf16[16,24,1024]{2,1,0:T(8,128)(2,1)}), bf16[16,24,1024]{2,1,0:T(8,128)(2,1)S(1)}, u32[]{:S(2)}, u32[]{:S(2)}) async-start(bf16[16,24,1024]{2,1,0:T(8,128)(2,1)} %add_convert_fusion.2), calls=%async_computation.5 | async-start | bytes 1572864 | tf_op jit(solution)/shard_map/all_to_all | solution.py:207
  434.5 2.6 multiply_reduce_fusion.3
  437.0 3.1 multiply_reduce_fusion.2
  445.6 4.7 all-to-all-done.4.got_ref
  451.3 3.9 resize_back.1
  455.1 7.3 %all-to-all-start.5 = ((f32[32,24,128]{2,1,0:T(8,128)}), f32[32,24,128]{2,1,0:T(8,128)S(1)}, u32[]{:S(2)}, u32[]{:S(2)}) async-start(f32[32,24,128]{2,1,0:T(8,128)} %get-tuple-element.218), calls=%async_computation.6 | async-start | bytes 786432 | tf_op jit(solution)/shard_map/all_to_all | solution.py:1212
  465.2 10.4 %all-to-all-done.5.got_ref = f32[32,24,128]{2,1,0:T(8,128)S(1)} async-done(((f32[32,24,128]{2,1,0:T(8,128)}), f32[32,24,128]{2,1,0:T(8,128)S(1)}, u32[]{:S(2)}, u32[]{:S(2)}) %all-to-all-start.5) | async-done | bytes 393248 | tf_op jit(solution)/shard_map/all_to_all | solution.py:1212
  476.4 5.5 %update.1 = (f32[24,2304]{1,0:T(8,128)}, f32[24,768]{1,0:T(8,128)}, f32[2,24,3072]{2,1,0:T(8,128)}, f32[96,768]{1,0:T(8,128)}, f32[24,49]{1,0:T(8,128)}, /*index...) custom-call(f32[32,24,128]{2,1,0:T(8,128)} %copy-done.6, ...), custom_call_target="tpu_custom_call" | custom-call | flops 8388608 | bytes 524288 | tf_op jit(solution)/shard_map/update/pallas_call | solution.py:964
  (170 shorter events, 45.6 us)
Async XLA Ops:
  9.0 26.6 %collective-permute-start.2 = (bf16[1,24,1152]{2,1,0:T(8,128)(2,1)}, bf16[1,24,1152]{2,1,0:T(8,128)(2,1)}, u32[]{:S(2)}, u32[]{:S(2)}) collective-permute-start(bf16[1,24,1152]{2,1,0:T(8,128)(2,1)} %broadcast_in_dim_reshape.3), channel_id=1, source_target_pairs={{0,24},{8,0},{16,8},{24,16},{1,25},{9,1},{17,9},{25,17},{2,26},{10... | collective-permute-start | bytes 165896 | tf_op jit(solution)/shard_map/ppermute | solution.py:126
  13.1 22.5 %collective-permute-start.1 = (bf16[1,24,1152]{2,1,0:T(8,128)(2,1)}, bf16[1,24,1152]{2,1,0:T(8,128)(2,1)}, u32[]{:S(2)}, u32[]{:S(2)}) collective-permute-start(bf16[1,24,1152]{2,1,0:T(8,128)(2,1)} %broadcast_in_dim_reshape.3), channel_id=1, source_target_pairs={{0,16},{8,24},{16,0},{24,8},{1,17},{9,25},{17,1},{25,9},{2,18},{10... | collective-permute-start | bytes 165896 | tf_op jit(solution)/shard_map/ppermute | solution.py:126
  13.1 22.5 %collective-permute-start = (bf16[1,24,1152]{2,1,0:T(8,128)(2,1)}, bf16[1,24,1152]{2,1,0:T(8,128)(2,1)}, u32[]{:S(2)}, u32[]{:S(2)}) collective-permute-start(bf16[1,24,1152]{2,1,0:T(8,128)(2,1)} %broadcast_in_dim_reshape.3), channel_id=1, source_target_pairs={{0,8},{8,16},{16,24},{24,0},{1,9},{9,17},{17,25},{25,1},{2,10},{10... | collective-permute-start | bytes 165896 | tf_op jit(solution)/shard_map/ppermute | solution.py:126
  20.2 10.7 %copy-start.16 = (f32[24,768]{1,0:T(8,128)S(1)}, f32[24,768]{1,0:T(8,128)}, u32[]{:S(2)}) copy-start(f32[24,768]{1,0:T(8,128)} %refs_1_.1) | copy-start | bytes 221188
  20.2 11.4 %copy-start.4 = (f32[2,24,3072]{2,1,0:T(8,128)S(1)}, f32[2,24,3072]{2,1,0:T(8,128)}, u32[]{:S(2)}) copy-start(f32[2,24,3072]{2,1,0:T(8,128)} %refs_2_.1) | copy-start | bytes 1769476
  21.0 22.0 %all-to-all-start = ((bf16[32,24,128]{2,1,0:T(8,128)(2,1)}), bf16[32,24,128]{2,1,0:T(8,128)(2,1)S(1)}, u32[]{:S(2)}, u32[]{:S(2)}) async-start(bf16[32,24,128]{2,1,0:T(8,128)(2,1)} %bitcast.7), calls=%async_computation | async-start | bytes 393216 | tf_op jit(solution)/shard_map/all_to_all | solution.py:1038
  27.3 4.4 copy-start.17
  27.3 112.9 %all-gather.4.cloned.1.call-start = ((), (), s32[]{:S(2)}) async-start(), calls=%async_computation.7 | async-start | bytes 9732096 | tf_op jit(solution)/shard_map/all_gather | solution.py:1060
  27.9 23.2 %collective-permute-start.4 = (bf16[1024,432]{0,1:T(8,128)(2,1)S(1)}, bf16[1024,432]{0,1:T(8,128)(2,1)S(1)}, u32[]{:S(2)}, u32[]{:S(2)}) collective-permute-start(bf16[1024,432]{0,1:T(8,128)(2,1)S(1)} %copy.117), channel_id=1, source_target_pairs={{0,1},{1,0},{2,3},{3,2},{4,5},{5,4},{6,7},{7,6},{8,9},{9,8},{10,11... | collective-permute-start | bytes 2654216 | tf_op jit(solution)/shard_map/ppermute | solution.py:126
  31.6 6.2 %copy-start.13 = (bf16[8,24,1152]{2,1,0:T(8,128)(2,1)S(1)}, bf16[8,24,1152]{2,1,0:T(8,128)(2,1)}, u32[]{:S(2)}) copy-start(bf16[8,24,1152]{2,1,0:T(8,128)(2,1)} %constant_dynamic-update-slice_fusion.4) | copy-start | bytes 1327108
  31.7 19.5 %copy-start.21 = (f32[2,24]{1,0:T(2,128)S(1)}, f32[2,24]{1,0:T(2,128)}, u32[]{:S(2)}) copy-start(f32[2,24]{1,0:T(2,128)} %refs_6_.1) | copy-start | bytes 580
  31.7 19.6 %copy-start.18 = (f32[49,24]{0,1:T(8,128)S(1)}, f32[49,24]{0,1:T(8,128)}, u32[]{:S(2)}) copy-start(f32[49,24]{0,1:T(8,128)} %param.46) | copy-start | bytes 14116
  34.0 20.0 %copy-start.12 = (f32[144,1024,1]{1,0,2:T(8,128)S(1)}, f32[144,1024,1]{1,0,2:T(8,128)}, u32[]{:S(2)}) copy-start(f32[144,1024,1]{1,0,2:T(8,128)} %constant.165) | copy-start | bytes 1769476
  36.5 6.4 %collective-permute-start.3 = (bf16[4,24,1152]{2,1,0:T(8,128)(2,1)S(1)}, bf16[4,24,1152]{2,1,0:T(8,128)(2,1)S(1)}, u32[]{:S(2)}, u32[]{:S(2)}) collective-permute-start(bf16[4,24,1152]{2,1,0:T(8,128)(2,1)S(1)} %pad_maximum_fusion.4), channel_id=1, source_target_pairs={{0,4},{4,0},{1,5},{5,1},{2,6},{6,2},{3,7},{7,3},{8,12},{12,8},{9,1... | collective-permute-start | bytes 663560 | tf_op jit(solution)/shard_map/ppermute | solution.py:126
  43.0 12.7 %copy-start.9 = (bf16[32,24,128]{2,1,0:T(8,128)(2,1)}, bf16[32,24,128]{2,1,0:T(8,128)(2,1)S(1)}, u32[]{:S(2)}) copy-start(bf16[32,24,128]{2,1,0:T(8,128)(2,1)S(1)} %all-to-all-done) | copy-start | bytes 589828
  54.0 32.6 %copy-start.15 = (f32[24,1000]{1,0:T(8,128)S(1)}, f32[24,1000]{1,0:T(8,128)}, u32[]{:S(2)}) copy-start(f32[24,1000]{1,0:T(8,128)} %refs_5_.1) | copy-start | bytes 288004
  55.7 29.3 %all-to-all-start.1 = ((bf16[16,24,1024]{2,1,0:T(8,128)(2,1)}), bf16[16,24,1024]{2,1,0:T(8,128)(2,1)S(1)}, u32[]{:S(2)}, u32[]{:S(2)}) async-start(bf16[16,24,1024]{2,1,0:T(8,128)(2,1)} %broadcast_in_dim.25), calls=%async_computation.1 | async-start | bytes 1572864 | tf_op jit(solution)/shard_map/all_to_all | solution.py:138
  60.9 155.9 %all-gather.6.cloned.1.call-start = ((), (), s32[]{:S(2)}) async-start(), calls=%async_computation.8 | async-start | bytes 6488064 | tf_op jit(solution)/shard_map/all_gather | solution.py:1081
  60.9 19.3 %collective-permute-start.5 = (bf16[8,24,1152]{2,1,0:T(8,128)(2,1)S(1)}, bf16[8,24,1152]{2,1,0:T(8,128)(2,1)}, u32[]{:S(2)}, u32[]{:S(2)}) collective-permute-start(bf16[8,24,1152]{2,1,0:T(8,128)(2,1)S(1)} %constant_dynamic-update-slice_fusion), channel_id=1, source_target_pairs={{0,1},{1,0},{2,3},{3,2},{4,5},{5,4},{6,7},{7,6},{8,9},{9,8},{10,11... | collective-permute-start | bytes 1327112 | tf_op jit(solution)/shard_map/ppermute | solution.py:126
  85.0 3.4 collective-permute-start.6
  88.9 4.3 copy-start.2
  88.9 2.8 copy-start.26
  88.9 194.1 %all-gather.8.cloned.1.call-start = ((), (), s32[]{:S(2)}) async-start(), calls=%async_computation.9 | async-start | bytes 2973696 | tf_op jit(solution)/shard_map/all_gather | solution.py:1132
  89.2 7.4 %copy-start.22 = (s32[32]{0:T(128)S(1)}, s32[32]{0:T(128)}, u32[]{:S(2)}) copy-start(s32[32]{0:T(128)} %constant.164) | copy-start | bytes 388
  89.2 7.4 %copy-start.23 = (s32[32]{0:T(128)S(1)}, s32[32]{0:T(128)}, u32[]{:S(2)}) copy-start(s32[32]{0:T(128)} %constant.163) | copy-start | bytes 388
  89.3 7.4 %copy-start.24 = (s32[32]{0:T(128)S(1)}, s32[32]{0:T(128)}, u32[]{:S(2)}) copy-start(s32[32]{0:T(128)} %constant.162) | copy-start | bytes 388
  89.3 7.4 %copy-start.25 = (s32[32]{0:T(128)S(1)}, s32[32]{0:T(128)}, u32[]{:S(2)}) copy-start(s32[32]{0:T(128)} %constant.161) | copy-start | bytes 388
  90.6 8.9 %copy-start.5 = (bf16[16,24,1152]{2,1,0:T(8,128)(2,1)}, bf16[16,24,1152]{2,1,0:T(8,128)(2,1)S(1)}, u32[]{:S(2)}) copy-start(bf16[16,24,1152]{2,1,0:T(8,128)(2,1)S(1)} %constant_dynamic-update-slice_fusion.5.refs_0_) | copy-start | bytes 2654212
  90.6 5.8 %collective-permute-start.7 = (bf16[16,24,1152]{2,1,0:T(8,128)(2,1)S(1)}, bf16[16,24,1152]{2,1,0:T(8,128)(2,1)}, u32[]{:S(2)}, u32[]{:S(2)}) collective-permute-start(bf16[16,24,1152]{2,1,0:T(8,128)(2,1)S(1)} %constant_dynamic-update-slice_fusion.5.refs_0_), channel_id=1, source_target_pairs={{0,2},{2,0},{1,3},{3,1},{4,6},{6,4},{5,7},{7,5},{8,10},{10,8},{9,1... | collective-permute-start | bytes 2654216 | tf_op jit(solution)/shard_map/ppermute | solution.py:126
  92.6 5.6 %copy-start.8 = (bf16[1024,432]{0,1:T(8,128)(2,1)S(1)}, bf16[1024,432]{0,1:T(8,128)(2,1)}, u32[]{:S(2)}) copy-start(bf16[1024,432]{0,1:T(8,128)(2,1)} %copy-done.7) | copy-start | bytes 2654212
  96.3 15.6 %collective-permute-start.8 = (bf16[288,768]{1,0:T(8,128)(2,1)}, bf16[288,768]{1,0:T(8,128)(2,1)S(1)}, u32[]{:S(2)}, u32[]{:S(2)}) collective-permute-start(bf16[288,768]{1,0:T(8,128)(2,1)} %get-tuple-element.142), channel_id=1, source_target_pairs={{0,1},{1,0},{2,3},{3,2},{4,5},{5,4},{6,7},{7,6},{8,9},{9,8},{10,11... | collective-permute-start | bytes 1327112 | tf_op jit(solution)/shard_map/ppermute | solution.py:126
  103.1 8.8 %copy-start.14 = (bf16[288,768]{1,0:T(8,128)(2,1)S(1)}, bf16[288,768]{1,0:T(8,128)(2,1)}, u32[]{:S(2)}) copy-start(bf16[288,768]{1,0:T(8,128)(2,1)} %get-tuple-element.142) | copy-start | bytes 1327108
  186.9 29.2 %collective-permute-start.9 = (f32[1,3840]{1,0:T(1,128)S(1)}, f32[1,3840]{1,0:T(1,128)S(1)}, u32[]{:S(2)}, u32[]{:S(2)}) collective-permute-start(f32[1,3840]{1,0:T(1,128)S(1)} %pad_maximum_fusion.6), channel_id=1, source_target_pairs={{0,1},{1,0},{2,3},{3,2},{4,5},{5,4},{6,7},{7,6},{8,9},{9,8},{10,11... | collective-permute-start | bytes 46088 | tf_op jit(solution)/shard_map/ppermute | solution.py:126
  187.7 28.4 %copy-start.19 = (f32[1,1,3072]{2,1,0:T(1,128)S(1)}, f32[1,1,3072]{2,1,0:T(1,128)}, u32[]{:S(2)}) copy-start(f32[1,1,3072]{2,1,0:T(1,128)} %get-tuple-element.170) | copy-start | bytes 36868
  187.7 28.4 %copy-start.20 = (f32[1,1,768]{2,1,0:T(1,128)S(1)}, f32[1,1,768]{2,1,0:T(1,128)}, u32[]{:S(2)}) copy-start(f32[1,1,768]{2,1,0:T(1,128)} %get-tuple-element.169) | copy-start | bytes 9220
  224.0 196.2 %reduce-scatter.2.cloned.1.call-start = ((), (), s32[]{:S(2)}) async-start(), calls=%async_computation.10 | async-start | bytes 6082560 | tf_op jit(solution)/shard_map/reduce_scatter | solution.py:1152
  285.7 44.5 %collective-permute-start.10 = (bf16[288,1152]{1,0:T(8,128)(2,1)S(1)}, bf16[288,1152]{1,0:T(8,128)(2,1)S(1)}, u32[]{:S(2)}, u32[]{:S(2)}) collective-permute-start(bf16[288,1152]{1,0:T(8,128)(2,1)S(1)} %slice.80), channel_id=1, source_target_pairs={{0,1},{1,0},{2,3},{3,2},{4,5},{5,4},{6,7},{7,6},{8,9},{9,8},{10,11... | collective-permute-start | bytes 1990664 | tf_op jit(solution)/shard_map/ppermute | solution.py:126
  287.0 43.3 %collective-permute-start.11 = (bf16[288,1152]{1,0:T(8,128)(2,1)S(1)}, bf16[288,1152]{1,0:T(8,128)(2,1)S(1)}, u32[]{:S(2)}, u32[]{:S(2)}) collective-permute-start(bf16[288,1152]{1,0:T(8,128)(2,1)S(1)} %slice.81), channel_id=1, source_target_pairs={{0,1},{1,0},{2,3},{3,2},{4,5},{5,4},{6,7},{7,6},{8,9},{9,8},{10,11... | collective-permute-start | bytes 1990664 | tf_op jit(solution)/shard_map/ppermute | solution.py:126
  330.3 5.5 %copy-start.10 = (bf16[288,1152]{1,0:T(8,128)(2,1)}, bf16[288,1152]{1,0:T(8,128)(2,1)S(1)}, u32[]{:S(2)}) copy-start(bf16[288,1152]{1,0:T(8,128)(2,1)S(1)} %collective-permute-done.10.refs_12_) | copy-start | bytes 1990660
  330.3 5.5 %copy-start.11 = (bf16[288,1152]{1,0:T(8,128)(2,1)}, bf16[288,1152]{1,0:T(8,128)(2,1)S(1)}, u32[]{:S(2)}) copy-start(bf16[288,1152]{1,0:T(8,128)(2,1)S(1)} %collective-permute-done.11.refs_14_) | copy-start | bytes 1990660
  330.3 3.1 collective-permute-start.12
  335.8 47.5 %all-to-all-start.2 = ((bf16[16,24,1152]{2,1,0:T(8,128)(2,1)}), bf16[16,24,1152]{2,1,0:T(8,128)(2,1)S(1)}, u32[]{:S(2)}, u32[]{:S(2)}) async-start(bf16[16,24,1152]{2,1,0:T(8,128)(2,1)} %add_convert_fusion.1), calls=%async_computation.3 | async-start | bytes 1769472 | tf_op jit(solution)/shard_map/all_to_all | solution.py:207
  383.3 3.0 collective-permute-start.13
  388.6 32.5 %all-to-all-start.3 = ((bf16[16,24,1152]{2,1,0:T(8,128)(2,1)}), bf16[16,24,1152]{2,1,0:T(8,128)(2,1)S(1)}, u32[]{:S(2)}, u32[]{:S(2)}) async-start(bf16[16,24,1152]{2,1,0:T(8,128)(2,1)} %add_convert_fusion), calls=%async_computation.4 | async-start | bytes 1769472 | tf_op jit(solution)/shard_map/all_to_all | solution.py:207
  421.1 3.0 collective-permute-start.14
  426.5 23.9 %all-to-all-start.4 = ((bf16[16,24,1024]{2,1,0:T(8,128)(2,1)}), bf16[16,24,1024]{2,1,0:T(8,128)(2,1)S(1)}, u32[]{:S(2)}, u32[]{:S(2)}) async-start(bf16[16,24,1024]{2,1,0:T(8,128)(2,1)} %add_convert_fusion.2), calls=%async_computation.5 | async-start | bytes 1572864 | tf_op jit(solution)/shard_map/all_to_all | solution.py:207
  440.2 4.9 %copy-start.28 = (f32[1,128]{1,0:T(1,128)S(1)}, f32[1,128]{1,0:T(1,128)}, u32[]{:S(2)}) copy-start(f32[1,128]{1,0:T(1,128)} %get-tuple-element.214) | copy-start | bytes 1540
  455.1 20.5 %all-to-all-start.5 = ((f32[32,24,128]{2,1,0:T(8,128)}), f32[32,24,128]{2,1,0:T(8,128)S(1)}, u32[]{:S(2)}, u32[]{:S(2)}) async-start(f32[32,24,128]{2,1,0:T(8,128)} %get-tuple-element.218), calls=%async_computation.6 | async-start | bytes 786432 | tf_op jit(solution)/shard_map/all_to_all | solution.py:1212
  (6 other events, 8.1 us)
Sparse Core Ops, SparseCore 0:
  51.3 88.9 all-gather.3
  143.7 68.6 all-gather.5
  224.1 58.8 all-gather.7
  288.5 128.3 reduce-scatter.1

commit v5 on v4

--- a/solution.py
+++ b/solution.py
@@ -1017,20 +1017,21 @@
             pixels_b, ((row + step) % seq) * own_b, own_b, 0
         )
         part = part.reshape(own_b * rows_b * grid_b, depth_b)
-        slices.append(part)
+        if step:
+            slices.append(part)
         parts_b.append(shift(part, "y", step) if step else part)
         tabs_b.append(lax.dynamic_slice_in_dim(table_b, ((row - step) % seq) * span_b, span_b, 0))
     tab_a = lax.dynamic_slice_in_dim(table_a, row * span_a, span_a, 0)
     whole_a, whole_b = grid_a * grid_a, grid_b * grid_b
 
-    alive_a = live_a.astype(F32)[:, None]
-    counts = jnp.stack([lead * jnp.sum(alive_a), lead * jnp.sum(live_b.astype(F32))]).astype(BF)
-    lanes = round_up(rows_kern + 2, 128)
+    flags = (jnp.concatenate([live_a, live_b]).astype(F32) * lead).astype(BF)
+    slots = flags.shape[0]
+    lanes = round_up(rows_kern + slots, 128)
     sent = jnp.concatenate(
         [
             kern_w.astype(BF).T,
-            jnp.broadcast_to(counts[None], (width, 2)),
-            jnp.zeros((width, lanes - rows_kern - 2), BF),
+            jnp.broadcast_to(flags[None], (width, slots)),
+            jnp.zeros((width, lanes - rows_kern - slots), BF),
         ],
         1,
     )
@@ -1053,7 +1054,7 @@
     )
     held = stage(held, STAGES[2])
     got = got.reshape(count_all, rows_own, lanes)
-    counts = got[:, 0, rows_kern : rows_kern + 2]
+    counts = got[:, 0, rows_kern : rows_kern + slots]
     got = got.astype(F32)
     kern_cols = got[:, :, :rows_kern].transpose(1, 0, 2).reshape(rows_own, 3, BASE * BASE)
 
@@ -1120,7 +1121,11 @@
 
     images = jnp.concatenate([labels_b, live_b, labels_a, live_a, row.reshape(1).astype(jnp.int32)])
     images, counts, h1_b = lax.optimization_barrier((images, counts, h1_b))
-    count = jnp.sum(counts.astype(F32), 0, keepdims=True)
+    counts = jnp.sum(counts.astype(F32), 0, keepdims=True)
+    split = live_a.shape[0]
+    count = jnp.concatenate(
+        [jnp.sum(part, 1, keepdims=True) for part in (counts[:, :split], counts[:, split:])], 1
+    )
     total = jnp.maximum(jnp.sum(count), 1.0)
     rows_up = round_up(own_b + 1, 8)
     whole = np.ones((rows_up, 1), np.float32)

time: 494 us -> 493 us (level)
  transfers between devices with their start and end apart: 25 -> 25, of which waited for: 12 -> 12; matrix products, arithmetic and copies ran while one was open for 10% -> 10% of each run, Pallas kernels for 57% -> 58%
where the time goes in v5:
time: 493 us; the launch traced here: 487 us
  Pallas kernels  297 us (60%)
  waiting for transfers between devices  60.9 us (12%)
  starting transfers between devices  52.8 us (11%)
  local copies, waits for them, and re-layouts  27.9 us (6%)
  other arithmetic  21.9 us (4%)
  between operations  19.3 us (4%)
  matrix products  7.57 us (2%)
    pallas_call x2, Pallas kernels, attend_back_grad(): pl.pallas_call(partial(attend_back_grad_kernel, images=images, blocks=blo...  86 us
    pallas_call x4, Pallas kernels, attend_pairs(): pl.pallas_call(partial(attend_kernel, items=items, n_query=n_query), out_...  63.1 us
    pallas_call x1, Pallas kernels, mlp_back(): pl.pallas_call(partial(mlp_back_kernel, steps=steps), out_shape=(*outs, j...  42.1 us
    ppermute x15, waiting for transfers between devices, shift(): return lax.ppermute(value, axis, pairs)  36.6 us
    pallas_call x2, Pallas kernels, mlp(): pl.pallas_call(partial(mlp_kernel, per=per), out_shape=(jax.ShapeDtypeStr...  36 us
    pallas_call x1, Pallas kernels, embed_back(): pl.pallas_call(partial(embed_back_kernel, steps=steps, groups=len(d_b), p...  24.6 us
    all_to_all x3, starting transfers between devices, scatter_rows(): return lax.all_to_all(both, CHIPS, split_axis=0, concat_axis=0, tiled=True)  18.1 us
    ppermute x15, starting transfers between devices, shift(): return lax.ppermute(value, axis, pairs)  15.7 us
  transfers between devices with their start and end apart: 25, of which 12 were waited for; matrix products, arithmetic and copies ran while one was open for 10% of the time, Pallas kernels for 58%

profile of v5, /device:TPU:1, one launch (start us, length us, event | category | flops | bytes accessed | tf_op | source)
XLA Modules:
  0.0 487.3 jit_solution(6688432806388926049)
XLA Ops:
  9.0 4.2 collective-permute-start.2
  16.2 2.7 constant_dynamic-slice_fusion
  19.8 6.3 %all-to-all-start = ((bf16[32,24,128]{2,1,0:T(8,128)(2,1)}), bf16[32,24,128]{2,1,0:T(8,128)(2,1)S(1)}, u32[]{:S(2)}, u32[]{:S(2)}) async-start(bf16[32,24,128]{2,1,0:T(8,128)(2,1)} %bitcast.3), calls=%async_computation | async-start | bytes 393216 | tf_op jit(solution)/shard_map/all_to_all | solution.py:1039
  26.7 1.5 collective-permute-start.4
  28.2 1.4 constant_dynamic-update-slice_fusion.4
  31.2 1.5 pad_maximum_fusion.2
  32.8 1.6 constant_dynamic-slice_fusion.3.refs_1_.refs_9_
  39.0 2.7 collective-permute-done.3
  41.8 8.1 %collective-permute-done.4 = bf16[1024,432]{0,1:T(8,128)(2,1)S(1)} collective-permute-done((bf16[1024,432]{0,1:T(8,128)(2,1)S(1)}, bf16[1024,432]{0,1:T(8,128)(2,1)S(1)}, u32[]{:S(2)}, u32[]{:S(2)}) %collective-permute-start.4) | collective-permute-done | bytes 884768 | tf_op jit(solution)/shard_map/ppermute | solution.py:126
  51.2 1.4 convolution_convert_fusion.1
  54.5 5.2 %all-to-all-start.1 = ((bf16[16,24,1024]{2,1,0:T(8,128)(2,1)}), bf16[16,24,1024]{2,1,0:T(8,128)(2,1)S(1)}, u32[]{:S(2)}, u32[]{:S(2)}) async-start(bf16[16,24,1024]{2,1,0:T(8,128)(2,1)} %broadcast_in_dim.28), calls=%async_computation.1 | async-start | bytes 1572864 | tf_op jit(solution)/shard_map/all_to_all | solution.py:138
  59.7 1.4 collective-permute-start.5
  61.2 17.9 %collective-permute-done.5 = bf16[8,24,1152]{2,1,0:T(8,128)(2,1)} collective-permute-done((bf16[8,24,1152]{2,1,0:T(8,128)(2,1)S(1)}, bf16[8,24,1152]{2,1,0:T(8,128)(2,1)}, u32[]{:S(2)}, u32[]{:S(2)}) %collective-permute-start.5) | collective-permute-done | bytes 442400 | tf_op jit(solution)/shard_map/ppermute | solution.py:126
  79.0 4.8 all-to-all-done.1
  83.8 1.5 collective-permute-start.6
  92.0 3.2 embed.2
  98.3 3.6 place_blocks.1
  101.9 8.7 %embed.3 = (f32[2048,768]{1,0:T(8,128)}, bf16[2048,768]{1,0:T(8,128)(2,1)}) custom-call(bf16[1024,432]{1,0:T(8,128)(2,1)} %bitcast.59, bf16[1024,432]{1,0:T(8,128)(2,1)} %copy.126.refs_1_.refs_4_, bf16[1024,128]{1,0:T(8,128)(2,1)} %pad_maximum_fusion.3.refs_2_, bf16[768,1024]{1,0:T(8,128)(2,1)} %bitcast.58, f32[1,768]{1,0:T(1,128)} %get-tuple-element.256.refs_3_.refs_4_.refs_15_), custom_call_target="tpu_custom_call" | custom-call | flops 2415919104 | bytes 12582912 | tf_op jit(solution)/shard_map/embed/pallas_call | solution.py:293
  111.7 24.9 %attend.4 = (bf16[2048,1152]{1,0:T(8,128)(2,1)}, bf16[2048,384]{1,0:T(8,128)(2,1)}, f32[2,3,2,1024]{3,2,1,0:T(2,128)}) custom-call(bf16[2048,768]{1,0:T(8,128)(2,1)} %get-tuple-element.185.h1_ref, bf16[768,1152]{1,0:T(8,128)(2,1)} %bitcast.67), custom_call_target="tpu_custom_call" | custom-call | flops 18723373056 | bytes 12582912 | tf_op jit(solution)/shard_map/attend/pallas_call | solution.py:369
  139.1 25.1 %attend.5 = (bf16[2048,1152]{1,0:T(8,128)(2,1)}, bf16[2048,384]{1,0:T(8,128)(2,1)}, f32[2,3,2,1024]{3,2,1,0:T(2,128)}) custom-call(bf16[2048,768]{1,0:T(8,128)(2,1)} %get-tuple-element.185.h1_ref, bf16[768,6144]{1,0:T(8,128)(2,1)} %all-gather.4.cloned.1.call-done.weight_ref.wout_ref.wup_ref.refs_12_.refs_14_.refs_17_.refs_18_), custom_call_target="tpu_custom_call" | custom-call | flops 18723373056 | bytes 12582912 | tf_op jit(solution)/shard_map/attend/pallas_call | solution.py:369
  164.2 6.4 %attend.7 = (bf16[576,1152]{1,0:T(8,128)(2,1)}, bf16[288,384]{1,0:T(8,128)(2,1)}, f32[1,3,2,288]{3,2,1,0:T(2,128)}) custom-call(bf16[576,768]{1,0:T(8,128)(2,1)} %pad_maximum_fusion.1.h1_ref.h1_a_ref, bf16[768,6144]{1,0:T(8,128)(2,1)} %all-gather.4.cloned.1.call-done.weight_ref.wout_ref.wup_ref.refs_12_.refs_14_.refs_17_.refs_18_), custom_call_target="tpu_custom_call" | custom-call | flops 2213609472 | bytes 3538944 | tf_op jit(solution)/shard_map/attend/pallas_call | solution.py:369
  170.6 6.8 %attend.6 = (bf16[576,1152]{1,0:T(8,128)(2,1)}, bf16[288,384]{1,0:T(8,128)(2,1)}, f32[1,3,2,288]{3,2,1,0:T(2,128)}) custom-call(bf16[576,768]{1,0:T(8,128)(2,1)} %pad_maximum_fusion.1.h1_ref.h1_a_ref, bf16[768,6144]{1,0:T(8,128)(2,1)} %all-gather.4.cloned.1.call-done.weight_ref.wout_ref.wup_ref.refs_12_.refs_14_.refs_17_.refs_18_), custom_call_target="tpu_custom_call" | custom-call | flops 2213609472 | bytes 3538944 | tf_op jit(solution)/shard_map/attend/pallas_call | solution.py:369
  177.4 7.7 %mlp.2 = (f32[288,768]{1,0:T(8,128)}, bf16[288,3072]{1,0:T(8,128)(2,1)}, f32[1,1,768]{2,1,0:T(1,128)}, f32[1,1,3072]{2,1,0:T(1,128)}) custom-call(f32[288,768]{1,0:T(8,128)} %get-tuple-element.147.x0_ref.refs_7_, bf16[288,384]{1,0:T(8,128)(2,1)} %get-tuple-element.159.mixed0_ref.refs_10_.o_ref, ...), custom_call_target="tpu_custom_call" | custom-call | flops 106168320 | bytes 110592 | tf_op jit(solution)/shard_map/mlp/pallas_call | solution.py:549
  186.6 28.3 %mlp.3 = (f32[2048,768]{1,0:T(8,128)}, bf16[2048,3072]{1,0:T(8,128)(2,1)}, f32[2,1,768]{2,1,0:T(1,128)}, f32[2,1,3072]{2,1,0:T(1,128)}) custom-call(f32[2048,768]{1,0:T(8,128)} %get-tuple-element.162.x0_ref.refs_0_, bf16[2048,384]{1,0:T(8,128)(2,1)} %get-tuple-element.163.mixed0_ref.refs_4_.o_ref, ...), custom_call_target="tpu_custom_call" | custom-call | flops 754974720 | bytes 786432 | tf_op jit(solution)/shard_map/mlp/pallas_call | solution.py:549
  215.5 7.2 %head.1 = (f32[1,128]{1,0:T(1,128)}, bf16[8,5632]{1,0:T(8,128)(2,1)}, f32[3,1,768]{2,1,0:T(1,128)}, f32[3,1,3072]{2,1,0:T(1,128)}) custom-call(s32[11]{0:T(128)} %concatenate.57.image_ref, f32[2,1,768]{2,1,0:T(1,128)} %get-tuple-element.167.xsum_ref, f32[2,1,3072]{2,1,0:T(1,128)} %get-tuple-element.168.asum_ref, f32[1,3840]{1,0:T(1,128)} %fusion.25.sums_a_ref, ...), custom_call_target="tpu_custom_call" | custom-call | flops 134217728 | bytes 262144 | tf_op jit(solution)/shard_map/head/pallas_call | solution.py:650
  222.8 42.1 %mlp_back.1 = (f32[2048,768]{1,0:T(8,128)}, bf16[2048,384]{1,0:T(8,128)(2,1)}, bf16[2048,384]{1,0:T(8,128)(2,1)}, f32[288,768]{1,0:T(8,128)}, bf16[288,384]{1,0:...) custom-call(bf16[2048,3072]{1,0:T(8,128)(2,1)} %get-tuple-element.165.refs_0_, ...), custom_call_target="tpu_custom_call" | custom-call | flops 861143040 | bytes 897024 | tf_op jit(solution)/shard_map/mlp_back/pallas_call | solution.py:742
  264.9 6.6 %attend_back_apart.3.d_a_ref.refs_11_ = bf16[576,1152]{1,0:T(8,128)(2,1)} custom-call(bf16[576,1152]{1,0:T(8,128)(2,1)} %get-tuple-element.186.q_ref.kv_ref, bf16[576,1152]{1,0:T(8,128)(2,1)} %get-tuple-element.186.q_ref.kv_ref, bf16[288,384]{1,0:T(8,128)(2,1)} %get-tuple-element.187.do_ref, bf16[288,384]{1,0:T(8,128)(2,1)} %get-tuple-element.159.mixed0_ref.refs_10_.o_ref, ...), custom_call_target="tpu_custom_call" | custom-call | flops 74649600 | bytes 82944 | tf_op jit(solution)/shard_map/attend_back_apart/pallas_call | solution.py:435
  271.5 6.4 %attend_back_apart.2.d_a_ref.refs_13_ = bf16[576,1152]{1,0:T(8,128)(2,1)} custom-call(bf16[576,1152]{1,0:T(8,128)(2,1)} %get-tuple-element.180.q_ref.kv_ref, bf16[576,1152]{1,0:T(8,128)(2,1)} %get-tuple-element.180.q_ref.kv_ref, bf16[288,384]{1,0:T(8,128)(2,1)} %get-tuple-element.181.do_ref, bf16[288,384]{1,0:T(8,128)(2,1)} %get-tuple-element.160.mixed1_ref.refs_11_.o_ref, ...), custom_call_target="tpu_custom_call" | custom-call | flops 74649600 | bytes 82944 | tf_op jit(solution)/shard_map/attend_back_apart/pallas_call | solution.py:435
  277.9 3.9 all-gather.8.cloned.1.call-done
  286.1 43.0 %attend_back.2 = (bf16[2048,1152]{1,0:T(8,128)(2,1)}, bf16[16,24,1152]{2,1,0:T(8,128)(2,1)}, bf16[16,24,1152]{2,1,0:T(8,128)(2,1)}) custom-call(s32[1]{0:T(128)} %bitcast.core_ref, bf16[2048,1152]{1,0:T(8,128)(2,1)} %get-tuple-element.154.qkv_ref, bf16[2048,384]{1,0:T(8,128)(2,1)} %get-tuple-element.183.do_ref, ...), custom_call_target="tpu_custom_call" | custom-call | flops 1101004800 | bytes 393216 | tf_op jit(solution)/shard_map/attend_back/pallas_call | solution.py:484
  330.0 2.3 collective-permute-done.12
  332.2 2.3 add_convert_fusion.1
  334.6 4.4 all-to-all-start.2
  339.0 43.1 %attend_back.3 = (bf16[2048,1152]{1,0:T(8,128)(2,1)}, bf16[16,24,1152]{2,1,0:T(8,128)(2,1)}, bf16[16,24,1152]{2,1,0:T(8,128)(2,1)}) custom-call(s32[1]{0:T(128)} %bitcast.core_ref, bf16[2048,1152]{1,0:T(8,128)(2,1)} %get-tuple-element.157.qkv_ref, bf16[2048,384]{1,0:T(8,128)(2,1)} %get-tuple-element.190.do_ref, ...), custom_call_target="tpu_custom_call" | custom-call | flops 1101004800 | bytes 393216 | tf_op jit(solution)/shard_map/attend_back/pallas_call | solution.py:484
  382.8 2.3 collective-permute-done.13
  385.0 2.4 add_convert_fusion
  387.4 6.9 %all-to-all-start.3 = ((bf16[16,24,1152]{2,1,0:T(8,128)(2,1)}), bf16[16,24,1152]{2,1,0:T(8,128)(2,1)S(1)}, u32[]{:S(2)}, u32[]{:S(2)}) async-start(bf16[16,24,1152]{2,1,0:T(8,128)(2,1)} %add_convert_fusion), calls=%async_computation.4 | async-start | bytes 1769472 | tf_op jit(solution)/shard_map/all_to_all | solution.py:207
  394.3 24.6 %embed_back.1 = (bf16[16,24,1024]{2,1,0:T(8,128)(2,1)}, bf16[16,24,1024]{2,1,0:T(8,128)(2,1)}) custom-call(s32[1]{0:T(128)} %bitcast.core_ref, f32[2048,768]{1,0:T(8,128)} %get-tuple-element.162.x0_ref.refs_0_, f32[2048,768]{1,0:T(8,128)} %get-tuple-element.193.refs_1_, bf16[1024,128]{1,0:T(8,128)(2,1)} %pad_maximum_fusion.3.refs_2_, ...), custom_call_target="tpu_custom_call" | custom-call | flops 289406976 | bytes 640000 | tf_op jit(solution)/shard_map/embed_back/pallas_call | solution.py:844
  420.8 2.1 collective-permute-done.14
  422.9 2.3 add_convert_fusion.2
  425.2 6.8 %all-to-all-start.4 = ((bf16[16,24,1024]{2,1,0:T(8,128)(2,1)}), bf16[16,24,1024]{2,1,0:T(8,128)(2,1)S(1)}, u32[]{:S(2)}, u32[]{:S(2)}) async-start(bf16[16,24,1024]{2,1,0:T(8,128)(2,1)} %add_convert_fusion.2), calls=%async_computation.5 | async-start | bytes 1572864 | tf_op jit(solution)/shard_map/all_to_all | solution.py:207
  433.2 2.6 multiply_reduce_fusion.3
  435.8 3.1 multiply_reduce_fusion.2
  444.4 4.7 all-to-all-done.4.got_ref
  450.0 3.9 resize_back.1
  453.9 7.3 %all-to-all-start.5 = ((f32[32,24,128]{2,1,0:T(8,128)}), f32[32,24,128]{2,1,0:T(8,128)S(1)}, u32[]{:S(2)}, u32[]{:S(2)}) async-start(f32[32,24,128]{2,1,0:T(8,128)} %get-tuple-element.218), calls=%async_computation.6 | async-start | bytes 786432 | tf_op jit(solution)/shard_map/all_to_all | solution.py:1217
  464.6 9.7 %all-to-all-done.5.got_ref = f32[32,24,128]{2,1,0:T(8,128)S(1)} async-done(((f32[32,24,128]{2,1,0:T(8,128)}), f32[32,24,128]{2,1,0:T(8,128)S(1)}, u32[]{:S(2)}, u32[]{:S(2)}) %all-to-all-start.5) | async-done | bytes 393248 | tf_op jit(solution)/shard_map/all_to_all | solution.py:1217
  475.1 5.5 %update.1 = (f32[24,2304]{1,0:T(8,128)}, f32[24,768]{1,0:T(8,128)}, f32[2,24,3072]{2,1,0:T(8,128)}, f32[96,768]{1,0:T(8,128)}, f32[24,49]{1,0:T(8,128)}, /*index...) custom-call(f32[32,24,128]{2,1,0:T(8,128)} %copy-done.6, ...), custom_call_target="tpu_custom_call" | custom-call | flops 8388608 | bytes 524288 | tf_op jit(solution)/shard_map/update/pallas_call | solution.py:964
  (172 shorter events, 45.8 us)
Async XLA Ops:
  9.0 25.4 %collective-permute-start.2 = (bf16[1,24,1152]{2,1,0:T(8,128)(2,1)}, bf16[1,24,1152]{2,1,0:T(8,128)(2,1)}, u32[]{:S(2)}, u32[]{:S(2)}) collective-permute-start(bf16[1,24,1152]{2,1,0:T(8,128)(2,1)} %broadcast_in_dim_reshape.3), channel_id=1, source_target_pairs={{0,24},{8,0},{16,8},{24,16},{1,25},{9,1},{17,9},{25,17},{2,26},{10... | collective-permute-start | bytes 165896 | tf_op jit(solution)/shard_map/ppermute | solution.py:126
  13.1 21.2 %collective-permute-start.1 = (bf16[1,24,1152]{2,1,0:T(8,128)(2,1)}, bf16[1,24,1152]{2,1,0:T(8,128)(2,1)}, u32[]{:S(2)}, u32[]{:S(2)}) collective-permute-start(bf16[1,24,1152]{2,1,0:T(8,128)(2,1)} %broadcast_in_dim_reshape.3), channel_id=1, source_target_pairs={{0,16},{8,24},{16,0},{24,8},{1,17},{9,25},{17,1},{25,9},{2,18},{10... | collective-permute-start | bytes 165896 | tf_op jit(solution)/shard_map/ppermute | solution.py:126
  13.1 21.2 %collective-permute-start = (bf16[1,24,1152]{2,1,0:T(8,128)(2,1)}, bf16[1,24,1152]{2,1,0:T(8,128)(2,1)}, u32[]{:S(2)}, u32[]{:S(2)}) collective-permute-start(bf16[1,24,1152]{2,1,0:T(8,128)(2,1)} %broadcast_in_dim_reshape.3), channel_id=1, source_target_pairs={{0,8},{8,16},{16,24},{24,0},{1,9},{9,17},{17,25},{25,1},{2,10},{10... | collective-permute-start | bytes 165896 | tf_op jit(solution)/shard_map/ppermute | solution.py:126
  19.0 10.7 %copy-start.16 = (f32[24,768]{1,0:T(8,128)S(1)}, f32[24,768]{1,0:T(8,128)}, u32[]{:S(2)}) copy-start(f32[24,768]{1,0:T(8,128)} %refs_1_.1) | copy-start | bytes 221188
  19.0 11.4 %copy-start.4 = (f32[2,24,3072]{2,1,0:T(8,128)S(1)}, f32[2,24,3072]{2,1,0:T(8,128)}, u32[]{:S(2)}) copy-start(f32[2,24,3072]{2,1,0:T(8,128)} %refs_2_.1) | copy-start | bytes 1769476
  19.8 22.0 %all-to-all-start = ((bf16[32,24,128]{2,1,0:T(8,128)(2,1)}), bf16[32,24,128]{2,1,0:T(8,128)(2,1)S(1)}, u32[]{:S(2)}, u32[]{:S(2)}) async-start(bf16[32,24,128]{2,1,0:T(8,128)(2,1)} %bitcast.3), calls=%async_computation | async-start | bytes 393216 | tf_op jit(solution)/shard_map/all_to_all | solution.py:1039
  26.1 4.4 copy-start.17
  26.1 113.0 %all-gather.4.cloned.1.call-start = ((), (), s32[]{:S(2)}) async-start(), calls=%async_computation.7 | async-start | bytes 9732096 | tf_op jit(solution)/shard_map/all_gather | solution.py:1061
  26.7 23.2 %collective-permute-start.4 = (bf16[1024,432]{0,1:T(8,128)(2,1)S(1)}, bf16[1024,432]{0,1:T(8,128)(2,1)S(1)}, u32[]{:S(2)}, u32[]{:S(2)}) collective-permute-start(bf16[1024,432]{0,1:T(8,128)(2,1)S(1)} %copy.117), channel_id=1, source_target_pairs={{0,1},{1,0},{2,3},{3,2},{4,5},{5,4},{6,7},{7,6},{8,9},{9,8},{10,11... | collective-permute-start | bytes 2654216 | tf_op jit(solution)/shard_map/ppermute | solution.py:126
  30.4 6.2 %copy-start.13 = (bf16[8,24,1152]{2,1,0:T(8,128)(2,1)S(1)}, bf16[8,24,1152]{2,1,0:T(8,128)(2,1)}, u32[]{:S(2)}) copy-start(bf16[8,24,1152]{2,1,0:T(8,128)(2,1)} %constant_dynamic-update-slice_fusion.4) | copy-start | bytes 1327108
  30.4 19.5 %copy-start.22 = (f32[2,24]{1,0:T(2,128)S(1)}, f32[2,24]{1,0:T(2,128)}, u32[]{:S(2)}) copy-start(f32[2,24]{1,0:T(2,128)} %refs_6_.1) | copy-start | bytes 580
  30.5 19.6 %copy-start.18 = (f32[49,24]{0,1:T(8,128)S(1)}, f32[49,24]{0,1:T(8,128)}, u32[]{:S(2)}) copy-start(f32[49,24]{0,1:T(8,128)} %param.46) | copy-start | bytes 14116
  32.8 20.0 %copy-start.12 = (f32[144,1024,1]{1,0,2:T(8,128)S(1)}, f32[144,1024,1]{1,0,2:T(8,128)}, u32[]{:S(2)}) copy-start(f32[144,1024,1]{1,0,2:T(8,128)} %constant.163) | copy-start | bytes 1769476
  35.3 6.4 %collective-permute-start.3 = (bf16[4,24,1152]{2,1,0:T(8,128)(2,1)S(1)}, bf16[4,24,1152]{2,1,0:T(8,128)(2,1)S(1)}, u32[]{:S(2)}, u32[]{:S(2)}) collective-permute-start(bf16[4,24,1152]{2,1,0:T(8,128)(2,1)S(1)} %pad_maximum_fusion.4), channel_id=1, source_target_pairs={{0,4},{4,0},{1,5},{5,1},{2,6},{6,2},{3,7},{7,3},{8,12},{12,8},{9,1... | collective-permute-start | bytes 663560 | tf_op jit(solution)/shard_map/ppermute | solution.py:126
  41.8 12.7 %copy-start.9 = (bf16[32,24,128]{2,1,0:T(8,128)(2,1)}, bf16[32,24,128]{2,1,0:T(8,128)(2,1)S(1)}, u32[]{:S(2)}) copy-start(bf16[32,24,128]{2,1,0:T(8,128)(2,1)S(1)} %all-to-all-done) | copy-start | bytes 589828
  52.8 32.6 %copy-start.15 = (f32[24,1000]{1,0:T(8,128)S(1)}, f32[24,1000]{1,0:T(8,128)}, u32[]{:S(2)}) copy-start(f32[24,1000]{1,0:T(8,128)} %refs_5_.1) | copy-start | bytes 288004
  54.5 29.3 %all-to-all-start.1 = ((bf16[16,24,1024]{2,1,0:T(8,128)(2,1)}), bf16[16,24,1024]{2,1,0:T(8,128)(2,1)S(1)}, u32[]{:S(2)}, u32[]{:S(2)}) async-start(bf16[16,24,1024]{2,1,0:T(8,128)(2,1)} %broadcast_in_dim.28), calls=%async_computation.1 | async-start | bytes 1572864 | tf_op jit(solution)/shard_map/all_to_all | solution.py:138
  59.7 155.8 %all-gather.6.cloned.1.call-start = ((), (), s32[]{:S(2)}) async-start(), calls=%async_computation.8 | async-start | bytes 6488064 | tf_op jit(solution)/shard_map/all_gather | solution.py:1082
  59.7 19.3 %collective-permute-start.5 = (bf16[8,24,1152]{2,1,0:T(8,128)(2,1)S(1)}, bf16[8,24,1152]{2,1,0:T(8,128)(2,1)}, u32[]{:S(2)}, u32[]{:S(2)}) collective-permute-start(bf16[8,24,1152]{2,1,0:T(8,128)(2,1)S(1)} %constant_dynamic-update-slice_fusion), channel_id=1, source_target_pairs={{0,1},{1,0},{2,3},{3,2},{4,5},{5,4},{6,7},{7,6},{8,9},{9,8},{10,11... | collective-permute-start | bytes 1327112 | tf_op jit(solution)/shard_map/ppermute | solution.py:126
  83.8 3.4 collective-permute-start.6
  87.7 4.3 copy-start.2
  87.7 2.8 copy-start.21
  87.7 194.1 %all-gather.8.cloned.1.call-start = ((), (), s32[]{:S(2)}) async-start(), calls=%async_computation.9 | async-start | bytes 2973696 | tf_op jit(solution)/shard_map/all_gather | solution.py:1137
  88.0 7.4 %copy-start.23 = (s32[32]{0:T(128)S(1)}, s32[32]{0:T(128)}, u32[]{:S(2)}) copy-start(s32[32]{0:T(128)} %constant.162) | copy-start | bytes 388
  88.0 7.4 %copy-start.24 = (s32[32]{0:T(128)S(1)}, s32[32]{0:T(128)}, u32[]{:S(2)}) copy-start(s32[32]{0:T(128)} %constant.161) | copy-start | bytes 388
  88.0 7.4 %copy-start.25 = (s32[32]{0:T(128)S(1)}, s32[32]{0:T(128)}, u32[]{:S(2)}) copy-start(s32[32]{0:T(128)} %constant.160) | copy-start | bytes 388
  88.1 7.4 %copy-start.26 = (s32[32]{0:T(128)S(1)}, s32[32]{0:T(128)}, u32[]{:S(2)}) copy-start(s32[32]{0:T(128)} %constant.159) | copy-start | bytes 388
  89.4 8.9 %copy-start.5 = (bf16[16,24,1152]{2,1,0:T(8,128)(2,1)}, bf16[16,24,1152]{2,1,0:T(8,128)(2,1)S(1)}, u32[]{:S(2)}) copy-start(bf16[16,24,1152]{2,1,0:T(8,128)(2,1)S(1)} %constant_dynamic-update-slice_fusion.5.refs_0_) | copy-start | bytes 2654212
  89.4 5.8 %collective-permute-start.7 = (bf16[16,24,1152]{2,1,0:T(8,128)(2,1)S(1)}, bf16[16,24,1152]{2,1,0:T(8,128)(2,1)}, u32[]{:S(2)}, u32[]{:S(2)}) collective-permute-start(bf16[16,24,1152]{2,1,0:T(8,128)(2,1)S(1)} %constant_dynamic-update-slice_fusion.5.refs_0_), channel_id=1, source_target_pairs={{0,2},{2,0},{1,3},{3,1},{4,6},{6,4},{5,7},{7,5},{8,10},{10,8},{9,1... | collective-permute-start | bytes 2654216 | tf_op jit(solution)/shard_map/ppermute | solution.py:126
  91.4 5.6 %copy-start.8 = (bf16[1024,432]{0,1:T(8,128)(2,1)S(1)}, bf16[1024,432]{0,1:T(8,128)(2,1)}, u32[]{:S(2)}) copy-start(bf16[1024,432]{0,1:T(8,128)(2,1)} %copy-done.7) | copy-start | bytes 2654212
  95.1 15.6 %collective-permute-start.8 = (bf16[288,768]{1,0:T(8,128)(2,1)}, bf16[288,768]{1,0:T(8,128)(2,1)S(1)}, u32[]{:S(2)}, u32[]{:S(2)}) collective-permute-start(bf16[288,768]{1,0:T(8,128)(2,1)} %get-tuple-element.142), channel_id=1, source_target_pairs={{0,1},{1,0},{2,3},{3,2},{4,5},{5,4},{6,7},{7,6},{8,9},{9,8},{10,11... | collective-permute-start | bytes 1327112 | tf_op jit(solution)/shard_map/ppermute | solution.py:126
  101.9 8.8 %copy-start.14 = (bf16[288,768]{1,0:T(8,128)(2,1)S(1)}, bf16[288,768]{1,0:T(8,128)(2,1)}, u32[]{:S(2)}) copy-start(bf16[288,768]{1,0:T(8,128)(2,1)} %get-tuple-element.142) | copy-start | bytes 1327108
  185.8 29.0 %collective-permute-start.9 = (f32[1,3840]{1,0:T(1,128)S(1)}, f32[1,3840]{1,0:T(1,128)S(1)}, u32[]{:S(2)}, u32[]{:S(2)}) collective-permute-start(f32[1,3840]{1,0:T(1,128)S(1)} %pad_maximum_fusion.6), channel_id=1, source_target_pairs={{0,1},{1,0},{2,3},{3,2},{4,5},{5,4},{6,7},{7,6},{8,9},{9,8},{10,11... | collective-permute-start | bytes 46088 | tf_op jit(solution)/shard_map/ppermute | solution.py:126
  186.6 28.3 %copy-start.19 = (f32[1,1,3072]{2,1,0:T(1,128)S(1)}, f32[1,1,3072]{2,1,0:T(1,128)}, u32[]{:S(2)}) copy-start(f32[1,1,3072]{2,1,0:T(1,128)} %get-tuple-element.170) | copy-start | bytes 36868
  186.6 28.3 %copy-start.20 = (f32[1,1,768]{2,1,0:T(1,128)S(1)}, f32[1,1,768]{2,1,0:T(1,128)}, u32[]{:S(2)}) copy-start(f32[1,1,768]{2,1,0:T(1,128)} %get-tuple-element.169) | copy-start | bytes 9220
  222.7 196.2 %reduce-scatter.2.cloned.1.call-start = ((), (), s32[]{:S(2)}) async-start(), calls=%async_computation.10 | async-start | bytes 6082560 | tf_op jit(solution)/shard_map/reduce_scatter | solution.py:1157
  284.5 44.5 %collective-permute-start.10 = (bf16[288,1152]{1,0:T(8,128)(2,1)S(1)}, bf16[288,1152]{1,0:T(8,128)(2,1)S(1)}, u32[]{:S(2)}, u32[]{:S(2)}) collective-permute-start(bf16[288,1152]{1,0:T(8,128)(2,1)S(1)} %slice.88), channel_id=1, source_target_pairs={{0,1},{1,0},{2,3},{3,2},{4,5},{5,4},{6,7},{7,6},{8,9},{9,8},{10,11... | collective-permute-start | bytes 1990664 | tf_op jit(solution)/shard_map/ppermute | solution.py:126
  285.8 43.3 %collective-permute-start.11 = (bf16[288,1152]{1,0:T(8,128)(2,1)S(1)}, bf16[288,1152]{1,0:T(8,128)(2,1)S(1)}, u32[]{:S(2)}, u32[]{:S(2)}) collective-permute-start(bf16[288,1152]{1,0:T(8,128)(2,1)S(1)} %slice.89), channel_id=1, source_target_pairs={{0,1},{1,0},{2,3},{3,2},{4,5},{5,4},{6,7},{7,6},{8,9},{9,8},{10,11... | collective-permute-start | bytes 1990664 | tf_op jit(solution)/shard_map/ppermute | solution.py:126
  329.1 5.5 %copy-start.10 = (bf16[288,1152]{1,0:T(8,128)(2,1)}, bf16[288,1152]{1,0:T(8,128)(2,1)S(1)}, u32[]{:S(2)}) copy-start(bf16[288,1152]{1,0:T(8,128)(2,1)S(1)} %collective-permute-done.10.refs_12_) | copy-start | bytes 1990660
  329.1 5.5 %copy-start.11 = (bf16[288,1152]{1,0:T(8,128)(2,1)}, bf16[288,1152]{1,0:T(8,128)(2,1)S(1)}, u32[]{:S(2)}) copy-start(bf16[288,1152]{1,0:T(8,128)(2,1)S(1)} %collective-permute-done.11.refs_14_) | copy-start | bytes 1990660
  329.1 3.1 collective-permute-start.12
  334.6 47.5 %all-to-all-start.2 = ((bf16[16,24,1152]{2,1,0:T(8,128)(2,1)}), bf16[16,24,1152]{2,1,0:T(8,128)(2,1)S(1)}, u32[]{:S(2)}, u32[]{:S(2)}) async-start(bf16[16,24,1152]{2,1,0:T(8,128)(2,1)} %add_convert_fusion.1), calls=%async_computation.3 | async-start | bytes 1769472 | tf_op jit(solution)/shard_map/all_to_all | solution.py:207
  382.0 3.0 collective-permute-start.13
  387.4 32.5 %all-to-all-start.3 = ((bf16[16,24,1152]{2,1,0:T(8,128)(2,1)}), bf16[16,24,1152]{2,1,0:T(8,128)(2,1)S(1)}, u32[]{:S(2)}, u32[]{:S(2)}) async-start(bf16[16,24,1152]{2,1,0:T(8,128)(2,1)} %add_convert_fusion), calls=%async_computation.4 | async-start | bytes 1769472 | tf_op jit(solution)/shard_map/all_to_all | solution.py:207
  419.9 3.0 collective-permute-start.14
  425.2 23.8 %all-to-all-start.4 = ((bf16[16,24,1024]{2,1,0:T(8,128)(2,1)}), bf16[16,24,1024]{2,1,0:T(8,128)(2,1)S(1)}, u32[]{:S(2)}, u32[]{:S(2)}) async-start(bf16[16,24,1024]{2,1,0:T(8,128)(2,1)} %add_convert_fusion.2), calls=%async_computation.5 | async-start | bytes 1572864 | tf_op jit(solution)/shard_map/all_to_all | solution.py:207
  438.9 4.9 %copy-start.28 = (f32[1,128]{1,0:T(1,128)S(1)}, f32[1,128]{1,0:T(1,128)}, u32[]{:S(2)}) copy-start(f32[1,128]{1,0:T(1,128)} %get-tuple-element.214) | copy-start | bytes 1540
  453.9 20.5 %all-to-all-start.5 = ((f32[32,24,128]{2,1,0:T(8,128)}), f32[32,24,128]{2,1,0:T(8,128)S(1)}, u32[]{:S(2)}, u32[]{:S(2)}) async-start(f32[32,24,128]{2,1,0:T(8,128)} %get-tuple-element.218), calls=%async_computation.6 | async-start | bytes 786432 | tf_op jit(solution)/shard_map/all_to_all | solution.py:1217
  (6 other events, 8.1 us)
Sparse Core Ops, SparseCore 0:
  50.0 89.0 all-gather.3
  142.6 68.5 all-gather.5
  222.8 58.9 all-gather.7
  287.3 128.2 reduce-scatter.1
